TPU v7x, 512 devices: a whole 4x8x8 slice. The times are simulated.
512 devices in a mesh: row: 32 (over z_lo, x, core), col: 16 (over z_hi, y).
Axes of the slice: x: 4, y: 8, z: 8 (z_hi: 2, z_lo: 4; z = z_hi * 4 + z_lo), core: 2. Of those that a mesh axis runs over, the one named last changes fastest.
Arguments:
- features: bfloat16 [65536, 512], P(('row', 'col')), may hold values from -6 to 6
- weight: bfloat16 [512, 512], replicated, may hold values from -0.25 to 0.25
- bias_term: float32 [512], replicated, may hold values from -3 to 3
- cotangent: bfloat16 [65536, 512], P(('row', 'col')), may hold values from -0.125 to 0.125
- tile_values: bfloat16 [32, 16, 11, 256, 256], P('row', 'col'), may hold values from -0.078125 to 0.078125
- tile_rows: int32 [32, 16, 11], P('row', 'col'), may hold values from 0 to 7
- tile_cols: int32 [32, 16, 11], P('row', 'col'), may hold values from 0 to 15
- tile_count: int32 [32, 16], P('row', 'col'), may hold values from 1 to 11, as said below
Outputs:
- activations: bfloat16 [65536, 512], P(('row', 'col'))
- weight_grad: float32 [512, 512], replicated
- bias_grad: float32 [512], replicated
Inputs may be any that keep to these rules, and one draw needn't show every extreme that they name: Slots from tile_count on hold no tile; some grid cell uses all 11 slots in every draw.
All inputs are finite; a program needn't handle non-finite values.
Results may differ from a plain program's by a relative error of at most 0.017.
Values may be sent and summed in bfloat16 or wider, within the bound.
No kernel may reach another device: no remote copies, remote signals or barrier semaphores. Data moves between devices by JAX's collectives and lax.ppermute only.
A program may use at most 64 MiB of HBM per device.

v0:
```python
import jax
import jax.numpy as jnp
from jax import lax
from jax.sharding import PartitionSpec as P


def add_product(buffer, tile_mat, window, tile_index):
    tile_size = tile_mat.shape[0]
    anchor = tile_index * tile_size
    current = lax.dynamic_slice_in_dim(buffer, anchor, tile_size, 0)
    product = jnp.dot(tile_mat, window, preferred_element_type=jnp.float32)
    return lax.dynamic_update_slice_in_dim(buffer, current + product, anchor, 0)


def per_device(
    features, weight, bias_term, cotangent, tile_values, tile_rows, tile_cols, tile_count
):
    tile_mats = tile_values[0, 0]
    row_ids = tile_rows[0, 0]
    col_ids = tile_cols[0, 0]
    used = tile_count[0, 0]
    tile_size = tile_mats.shape[1]
    local_rows, width = features.shape
    height = lax.axis_size("col") * local_rows
    gathered = lax.all_gather(features, "row", axis=0, tiled=True)
    buffer = jnp.zeros((height, width), jnp.float32)

    def own_step(slot_index, current):
        tile_mat = lax.dynamic_index_in_dim(tile_mats, slot_index, 0, keepdims=False)
        window = lax.dynamic_slice_in_dim(gathered, col_ids[slot_index] * tile_size, tile_size, 0)
        return add_product(current, tile_mat, window, row_ids[slot_index])

    aggregated = lax.psum_scatter(
        lax.fori_loop(0, used, own_step, buffer).astype(jnp.bfloat16),
        "col",
        scatter_dimension=0,
        tiled=True,
    )
    preact = jnp.dot(aggregated, weight, preferred_element_type=jnp.float32) + bias_term
    activations = jax.nn.silu(preact).astype(jnp.bfloat16)
    sigmoid_part = jax.nn.sigmoid(preact)
    grad_preact = (
        cotangent.astype(jnp.float32) * sigmoid_part * (1.0 + preact * (1.0 - sigmoid_part))
    )
    grad_rounded = grad_preact.astype(jnp.bfloat16)
    local_weight = jnp.einsum(
        "nf,ng->fg", aggregated, grad_rounded, preferred_element_type=jnp.float32
    )
    local_bias = jnp.sum(grad_preact, axis=0)
    weight_grad, bias_grad = lax.psum((local_weight, local_bias), ("row", "col"))
    return (activations, weight_grad, bias_grad)


def solution(mesh):
    return jax.shard_map(
        per_device,
        mesh=mesh,
        in_specs=(
            P(("row", "col"), None),
            P(),
            P(),
            P(("row", "col"), None),
            P("row", "col", None, None, None),
            P("row", "col", None),
            P("row", "col", None),
            P("row", "col"),
        ),
        out_specs=(P(("row", "col"), None), P(), P()),
        check_vma=False,
    )
```

profile of v0, /device:TPU:1, one launch (start us, length us, event | category | flops | bytes accessed | tf_op | source)
XLA Modules:
  0.0 657.4 jit_solution(4785398175929527123)
XLA Ops:
  7.2 0.0 copy-start
  7.2 0.0 copy-start.4
  7.2 0.0 copy-start.3
  7.2 0.0 all-gather.2.cloned.1.call-start
  7.2 0.7 all-gather.2.cloned.1.call-update
  7.9 0.0 reduce-scatter.2.cloned.1.call-start
  8.0 74.1 %all-gather.2.cloned.1.call-done = bf16[4096,512]{1,0:T(8,128)(2,1)} async-done(((bf16[128,512]{1,0:T(8,128)(2,1)}), bf16[4096,512]{1,0:T(8,128)(2,1)}) %all-gather.2.cloned.1.call-update) | async-done | bytes 4194320 | tf_op jit(solution)/shard_map/all_gather | solution.py:25
  82.1 2.5 broadcast_in_dim.4
  84.6 0.0 copy-done.4
  84.6 0.0 copy-done.3
  84.6 6.0 while.10
  85.3 0.6 dynamic_slice.31
  86.5 0.6 dynamic_slice.32
  87.8 2.2 fusion.16
  90.7 0.0 copy-start.1
  90.7 0.0 copy-start.2
  90.7 3.8 convert_element_type.12
  94.5 0.0 reduce-scatter.2.cloned.1.call-update
  94.5 0.0 all-reduce.2.cloned.1.call-start
  94.6 274.6 %reduce-scatter.2.cloned.1.call-done = bf16[128,512]{1,0:T(8,128)(2,1)} async-done(((bf16[2048,512]{1,0:T(8,128)(2,1)}), bf16[128,512]{1,0:T(8,128)(2,1)}) %reduce-scatter.2.cloned.1.call-update) | async-done | bytes 131088 | tf_op jit(solution)/shard_map/reduce_scatter | solution.py:33
  369.2 0.0 copy-done
  369.2 0.0 copy-done.1
  369.2 0.0 copy-done.2
  369.2 1.9 fusion.7
  371.1 2.3 fusion.5
  373.4 0.0 all-reduce.2.cloned.1.call-update
  373.4 101.2 %psum.15 = f32[512]{0:T(512)} all-reduce(f32[512]{0:T(512)S(1)} %get-tuple-element.56), channel_id=1, replica_groups=mesh['row'=32,'col'=16] {'row','col'}, use_global_device_ids=true, to_apply=%region_5.6 | all-reduce | flops 512 | bytes 4096 | tf_op jit(solution)/shard_map/psum | solution.py:50
  474.6 174.0 %all-reduce.2.cloned.1.call-done = f32[512,512]{1,0:T(8,128)} async-done(((f32[512,512]{1,0:T(8,128)}), f32[512,512]{1,0:T(8,128)}) %all-reduce.2.cloned.1.call-update) | async-done | bytes 1048592 | tf_op jit(solution)/shard_map/psum | solution.py:50
  648.6 2.3 copy.19
Async XLA Ops:
  7.2 362.0 %copy-start = (bf16[512,512]{1,0:T(8,128)(2,1)S(1)}, bf16[512,512]{1,0:T(8,128)(2,1)}, u32[]{:S(2)}) copy-start(bf16[512,512]{1,0:T(8,128)(2,1)} %param.11) | copy-start | bytes 1572868
  7.2 77.4 %copy-start.4 = (s32[1,1,11]{2,1,0:T(1,128)S(1)}, s32[1,1,11]{2,1,0:T(1,128)}, u32[]{:S(2)}) copy-start(s32[1,1,11]{2,1,0:T(1,128)} %param.16) | copy-start | bytes 136
  7.2 77.4 %copy-start.3 = (s32[1,1,11]{2,1,0:T(1,128)S(1)}, s32[1,1,11]{2,1,0:T(1,128)}, u32[]{:S(2)}) copy-start(s32[1,1,11]{2,1,0:T(1,128)} %param.15) | copy-start | bytes 136
  7.2 74.9 %all-gather.2.cloned.1.call-start = ((), (), s32[]{:S(2)}) async-start(), calls=%async_computation.1 | async-start | bytes 4325376 | tf_op jit(solution)/shard_map/all_gather | solution.py:25
  7.9 361.3 %reduce-scatter.2.cloned.1.call-start = ((), (), s32[]{:S(2)}) async-start(), calls=%async_computation.2 | async-start | bytes 2228224 | tf_op jit(solution)/shard_map/reduce_scatter | solution.py:33
  90.7 278.6 %copy-start.1 = (bf16[128,512]{1,0:T(8,128)(2,1)S(1)}, bf16[128,512]{1,0:T(8,128)(2,1)}, u32[]{:S(2)}) copy-start(bf16[128,512]{1,0:T(8,128)(2,1)} %param.13) | copy-start | bytes 393220
  90.7 278.5 %copy-start.2 = (f32[512]{0:T(512)S(1)}, f32[512]{0:T(512)}, u32[]{:S(2)}) copy-start(f32[512]{0:T(512)} %param.12) | copy-start | bytes 6148
  94.5 554.1 %all-reduce.2.cloned.1.call-start = ((), (), s32[]{:S(2)}) async-start(), calls=%async_computation.3 | async-start | bytes 2097152 | tf_op jit(solution)/shard_map/psum | solution.py:50
Sparse Core Ops, SparseCore 0:
  10.2 71.8 all-gather.1
  94.6 274.5 reduce-scatter.1
  375.6 272.9 all-reduce.1
where the time goes:
time: 658 us; the launch traced here: 657 us
  waiting for transfers between devices  523 us (79%)
  blocking collectives  101 us (15%)
  between operations  13.8 us (2%)
    reduce_scatter x1, waiting for transfers between devices, per_device(): lax.psum_scatter(lax.fori_loop(0, used, own_step, buffer).astype(jnp.bflo...  275 us
    psum x1, waiting for transfers between devices, per_device(): lax.psum((local_weight, local_bias), ('row', 'col'))  174 us
    psum x1, blocking collectives, per_device(): lax.psum((local_weight, local_bias), ('row', 'col'))  101 us
    all_gather x1, waiting for transfers between devices, per_device(): gathered = lax.all_gather(features, 'row', axis=0, tiled=True)  74.1 us
  transfers between devices with their start and end apart: 3, of which 3 were waited for; matrix products, arithmetic and copies ran while one was open for 0% of the time, Pallas kernels for 0%

commit v1 on v0

v1 whole, which is shorter than its diff:
```python
import jax
import jax.numpy as jnp
from jax import lax
from jax.experimental import pallas as pl
from jax.experimental.pallas import tpu as pltpu
from jax.sharding import PartitionSpec as P

F32 = jnp.float32
BF16 = jnp.bfloat16
LANES = 128
VMEM = pl.BlockSpec(memory_space=pltpu.VMEM)
SMEM = pl.BlockSpec(memory_space=pltpu.SMEM)
PARAMS = pltpu.CompilerParams(vmem_limit_bytes=40 * 1024 * 1024)


def tile_kernel(rows_ref, cols_ref, count_ref, tiles_ref, block_ref, out_ref, total):
    size = tiles_ref.shape[1]
    total[...] = jnp.zeros_like(total)

    def step(slot, carry):
        rows = pl.ds(pl.multiple_of(rows_ref[slot] * size, size), size)
        window = pl.ds(pl.multiple_of(cols_ref[slot] * size, size), size)
        total[rows, :] += jnp.dot(
            tiles_ref[slot], block_ref[window, :], preferred_element_type=F32
        )
        return carry

    lax.fori_loop(0, count_ref[0], step, 0)
    out_ref[...] = total[...].astype(BF16)


def split_column(column):
    high = column.astype(BF16)
    low = (column - high.astype(F32)).astype(BF16)
    lane = lax.broadcasted_iota(jnp.int32, column.shape, 1)
    return jnp.where(lane == 0, high.astype(F32), jnp.where(lane == 1, low.astype(F32), 0.0)).astype(BF16)


def node_kernel(shares_ref, weight_ref, bias_ref, cot_ref, act_ref, grads_ref):
    width = weight_ref.shape[1]
    total = shares_ref[0].astype(F32)
    for share in range(1, shares_ref.shape[0]):
        total = total + shares_ref[share].astype(F32)
    aggregated = total.astype(BF16)
    preact = jnp.dot(aggregated, weight_ref[...], preferred_element_type=F32) + bias_ref[...]
    sigmoid_part = jax.nn.sigmoid(preact)
    act_ref[...] = (preact * sigmoid_part).astype(BF16)
    grad = cot_ref[...].astype(F32) * sigmoid_part * (1.0 + preact * (1.0 - sigmoid_part))
    rounded = grad.astype(BF16)
    rest = (grad - rounded.astype(F32)).astype(BF16)
    over_nodes = (((0,), (0,)), ((), ()))
    grads_ref[:, :width] = lax.dot_general(
        aggregated, rounded, over_nodes, preferred_element_type=F32
    ).astype(BF16)
    ones = jnp.ones((grad.shape[0], LANES), BF16)
    column = lax.dot_general(rounded, ones, over_nodes, preferred_element_type=F32)
    column = column + lax.dot_general(rest, ones, over_nodes, preferred_element_type=F32)
    grads_ref[:, width:] = split_column(column)


def sum_kernel(parts_ref, out_ref):
    width = parts_ref.shape[2] - LANES
    total = parts_ref[0].astype(F32)
    for part in range(1, parts_ref.shape[0]):
        total = total + parts_ref[part].astype(F32)
    main = total[:, :width].astype(BF16)
    column = total[:, width : width + 1] + total[:, width + 1 : width + 2]
    side = split_column(jnp.broadcast_to(column, (column.shape[0], LANES)))
    for copy in range(out_ref.shape[0]):
        out_ref[copy, :, :width] = main
        out_ref[copy, :, width:] = side


def sum_parts(parts, copies):
    return pl.pallas_call(
        sum_kernel,
        out_shape=jax.ShapeDtypeStruct((copies,) + parts.shape[1:], BF16),
        in_specs=[VMEM],
        out_specs=VMEM,
        compiler_params=PARAMS,
    )(parts)


def per_device(
    features, weight, bias_term, cotangent, tile_values, tile_rows, tile_cols, tile_count
):
    n_rows, n_cols = lax.axis_size("row"), lax.axis_size("col")
    nodes, width = features.shape
    height = n_cols * nodes
    gathered = lax.all_gather(features, "row", axis=0, tiled=True)
    term = pl.pallas_call(
        tile_kernel,
        out_shape=jax.ShapeDtypeStruct((height, width), BF16),
        in_specs=[SMEM, SMEM, SMEM, VMEM, VMEM],
        out_specs=VMEM,
        scratch_shapes=[pltpu.VMEM((height, width), F32)],
        compiler_params=PARAMS,
    )(tile_rows[0, 0], tile_cols[0, 0], tile_count[0], tile_values[0, 0], gathered)
    shares = lax.all_to_all(term.reshape(n_cols, nodes, width), "col", 0, 0)
    activations, grads = pl.pallas_call(
        node_kernel,
        out_shape=(
            jax.ShapeDtypeStruct((nodes, width), BF16),
            jax.ShapeDtypeStruct((width, width + LANES), BF16),
        ),
        in_specs=[VMEM] * 4,
        out_specs=(VMEM, VMEM),
        compiler_params=PARAMS,
    )(shares, weight, bias_term[None, :], cotangent)
    chunk = width // n_rows
    grads = lax.all_to_all(grads.reshape(n_rows, chunk, width + LANES), "row", 0, 0)
    grads = lax.all_to_all(sum_parts(grads, n_cols), "col", 0, 0)
    grads = lax.all_to_all(sum_parts(grads, n_rows), "row", 0, 0)
    grads = grads.reshape(width, width + LANES).astype(F32)
    weight_grad = grads[:, :width]
    bias_grad = grads[:, width] + grads[:, width + 1]
    return activations, weight_grad, bias_grad


def solution(mesh):
    return jax.shard_map(
        per_device,
        mesh=mesh,
        in_specs=(
            P(("row", "col"), None),
            P(),
            P(),
            P(("row", "col"), None),
            P("row", "col", None, None, None),
            P("row", "col", None),
            P("row", "col", None),
            P("row", "col"),
        ),
        out_specs=(P(("row", "col"), None), P(), P()),
        check_vma=False,
    )
```

time: 658 us -> 231 us (0.35)
  waiting for transfers between devices: 523 us -> 74.2 us
  blocking collectives: 101 us -> 132 us
    reduce_scatter x1 -> x0, waiting for transfers between devices: 275 us -> none  [per_device(): lax.psum_scatter(lax.fori_loop(0, used, own_step, buffer).astype(jnp.bflo...]
    psum x1 -> x0, waiting for transfers between devices: 174 us -> none  [per_device(): lax.psum((local_weight, local_bias), ('row', 'col'))]
    all_to_all x0 -> x4, blocking collectives: none -> 132 us  [the longest x1 61.5 us: per_device(): shares = lax.all_to_all(term.reshape(n_cols, nodes, width), 'col', 0, 0)]
    psum x1 -> x0, blocking collectives: 101 us -> none  [per_device(): lax.psum((local_weight, local_bias), ('row', 'col'))]
  transfers between devices with their start and end apart: 3 -> 1, of which waited for: 3 -> 1; matrix products, arithmetic and copies ran while one was open for 0% -> 0% of each run, Pallas kernels for 0% -> 0%
where the time goes in v1:
time: 231 us; the launch traced here: 230 us
  blocking collectives  132 us (57%)
  waiting for transfers between devices  74.2 us (32%)
  between operations  14.7 us (6%)
  local copies, waits for them, and re-layouts  5.99 us (3%)
  Pallas kernels  2.68 us (1%)
    all_gather x1, waiting for transfers between devices, per_device(): gathered = lax.all_gather(features, 'row', axis=0, tiled=True)  73.5 us
    all_to_all x1, blocking collectives, per_device(): shares = lax.all_to_all(term.reshape(n_cols, nodes, width), 'col', 0, 0)  61.5 us
    all_to_all x1, blocking collectives, per_device(): lax.all_to_all(grads.reshape(n_rows, chunk, width + LANES), 'row', 0, 0)  27 us
    all_to_all x1, blocking collectives, per_device(): grads = lax.all_to_all(sum_parts(grads, n_rows), 'row', 0, 0)  24 us
    all_to_all x1, blocking collectives, per_device(): grads = lax.all_to_all(sum_parts(grads, n_cols), 'col', 0, 0)  19.3 us
    unnamed x14, local copies, waits for them, and re-layouts  4.88 us
  transfers between devices with their start and end apart: 1, of which 1 were waited for; matrix products, arithmetic and copies ran while one was open for 0% of the time, Pallas kernels for 0%

profile of v1, /device:TPU:1, one launch (start us, length us, event | category | flops | bytes accessed | tf_op | source)
XLA Modules:
  0.0 230.3 jit_solution(7067627815035510328)
XLA Ops:
  7.2 0.0 all-gather.2.cloned.1.call-start
  7.2 0.7 all-gather.2.cloned.1.call-update
  8.5 73.5 %all-gather.2.cloned.1.call-done.block_ref = bf16[4096,512]{1,0:T(8,128)(2,1)} async-done(((bf16[128,512]{1,0:T(8,128)(2,1)}), bf16[4096,512]{1,0:T(8,128)(2,1)}) %all-gather.2.cloned.1.call-update) | async-done | bytes 4194320 | tf_op jit(solution)/shard_map/all_gather | solution.py:90
  82.1 0.0 copy-start
  82.1 2.2 copy-done
  84.3 0.0 copy-start.1
  84.3 1.4 copy-done.1
  85.6 0.0 copy-start.5
  85.6 0.7 copy-done.5
  86.3 0.0 copy-start.6
  86.3 0.7 copy-done.6
  86.9 1.2 shard_map.103
  88.2 0.0 copy-start.2
  88.2 0.0 copy-start.3
  88.2 0.0 copy-start.4
  88.2 61.5 %all_to_all.20.shares_ref = bf16[16,128,512]{2,1,0:T(8,128)(2,1)S(1)} all-to-all(bf16[16,128,512]{2,1,0:T(8,128)(2,1)S(1)} %bitcast.11), channel_id=1, replica_groups=mesh['row'=32,'col'=16] {'col'}, dimensions={0} | all-to-all | bytes 4194304 | tf_op jit(solution)/shard_map/all_to_all | solution.py:99
  149.7 0.0 copy-done.2
  149.7 0.0 copy-done.3
  149.7 0.0 copy-done.4
  149.7 1.1 shard_map.104
  150.8 27.0 %all_to_all.21.parts_ref = bf16[32,16,640]{2,1,0:T(8,128)(2,1)S(1)} all-to-all(bf16[32,16,640]{2,1,0:T(8,128)(2,1)S(1)} %bitcast.13), channel_id=1, replica_groups=mesh['row'=32,'col'=16] {'row'}, dimensions={0} | all-to-all | bytes 1310720 | tf_op jit(solution)/shard_map/all_to_all | solution.py:111
  177.7 0.2 shard_map.105
  177.9 19.3 %all_to_all.22.parts_ref = bf16[16,16,640]{2,1,0:T(8,128)(2,1)S(1)} all-to-all(bf16[16,16,640]{2,1,0:T(8,128)(2,1)S(1)} %shard_map.105), channel_id=1, replica_groups=mesh['row'=32,'col'=16] {'col'}, dimensions={0} | all-to-all | bytes 655360 | tf_op jit(solution)/shard_map/all_to_all | solution.py:112
  197.2 0.2 shard_map.106
  197.4 24.0 %all_to_all.23 = bf16[32,16,640]{2,1,0:T(8,128)(2,1)S(1)} all-to-all(bf16[32,16,640]{2,1,0:T(8,128)(2,1)S(1)} %shard_map.106), channel_id=1, replica_groups=mesh['row'=32,'col'=16] {'row'}, dimensions={0} | all-to-all | bytes 1310720 | tf_op jit(solution)/shard_map/all_to_all | solution.py:113
  221.4 0.1 bitcast_convert_fusion
  221.6 0.8 fusion
  222.4 1.1 slice.12
Async XLA Ops:
  7.2 74.9 %all-gather.2.cloned.1.call-start = ((), (), s32[]{:S(2)}) async-start(), calls=%async_computation.4 | async-start | bytes 4325376 | tf_op jit(solution)/shard_map/all_gather | solution.py:90
  82.1 2.2 copy-start
  84.3 1.4 copy-start.1
  85.6 0.7 copy-start.5
  86.3 0.7 copy-start.6
  88.2 61.5 %copy-start.2 = (bf16[512,512]{1,0:T(8,128)(2,1)S(1)}, bf16[512,512]{1,0:T(8,128)(2,1)}, u32[]{:S(2)}) copy-start(bf16[512,512]{1,0:T(8,128)(2,1)} %weight_ref.1) | copy-start | bytes 1572868
  88.2 61.5 %copy-start.3 = (bf16[128,512]{1,0:T(8,128)(2,1)S(1)}, bf16[128,512]{1,0:T(8,128)(2,1)}, u32[]{:S(2)}) copy-start(bf16[128,512]{1,0:T(8,128)(2,1)} %cot_ref.1) | copy-start | bytes 393220
  88.2 61.5 %copy-start.4 = (f32[512]{0:T(512)S(1)}, f32[512]{0:T(512)}, u32[]{:S(2)}) copy-start(f32[512]{0:T(512)} %param.10) | copy-start | bytes 6148
Sparse Core Ops, SparseCore 0:
  10.1 71.8 all-gather.1

commit v2 on v1

--- a/solution.py
+++ b/solution.py
@@ -3,30 +3,87 @@
 from jax import lax
 from jax.experimental import pallas as pl
 from jax.experimental.pallas import tpu as pltpu
-from jax.sharding import PartitionSpec as P
+from jax.sharding import Mesh, PartitionSpec as P
 
 F32 = jnp.float32
 BF16 = jnp.bfloat16
 LANES = 128
 VMEM = pl.BlockSpec(memory_space=pltpu.VMEM)
 SMEM = pl.BlockSpec(memory_space=pltpu.SMEM)
+ANY = pl.BlockSpec(memory_space=pl.ANY)
 PARAMS = pltpu.CompilerParams(vmem_limit_bytes=40 * 1024 * 1024)
-
-
-def tile_kernel(rows_ref, cols_ref, count_ref, tiles_ref, block_ref, out_ref, total):
-    size = tiles_ref.shape[1]
+AXES = ("z_lo", "x", "core", "z_hi", "y_pair", "y_odd")
+ROW = ("z_lo", "x", "core")
+COL = ("z_hi", "y_pair", "y_odd")
+Y = ("y_pair", "y_odd")
+Z_LO, X, Y_SIZE = 4, 4, 8
+
+
+def tile_kernel(
+    place_ref, rows_ref, cols_ref, count_ref, tiles_ref, *refs
+):
+    own, other = refs[:5], refs[5:10]
+    keep_ref, left_ref, right_ref, tiles, windows, total, sems = refs[10:]
+    slots, size, _ = tiles.shape
+    half = size // 2
+    lanes = left_ref.shape[2]
+    z, x, core, odd = place_ref[0], place_ref[1], place_ref[2], place_ref[3]
+    used = count_ref[0]
+
+    def tile_copy(slot):
+        return pltpu.make_async_copy(tiles_ref.at[slot], tiles.at[slot], sems.at[0, slot])
+
+    def half_copy(ref, index, slot, which):
+        return pltpu.make_async_copy(ref.at[index], windows.at[slot, which], sems.at[1 + which, slot])
+
+    def fetch(slot, carry):
+        tile_copy(slot).start()
+        chip = cols_ref[slot]
+        dz = lax.rem(z - chip // X + Z_LO, Z_LO)
+        dx = lax.rem(x - lax.rem(chip, X) + X, X)
+        late = dz >= Z_LO // 2
+        cases = (
+            (dx == 0, 0, dz),
+            (dx == 1, 1, dz),
+            (dx == 3, 2, dz),
+            (jnp.logical_and(dx == 2, jnp.logical_not(late)), 3, dz),
+            (jnp.logical_and(dx == 2, late), 4, dz - Z_LO // 2),
+        )
+        for condition, block, index in cases:
+
+            @pl.when(condition)
+            def _():
+                half_copy(own[block], index, slot, core).start()
+                half_copy(other[block], index, slot, 1 - core).start()
+
+        return carry
+
+    lax.fori_loop(0, used, fetch, 0)
     total[...] = jnp.zeros_like(total)
 
     def step(slot, carry):
-        rows = pl.ds(pl.multiple_of(rows_ref[slot] * size, size), size)
-        window = pl.ds(pl.multiple_of(cols_ref[slot] * size, size), size)
-        total[rows, :] += jnp.dot(
-            tiles_ref[slot], block_ref[window, :], preferred_element_type=F32
-        )
+        tile_copy(slot).wait()
+        half_copy(own[0], 0, slot, 0).wait()
+        half_copy(own[0], 0, slot, 1).wait()
+        window = windows[slot].reshape(size, windows.shape[3])
+        total[rows_ref[slot]] += jnp.dot(tiles[slot], window, preferred_element_type=F32)
         return carry
 
-    lax.fori_loop(0, count_ref[0], step, 0)
-    out_ref[...] = total[...].astype(BF16)
+    lax.fori_loop(0, used, step, 0)
+    mine = pl.multiple_of(odd * half, half)
+    theirs = pl.multiple_of((1 - odd) * half, half)
+    for row in range(total.shape[0]):
+        keep_ref[row] = total[row, pl.ds(mine, half), :].astype(BF16)
+        send = total[row, pl.ds(theirs, half), :].astype(BF16)
+        left_ref[row] = send[:, :lanes]
+        right_ref[row] = send[:, lanes:]
+
+
+def pair_kernel(keep_ref, left_ref, right_ref, out_ref):
+    lanes = left_ref.shape[2]
+    keep = keep_ref[...].astype(F32)
+    out_ref[:, :, :lanes] = (keep[:, :, :lanes] + left_ref[...].astype(F32)).astype(BF16)
+    out_ref[:, :, lanes:] = (keep[:, :, lanes:] + right_ref[...].astype(F32)).astype(BF16)
 
 
 def split_column(column):
@@ -81,22 +138,64 @@
     )(parts)
 
 
+def shift(array, axis, size, by):
+    return lax.ppermute(array, axis, [(i, (i + by) % size) for i in range(size)])
+
+
+def gather_row(features):
+    near = [features] + [shift(features, "z_lo", Z_LO, by) for by in range(1, Z_LO)]
+    own = jnp.stack(near)
+    left, right = shift(own, "x", X, 1), shift(own, "x", X, -1)
+    far_left = shift(left[: Z_LO // 2], "x", X, 1)
+    far_right = shift(right[Z_LO // 2 :], "x", X, -1)
+    blocks = [own, left, right, far_left, far_right]
+    return blocks, [shift(block, "core", 2, 1) for block in blocks]
+
+
 def per_device(
     features, weight, bias_term, cotangent, tile_values, tile_rows, tile_cols, tile_count
 ):
-    n_rows, n_cols = lax.axis_size("row"), lax.axis_size("col")
+    n_rows, n_cols = lax.axis_size(ROW), lax.axis_size(COL)
     nodes, width = features.shape
-    height = n_cols * nodes
-    gathered = lax.all_gather(features, "row", axis=0, tiled=True)
-    term = pl.pallas_call(
+    _, _, slots, size, _ = tile_values.shape
+    n_tiles = n_cols * nodes // size
+    own, other = gather_row(features)
+    place = jnp.stack([lax.axis_index(axis) for axis in ("z_lo", "x", "core", "y_odd")])
+    keep, left, right = pl.pallas_call(
         tile_kernel,
-        out_shape=jax.ShapeDtypeStruct((height, width), BF16),
-        in_specs=[SMEM, SMEM, SMEM, VMEM, VMEM],
+        out_shape=(
+            jax.ShapeDtypeStruct((n_tiles, nodes, width), BF16),
+            jax.ShapeDtypeStruct((n_tiles, nodes, width // 2), BF16),
+            jax.ShapeDtypeStruct((n_tiles, nodes, width // 2), BF16),
+        ),
+        in_specs=[SMEM] * 4 + [ANY] * 11,
+        out_specs=(VMEM, VMEM, VMEM),
+        scratch_shapes=[
+            pltpu.VMEM((slots, size, size), BF16),
+            pltpu.VMEM((slots, 2, size // 2, width), BF16),
+            pltpu.VMEM((n_tiles, size, width), F32),
+            pltpu.SemaphoreType.DMA((3, slots)),
+        ],
+        compiler_params=PARAMS,
+    )(
+        place.astype(jnp.int32),
+        tile_rows[0, 0],
+        tile_cols[0, 0],
+        tile_count[0],
+        tile_values[0, 0],
+        *own,
+        *other,
+    )
+    left = lax.ppermute(left, Y, [(i, i ^ 1) for i in range(Y_SIZE)])
+    right = lax.ppermute(right, Y, [(i, (i + 2 * (i % 2) - 1) % Y_SIZE) for i in range(Y_SIZE)])
+    paired = pl.pallas_call(
+        pair_kernel,
+        out_shape=jax.ShapeDtypeStruct((n_tiles, nodes, width), BF16),
+        in_specs=[VMEM] * 3,
         out_specs=VMEM,
-        scratch_shapes=[pltpu.VMEM((height, width), F32)],
-        compiler_params=PARAMS,
-    )(tile_rows[0, 0], tile_cols[0, 0], tile_count[0], tile_values[0, 0], gathered)
-    shares = lax.all_to_all(term.reshape(n_cols, nodes, width), "col", 0, 0)
+        compiler_params=PARAMS,
+    )(keep, left, right)
+    shares = lax.all_to_all(paired, ("z_hi", "y_pair"), 0, 0)
     activations, grads = pl.pallas_call(
         node_kernel,
         out_shape=(
@@ -108,9 +207,9 @@
         compiler_params=PARAMS,
     )(shares, weight, bias_term[None, :], cotangent)
     chunk = width // n_rows
-    grads = lax.all_to_all(grads.reshape(n_rows, chunk, width + LANES), "row", 0, 0)
-    grads = lax.all_to_all(sum_parts(grads, n_cols), "col", 0, 0)
-    grads = lax.all_to_all(sum_parts(grads, n_rows), "row", 0, 0)
+    grads = lax.all_to_all(grads.reshape(n_rows, chunk, width + LANES), ROW, 0, 0)
+    grads = lax.all_to_all(sum_parts(grads, n_cols), COL, 0, 0)
+    grads = lax.all_to_all(sum_parts(grads, n_rows), ROW, 0, 0)
     grads = grads.reshape(width, width + LANES).astype(F32)
     weight_grad = grads[:, :width]
     bias_grad = grads[:, width] + grads[:, width + 1]
@@ -118,19 +217,21 @@
 
 
 def solution(mesh):
+    cut = Mesh(mesh.devices.reshape(Z_LO, X, 2, 2, Y_SIZE // 2, 2), AXES)
+    everywhere = P(AXES, None)
     return jax.shard_map(
         per_device,
-        mesh=mesh,
+        mesh=cut,
         in_specs=(
-            P(("row", "col"), None),
+            everywhere,
             P(),
             P(),
-            P(("row", "col"), None),
-            P("row", "col", None, None, None),
-            P("row", "col", None),
-            P("row", "col", None),
-            P("row", "col"),
+            everywhere,
+            P(ROW, COL, None, None, None),
+            P(ROW, COL, None),
+            P(ROW, COL, None),
+            P(ROW, COL),
         ),
-        out_specs=(P(("row", "col"), None), P(), P()),
+        out_specs=(everywhere, P(), P()),
         check_vma=False,
     )

time: 231 us -> 204 us (0.88)
  starting transfers between devices: 0.04 us -> 49.7 us
  waiting for transfers between devices: 74.2 us -> 29.2 us
  blocking collectives: 132 us -> 115 us
  between operations: 14.7 us -> 1.53 us
  local copies, waits for them, and re-layouts: 5.99 us -> 1.18 us
    all_gather x1 -> x0, waiting for transfers between devices: 73.5 us -> none  [per_device(): gathered = lax.all_gather(features, 'row', axis=0, tiled=True)]
    ppermute x0 -> x14, starting transfers between devices: none -> 49.7 us  [the longest x12 41.6 us: shift(): lax.ppermute(array, axis, [(i, (i + by) % size) for i in range(size)])]
    ppermute x0 -> x14, waiting for transfers between devices: none -> 29.2 us  [the longest x12 19.7 us: shift(): lax.ppermute(array, axis, [(i, (i + by) % size) for i in range(size)])]
    all_to_all x4, blocking collectives: 132 us -> 115 us  [the longest x1 41.4 us: per_device(): shares = lax.all_to_all(paired, ('z_hi', 'y_pair'), 0, 0)]
    unnamed x14 -> x12, local copies, waits for them, and re-layouts: 4.88 us -> 0.03 us
  transfers between devices with their start and end apart: 1 -> 14, of which waited for: 1 -> 6; matrix products, arithmetic and copies ran while one was open for 0% -> 0% of each run, Pallas kernels for 0% -> 0%
where the time goes in v2:
time: 204 us; the launch traced here: 203 us
  blocking collectives  115 us (56%)
  starting transfers between devices  49.7 us (24%)
  waiting for transfers between devices  29.2 us (14%)
  Pallas kernels  4.48 us (2%)
    ppermute x12, starting transfers between devices, shift(): lax.ppermute(array, axis, [(i, (i + by) % size) for i in range(size)])  41.6 us
    all_to_all x1, blocking collectives, per_device(): shares = lax.all_to_all(paired, ('z_hi', 'y_pair'), 0, 0)  41.4 us
    all_to_all x1, blocking collectives, per_device(): lax.all_to_all(grads.reshape(n_rows, chunk, width + LANES), ROW, 0, 0)  31.9 us
    all_to_all x1, blocking collectives, per_device(): grads = lax.all_to_all(sum_parts(grads, n_rows), ROW, 0, 0)  23.7 us
    ppermute x12, waiting for transfers between devices, shift(): lax.ppermute(array, axis, [(i, (i + by) % size) for i in range(size)])  19.7 us
    all_to_all x1, blocking collectives, per_device(): grads = lax.all_to_all(sum_parts(grads, n_cols), COL, 0, 0)  17.9 us
    ppermute x1, waiting for transfers between devices, per_device(): lax.ppermute(right, Y, [(i, (i + 2 * (i % 2) - 1) % Y_SIZE) for i in rang...  6.45 us
    ppermute x1, starting transfers between devices, per_device(): lax.ppermute(right, Y, [(i, (i + 2 * (i % 2) - 1) % Y_SIZE) for i in rang...  5.27 us
  transfers between devices with their start and end apart: 14, of which 6 were waited for; matrix products, arithmetic and copies ran while one was open for 0% of the time, Pallas kernels for 0%

profile of v2, /device:TPU:1, one launch (start us, length us, event | category | flops | bytes accessed | tf_op | source)
XLA Modules:
  0.0 203.0 jit_solution(6986618695062907467)
XLA Ops:
  0.6 0.0 copy-start.5
  0.6 0.0 copy-start.4
  0.7 0.0 copy-start
  0.7 5.0 %collective-permute-start = (bf16[128,512]{1,0:T(8,128)(2,1)}, bf16[128,512]{1,0:T(8,128)(2,1)S(1)}, u32[]{:S(2)}, u32[]{:S(2)}) collective-permute-start(bf16[128,512]{1,0:T(8,128)(2,1)} %param.8), channel_id=1, source_target_pairs={{0,128},{128,256},{256,384},{384,0},{1,129},{129,257},{257,385},{3... | collective-permute-start | bytes 393224 | tf_op jit(solution)/shard_map/ppermute | solution.py:142
  5.6 5.5 %collective-permute-start.2 = (bf16[128,512]{1,0:T(8,128)(2,1)}, bf16[128,512]{1,0:T(8,128)(2,1)S(1)}, u32[]{:S(2)}, u32[]{:S(2)}) collective-permute-start(bf16[128,512]{1,0:T(8,128)(2,1)} %param.8), channel_id=1, source_target_pairs={{0,384},{128,0},{256,128},{384,256},{1,385},{129,1},{257,129},{385... | collective-permute-start | bytes 393224 | tf_op jit(solution)/shard_map/ppermute | solution.py:142
  11.2 2.2 %collective-permute-start.1 = (bf16[128,512]{1,0:T(8,128)(2,1)}, bf16[128,512]{1,0:T(8,128)(2,1)S(1)}, u32[]{:S(2)}, u32[]{:S(2)}) collective-permute-start(bf16[128,512]{1,0:T(8,128)(2,1)} %param.8), channel_id=1, source_target_pairs={{0,256},{128,384},{256,0},{384,128},{1,257},{129,385},{257,1},{385... | collective-permute-start | bytes 393224 | tf_op jit(solution)/shard_map/ppermute | solution.py:142
  13.4 0.0 collective-permute-done
  13.4 0.0 collective-permute-done.2
  13.4 7.6 %collective-permute-done.1 = bf16[128,512]{1,0:T(8,128)(2,1)S(1)} collective-permute-done((bf16[128,512]{1,0:T(8,128)(2,1)}, bf16[128,512]{1,0:T(8,128)(2,1)S(1)}, u32[]{:S(2)}, u32[]{:S(2)}) %collective-permute-start.1) | collective-permute-done | bytes 131104 | tf_op jit(solution)/shard_map/ppermute | solution.py:142
  21.0 1.0 pad_maximum_fusion.refs_0_
  22.0 4.9 %collective-permute-start.4 = (bf16[4,128,512]{2,1,0:T(8,128)(2,1)S(1)}, bf16[4,128,512]{2,1,0:T(8,128)(2,1)S(1)}, u32[]{:S(2)}, u32[]{:S(2)}) collective-permute-start(bf16[4,128,512]{2,1,0:T(8,128)(2,1)S(1)} %pad_maximum_fusion.refs_0_), channel_id=1, source_target_pairs={{0,96},{32,0},{64,32},{96,64},{1,97},{33,1},{65,33},{97,65},{2,98}... | collective-permute-start | bytes 1572872 | tf_op jit(solution)/shard_map/ppermute | solution.py:142
  26.9 1.9 collective-permute-start.3
  28.8 3.3 %collective-permute-start.7 = (bf16[4,128,512]{2,1,0:T(8,128)(2,1)S(1)}, bf16[4,128,512]{2,1,0:T(8,128)(2,1)S(1)}, u32[]{:S(2)}, u32[]{:S(2)}) collective-permute-start(bf16[4,128,512]{2,1,0:T(8,128)(2,1)S(1)} %pad_maximum_fusion.refs_0_), channel_id=1, source_target_pairs={{0,16},{16,0},{1,17},{17,1},{2,18},{18,2},{3,19},{19,3},{4,20},{20... | collective-permute-start | bytes 1572872 | tf_op jit(solution)/shard_map/ppermute | solution.py:142
  32.0 5.1 %collective-permute-done.4.refs_2_ = bf16[4,128,512]{2,1,0:T(8,128)(2,1)S(1)} collective-permute-done((bf16[4,128,512]{2,1,0:T(8,128)(2,1)S(1)}, bf16[4,128,512]{2,1,0:T(8,128)(2,1)S(1)}, u32[]{:S(2)}, u32[]{:S(2)}) %collective-permute-start.4) | collective-permute-done | bytes 524320 | tf_op jit(solution)/shard_map/ppermute | solution.py:142
  37.2 5.3 %collective-permute-start.6 = (bf16[2,128,512]{2,1,0:T(8,128)(2,1)S(1)}, bf16[2,128,512]{2,1,0:T(8,128)(2,1)}, u32[]{:S(2)}, u32[]{:S(2)}) collective-permute-start(bf16[2,128,512]{2,1,0:T(8,128)(2,1)S(1)} %slice.21), channel_id=1, source_target_pairs={{0,96},{32,0},{64,32},{96,64},{1,97},{33,1},{65,33},{97,65},{2,98}... | collective-permute-start | bytes 786440 | tf_op jit(solution)/shard_map/ppermute | solution.py:142
  42.5 4.0 %collective-permute-start.9 = (bf16[4,128,512]{2,1,0:T(8,128)(2,1)S(1)}, bf16[4,128,512]{2,1,0:T(8,128)(2,1)}, u32[]{:S(2)}, u32[]{:S(2)}) collective-permute-start(bf16[4,128,512]{2,1,0:T(8,128)(2,1)S(1)} %collective-permute-done.4.refs_2_), channel_id=1, source_target_pairs={{0,16},{16,0},{1,17},{17,1},{2,18},{18,2},{3,19},{19,3},{4,20},{20... | collective-permute-start | bytes 1572872 | tf_op jit(solution)/shard_map/ppermute | solution.py:142
  46.5 0.0 collective-permute-done.3.refs_1_
  46.6 1.9 collective-permute-start.8
  48.5 1.9 collective-permute-start.5
  50.4 0.0 collective-permute-done.6.refs_4_
  50.4 2.4 %collective-permute-start.11 = (bf16[2,128,512]{2,1,0:T(8,128)(2,1)}, bf16[2,128,512]{2,1,0:T(8,128)(2,1)}, u32[]{:S(2)}, u32[]{:S(2)}) collective-permute-start(bf16[2,128,512]{2,1,0:T(8,128)(2,1)} %collective-permute-done.6.refs_4_), channel_id=1, source_target_pairs={{0,16},{16,0},{1,17},{17,1},{2,18},{18,2},{3,19},{19,3},{4,20},{20... | collective-permute-start | bytes 786440 | tf_op jit(solution)/shard_map/ppermute | solution.py:142
  52.8 6.2 %collective-permute-done.5.refs_3_ = bf16[2,128,512]{2,1,0:T(8,128)(2,1)} collective-permute-done((bf16[2,128,512]{2,1,0:T(8,128)(2,1)S(1)}, bf16[2,128,512]{2,1,0:T(8,128)(2,1)}, u32[]{:S(2)}, u32[]{:S(2)}) %collective-permute-start.5) | collective-permute-done | bytes 262176 | tf_op jit(solution)/shard_map/ppermute | solution.py:142
  59.1 3.2 %collective-permute-start.10 = (bf16[2,128,512]{2,1,0:T(8,128)(2,1)}, bf16[2,128,512]{2,1,0:T(8,128)(2,1)}, u32[]{:S(2)}, u32[]{:S(2)}) collective-permute-start(bf16[2,128,512]{2,1,0:T(8,128)(2,1)} %collective-permute-done.5.refs_3_), channel_id=1, source_target_pairs={{0,16},{16,0},{1,17},{17,1},{2,18},{18,2},{3,19},{19,3},{4,20},{20... | collective-permute-start | bytes 786440 | tf_op jit(solution)/shard_map/ppermute | solution.py:142
  63.0 0.1 pad_add_fusion.place_ref
  63.1 0.0 collective-permute-done.7.refs_5_
  63.1 0.0 collective-permute-done.9.refs_7_
  63.1 0.0 collective-permute-done.8.refs_6_
  63.1 0.0 collective-permute-done.11.refs_9_
  63.1 0.7 collective-permute-done.10.refs_8_
  63.8 2.9 %shard_map.103 = (bf16[8,128,512]{2,1,0:T(8,128)(2,1)S(1)}, bf16[8,128,256]{2,1,0:T(8,128)(2,1)S(1)}, bf16[8,128,256]{2,1,0:T(8,128)(2,1)S(1)}) custom-call(s32[4]{0:T(128)S(1)} %pad_add_fusion.place_ref, s32[11]{0:T(128)S(1)} %bitcast.21, s32[11]{0:T(128)S(1)} %bitcast.22, s32[1]{0:T(128)} %bitcast.17.count_ref, bf16[11,256,256]{2,1,0:T(8,128)(2,1)S(1)} %bitcast.18, ...), custom_call_target="tpu_custom_call" | custom-call | tf_op jit(solution)/shard_map/pallas_call | solution.py:164
  66.7 2.9 %collective-permute-start.12 = (bf16[8,128,256]{2,1,0:T(8,128)(2,1)S(1)}, bf16[8,128,256]{2,1,0:T(8,128)(2,1)S(1)}, u32[]{:S(2)}, u32[]{:S(2)}) collective-permute-start(bf16[8,128,256]{2,1,0:T(8,128)(2,1)S(1)} %get-tuple-element.9), channel_id=1, source_target_pairs={{0,1},{1,0},{2,3},{3,2},{4,5},{5,4},{6,7},{7,6},{8,9},{9,8},{10,11... | collective-permute-start | bytes 1572872 | tf_op jit(solution)/shard_map/ppermute | solution.py:189
  69.6 5.3 %collective-permute-start.13 = (bf16[8,128,256]{2,1,0:T(8,128)(2,1)S(1)}, bf16[8,128,256]{2,1,0:T(8,128)(2,1)S(1)}, u32[]{:S(2)}, u32[]{:S(2)}) collective-permute-start(bf16[8,128,256]{2,1,0:T(8,128)(2,1)S(1)} %get-tuple-element.10), channel_id=1, source_target_pairs={{0,7},{1,2},{2,1},{3,4},{4,3},{5,6},{6,5},{7,0},{8,15},{9,10},{10,... | collective-permute-start | bytes 1572872 | tf_op jit(solution)/shard_map/ppermute | solution.py:190
  74.9 3.0 %collective-permute-done.12.left_ref = bf16[8,128,256]{2,1,0:T(8,128)(2,1)S(1)} collective-permute-done((bf16[8,128,256]{2,1,0:T(8,128)(2,1)S(1)}, bf16[8,128,256]{2,1,0:T(8,128)(2,1)S(1)}, u32[]{:S(2)}, u32[]{:S(2)}) %collective-permute-start.12) | collective-permute-done | bytes 524320 | tf_op jit(solution)/shard_map/ppermute | solution.py:189
  77.9 6.4 %collective-permute-done.13.right_ref = bf16[8,128,256]{2,1,0:T(8,128)(2,1)S(1)} collective-permute-done((bf16[8,128,256]{2,1,0:T(8,128)(2,1)S(1)}, bf16[8,128,256]{2,1,0:T(8,128)(2,1)S(1)}, u32[]{:S(2)}, u32[]{:S(2)}) %collective-permute-start.13) | collective-permute-done | bytes 524320 | tf_op jit(solution)/shard_map/ppermute | solution.py:190
  84.4 0.3 shard_map.104
  84.6 0.0 copy-start.1
  84.6 0.0 copy-start.2
  84.7 0.0 copy-start.3
  84.7 41.4 %all_to_all.20.shares_ref = bf16[8,128,512]{2,1,0:T(8,128)(2,1)S(1)} all-to-all(bf16[8,128,512]{2,1,0:T(8,128)(2,1)S(1)} %shard_map.104), channel_id=1, replica_groups=mesh['z_lo'=4,'x'=4,'core'=2,'z_hi'=2,'y_pair'=4,'y_odd'=2] {'z_hi','y_p..., dimensions={0} | all-to-all | bytes 2097152 | tf_op jit(solution)/shard_map/all_to_all | solution.py:198
  126.1 1.0 shard_map.105
  127.1 31.9 %all_to_all.21.parts_ref = bf16[32,16,640]{2,1,0:T(8,128)(2,1)S(1)} all-to-all(bf16[32,16,640]{2,1,0:T(8,128)(2,1)S(1)} %bitcast.19), channel_id=1, replica_groups=mesh['z_lo'=4,'x'=4,'core'=2,'z_hi'=2,'y_pair'=4,'y_odd'=2] {'z_lo','x',..., dimensions={0} | all-to-all | bytes 1310720 | tf_op jit(solution)/shard_map/all_to_all | solution.py:210
  158.9 0.2 shard_map.106
  159.1 17.9 %all_to_all.22.parts_ref = bf16[16,16,640]{2,1,0:T(8,128)(2,1)S(1)} all-to-all(bf16[16,16,640]{2,1,0:T(8,128)(2,1)S(1)} %shard_map.106), channel_id=1, replica_groups=mesh['z_lo'=4,'x'=4,'core'=2,'z_hi'=2,'y_pair'=4,'y_odd'=2] {'z_hi','y_p..., dimensions={0} | all-to-all | bytes 655360 | tf_op jit(solution)/shard_map/all_to_all | solution.py:211
  177.0 0.2 shard_map.107
  177.2 23.7 %all_to_all.23 = bf16[32,16,640]{2,1,0:T(8,128)(2,1)S(1)} all-to-all(bf16[32,16,640]{2,1,0:T(8,128)(2,1)S(1)} %shard_map.107), channel_id=1, replica_groups=mesh['z_lo'=4,'x'=4,'core'=2,'z_hi'=2,'y_pair'=4,'y_odd'=2] {'z_lo','x',..., dimensions={0} | all-to-all | bytes 1310720 | tf_op jit(solution)/shard_map/all_to_all | solution.py:212
  200.9 0.1 bitcast_convert_fusion
  201.0 0.8 fusion
  201.9 1.1 slice.22
  (8 shorter events, 0.0 us)
Async XLA Ops:
  0.6 63.2 %copy-start.5 = (s32[1,1,11]{2,1,0:T(1,128)S(1)}, s32[1,1,11]{2,1,0:T(1,128)}, u32[]{:S(2)}) copy-start(s32[1,1,11]{2,1,0:T(1,128)} %param.14) | copy-start | bytes 136
  0.6 63.2 %copy-start.4 = (s32[1,1,11]{2,1,0:T(1,128)S(1)}, s32[1,1,11]{2,1,0:T(1,128)}, u32[]{:S(2)}) copy-start(s32[1,1,11]{2,1,0:T(1,128)} %param.13) | copy-start | bytes 136
  0.7 63.2 %copy-start = (bf16[1,1,11,256,256]{4,3,2,1,0:T(8,128)(2,1)S(1)}, bf16[1,1,11,256,256]{4,3,2,1,0:T(8,128)(2,1)}, u32[]{:S(2)}) copy-start(bf16[1,1,11,256,256]{4,3,2,1,0:T(8,128)(2,1)} %param.12) | copy-start | bytes 4325380
  0.7 12.7 %collective-permute-start = (bf16[128,512]{1,0:T(8,128)(2,1)}, bf16[128,512]{1,0:T(8,128)(2,1)S(1)}, u32[]{:S(2)}, u32[]{:S(2)}) collective-permute-start(bf16[128,512]{1,0:T(8,128)(2,1)} %param.8), channel_id=1, source_target_pairs={{0,128},{128,256},{256,384},{384,0},{1,129},{129,257},{257,385},{3... | collective-permute-start | bytes 393224 | tf_op jit(solution)/shard_map/ppermute | solution.py:142
  5.6 7.8 %collective-permute-start.2 = (bf16[128,512]{1,0:T(8,128)(2,1)}, bf16[128,512]{1,0:T(8,128)(2,1)S(1)}, u32[]{:S(2)}, u32[]{:S(2)}) collective-permute-start(bf16[128,512]{1,0:T(8,128)(2,1)} %param.8), channel_id=1, source_target_pairs={{0,384},{128,0},{256,128},{384,256},{1,385},{129,1},{257,129},{385... | collective-permute-start | bytes 393224 | tf_op jit(solution)/shard_map/ppermute | solution.py:142
  11.2 9.8 %collective-permute-start.1 = (bf16[128,512]{1,0:T(8,128)(2,1)}, bf16[128,512]{1,0:T(8,128)(2,1)S(1)}, u32[]{:S(2)}, u32[]{:S(2)}) collective-permute-start(bf16[128,512]{1,0:T(8,128)(2,1)} %param.8), channel_id=1, source_target_pairs={{0,256},{128,384},{256,0},{384,128},{1,257},{129,385},{257,1},{385... | collective-permute-start | bytes 393224 | tf_op jit(solution)/shard_map/ppermute | solution.py:142
  22.0 15.1 %collective-permute-start.4 = (bf16[4,128,512]{2,1,0:T(8,128)(2,1)S(1)}, bf16[4,128,512]{2,1,0:T(8,128)(2,1)S(1)}, u32[]{:S(2)}, u32[]{:S(2)}) collective-permute-start(bf16[4,128,512]{2,1,0:T(8,128)(2,1)S(1)} %pad_maximum_fusion.refs_0_), channel_id=1, source_target_pairs={{0,96},{32,0},{64,32},{96,64},{1,97},{33,1},{65,33},{97,65},{2,98}... | collective-permute-start | bytes 1572872 | tf_op jit(solution)/shard_map/ppermute | solution.py:142
  26.9 19.7 %collective-permute-start.3 = (bf16[4,128,512]{2,1,0:T(8,128)(2,1)S(1)}, bf16[4,128,512]{2,1,0:T(8,128)(2,1)S(1)}, u32[]{:S(2)}, u32[]{:S(2)}) collective-permute-start(bf16[4,128,512]{2,1,0:T(8,128)(2,1)S(1)} %pad_maximum_fusion.refs_0_), channel_id=1, source_target_pairs={{0,32},{32,64},{64,96},{96,0},{1,33},{33,65},{65,97},{97,1},{2,34}... | collective-permute-start | bytes 1572872 | tf_op jit(solution)/shard_map/ppermute | solution.py:142
  28.8 34.3 %collective-permute-start.7 = (bf16[4,128,512]{2,1,0:T(8,128)(2,1)S(1)}, bf16[4,128,512]{2,1,0:T(8,128)(2,1)S(1)}, u32[]{:S(2)}, u32[]{:S(2)}) collective-permute-start(bf16[4,128,512]{2,1,0:T(8,128)(2,1)S(1)} %pad_maximum_fusion.refs_0_), channel_id=1, source_target_pairs={{0,16},{16,0},{1,17},{17,1},{2,18},{18,2},{3,19},{19,3},{4,20},{20... | collective-permute-start | bytes 1572872 | tf_op jit(solution)/shard_map/ppermute | solution.py:142
  37.2 13.3 %collective-permute-start.6 = (bf16[2,128,512]{2,1,0:T(8,128)(2,1)S(1)}, bf16[2,128,512]{2,1,0:T(8,128)(2,1)}, u32[]{:S(2)}, u32[]{:S(2)}) collective-permute-start(bf16[2,128,512]{2,1,0:T(8,128)(2,1)S(1)} %slice.21), channel_id=1, source_target_pairs={{0,96},{32,0},{64,32},{96,64},{1,97},{33,1},{65,33},{97,65},{2,98}... | collective-permute-start | bytes 786440 | tf_op jit(solution)/shard_map/ppermute | solution.py:142
  42.5 20.6 %collective-permute-start.9 = (bf16[4,128,512]{2,1,0:T(8,128)(2,1)S(1)}, bf16[4,128,512]{2,1,0:T(8,128)(2,1)}, u32[]{:S(2)}, u32[]{:S(2)}) collective-permute-start(bf16[4,128,512]{2,1,0:T(8,128)(2,1)S(1)} %collective-permute-done.4.refs_2_), channel_id=1, source_target_pairs={{0,16},{16,0},{1,17},{17,1},{2,18},{18,2},{3,19},{19,3},{4,20},{20... | collective-permute-start | bytes 1572872 | tf_op jit(solution)/shard_map/ppermute | solution.py:142
  46.6 16.5 %collective-permute-start.8 = (bf16[4,128,512]{2,1,0:T(8,128)(2,1)S(1)}, bf16[4,128,512]{2,1,0:T(8,128)(2,1)}, u32[]{:S(2)}, u32[]{:S(2)}) collective-permute-start(bf16[4,128,512]{2,1,0:T(8,128)(2,1)S(1)} %collective-permute-done.3.refs_1_), channel_id=1, source_target_pairs={{0,16},{16,0},{1,17},{17,1},{2,18},{18,2},{3,19},{19,3},{4,20},{20... | collective-permute-start | bytes 1572872 | tf_op jit(solution)/shard_map/ppermute | solution.py:142
  48.5 10.6 %collective-permute-start.5 = (bf16[2,128,512]{2,1,0:T(8,128)(2,1)S(1)}, bf16[2,128,512]{2,1,0:T(8,128)(2,1)}, u32[]{:S(2)}, u32[]{:S(2)}) collective-permute-start(bf16[2,128,512]{2,1,0:T(8,128)(2,1)S(1)} %slice.20), channel_id=1, source_target_pairs={{0,32},{32,64},{64,96},{96,0},{1,33},{33,65},{65,97},{97,1},{2,34}... | collective-permute-start | bytes 786440 | tf_op jit(solution)/shard_map/ppermute | solution.py:142
  50.4 12.6 %collective-permute-start.11 = (bf16[2,128,512]{2,1,0:T(8,128)(2,1)}, bf16[2,128,512]{2,1,0:T(8,128)(2,1)}, u32[]{:S(2)}, u32[]{:S(2)}) collective-permute-start(bf16[2,128,512]{2,1,0:T(8,128)(2,1)} %collective-permute-done.6.refs_4_), channel_id=1, source_target_pairs={{0,16},{16,0},{1,17},{17,1},{2,18},{18,2},{3,19},{19,3},{4,20},{20... | collective-permute-start | bytes 786440 | tf_op jit(solution)/shard_map/ppermute | solution.py:142
  59.1 4.7 %collective-permute-start.10 = (bf16[2,128,512]{2,1,0:T(8,128)(2,1)}, bf16[2,128,512]{2,1,0:T(8,128)(2,1)}, u32[]{:S(2)}, u32[]{:S(2)}) collective-permute-start(bf16[2,128,512]{2,1,0:T(8,128)(2,1)} %collective-permute-done.5.refs_3_), channel_id=1, source_target_pairs={{0,16},{16,0},{1,17},{17,1},{2,18},{18,2},{3,19},{19,3},{4,20},{20... | collective-permute-start | bytes 786440 | tf_op jit(solution)/shard_map/ppermute | solution.py:142
  66.7 11.2 %collective-permute-start.12 = (bf16[8,128,256]{2,1,0:T(8,128)(2,1)S(1)}, bf16[8,128,256]{2,1,0:T(8,128)(2,1)S(1)}, u32[]{:S(2)}, u32[]{:S(2)}) collective-permute-start(bf16[8,128,256]{2,1,0:T(8,128)(2,1)S(1)} %get-tuple-element.9), channel_id=1, source_target_pairs={{0,1},{1,0},{2,3},{3,2},{4,5},{5,4},{6,7},{7,6},{8,9},{9,8},{10,11... | collective-permute-start | bytes 1572872 | tf_op jit(solution)/shard_map/ppermute | solution.py:189
  69.6 14.8 %collective-permute-start.13 = (bf16[8,128,256]{2,1,0:T(8,128)(2,1)S(1)}, bf16[8,128,256]{2,1,0:T(8,128)(2,1)S(1)}, u32[]{:S(2)}, u32[]{:S(2)}) collective-permute-start(bf16[8,128,256]{2,1,0:T(8,128)(2,1)S(1)} %get-tuple-element.10), channel_id=1, source_target_pairs={{0,7},{1,2},{2,1},{3,4},{4,3},{5,6},{6,5},{7,0},{8,15},{9,10},{10,... | collective-permute-start | bytes 1572872 | tf_op jit(solution)/shard_map/ppermute | solution.py:190
  84.6 41.5 %copy-start.1 = (bf16[512,512]{1,0:T(8,128)(2,1)S(1)}, bf16[512,512]{1,0:T(8,128)(2,1)}, u32[]{:S(2)}) copy-start(bf16[512,512]{1,0:T(8,128)(2,1)} %weight_ref.1) | copy-start | bytes 1572868
  84.6 41.4 %copy-start.2 = (bf16[128,512]{1,0:T(8,128)(2,1)S(1)}, bf16[128,512]{1,0:T(8,128)(2,1)}, u32[]{:S(2)}) copy-start(bf16[128,512]{1,0:T(8,128)(2,1)} %cot_ref.1) | copy-start | bytes 393220
  84.7 41.4 %copy-start.3 = (f32[512]{0:T(512)S(1)}, f32[512]{0:T(512)}, u32[]{:S(2)}) copy-start(f32[512]{0:T(512)} %param.10) | copy-start | bytes 6148

commit v3 on v1

v3 whole, which is shorter than its diff:
```python
import jax
import jax.numpy as jnp
from jax import lax
from jax.experimental import pallas as pl
from jax.experimental.pallas import tpu as pltpu
from jax.sharding import Mesh, PartitionSpec as P

F32 = jnp.float32
BF16 = jnp.bfloat16
LANES = 128
VMEM = pl.BlockSpec(memory_space=pltpu.VMEM)
SMEM = pl.BlockSpec(memory_space=pltpu.SMEM)
ANY = pl.BlockSpec(memory_space=pl.ANY)
PARAMS = pltpu.CompilerParams(vmem_limit_bytes=40 * 1024 * 1024)
AXES = ("z_lo", "x", "core", "z_hi", "y_pair", "y_odd")
ROW = ("z_lo", "x", "core")
COL = ("z_hi", "y_pair", "y_odd")
QUAD = ("core", "y_odd")
REST = ("z_hi", "y_pair")
PLANE = ("x", "core", "y_pair", "y_odd")
DEPTH = ("z_lo", "z_hi")
SIZES = (4, 4, 2, 2, 4, 2)
SIDE = 16


def quarter_kernel(features_ref, side_ref, out_ref):
    nodes = features_ref.shape[0]
    for part in range(out_ref.shape[0]):
        out_ref[part, :nodes, :] = features_ref[:, part * LANES : (part + 1) * LANES]
        out_ref[part, nodes:, :] = side_ref[...]


def tile_kernel(place_ref, meta_ref, *refs):
    given, block_ref, out_ref, tiles, total, sems = refs[:4], refs[4], refs[5], refs[6], refs[7], refs[8]
    _, slots, size, _ = tiles.shape
    n_x = block_ref.shape[0]
    core, odd = place_ref[0], place_ref[1]

    def tile_copy(which, slot):
        return pltpu.make_async_copy(
            given[which].at[slot], tiles.at[which, slot], sems.at[which, slot]
        )

    def cell_of(which):
        cell_core, cell_odd = (core + which // 2) % 2, (odd + which % 2) % 2
        return cell_core, cell_odd, cell_core * 2 + cell_odd

    for which in range(4):

        def fetch(slot, carry):
            tile_copy(which, slot).start()
            return carry

        lax.fori_loop(0, meta_ref[cell_of(which)[2], 2, 0], fetch, 0)
    total[...] = jnp.zeros_like(total)
    for which in range(4):
        cell_core, cell_odd, cell = cell_of(which)

        def step(slot, carry):
            tile_copy(which, slot).wait()
            chip = meta_ref[cell, 1, slot]
            z, x = chip // n_x, lax.rem(chip, n_x)
            window = jnp.concatenate(
                [block_ref[x, z, cell_odd], block_ref[x, z, 2 + cell_odd]], axis=0
            )
            total[cell_core, meta_ref[cell, 0, slot]] += jnp.dot(
                tiles[which, slot], window, preferred_element_type=F32
            )
            return carry

        lax.fori_loop(0, meta_ref[cell, 2, 0], step, 0)
    for row in range(total.shape[1]):
        for cell_core in range(2):
            out_ref[row, cell_core] = total[cell_core, row].astype(BF16)


def add_kernel(parts_ref, out_ref):
    total = parts_ref[0].astype(F32)
    for part in range(1, parts_ref.shape[0]):
        total = total + parts_ref[part].astype(F32)
    out_ref[...] = total.astype(BF16)


def split_column(column):
    high = column.astype(BF16)
    low = (column - high.astype(F32)).astype(BF16)
    lane = lax.broadcasted_iota(jnp.int32, column.shape, 1)
    return jnp.where(lane == 0, high.astype(F32), jnp.where(lane == 1, low.astype(F32), 0.0)).astype(BF16)


def node_kernel(shares_ref, weight_ref, bias_ref, cot_ref, act_ref, grads_ref):
    width = weight_ref.shape[1]
    aggregated = jnp.concatenate([shares_ref[part] for part in range(shares_ref.shape[0])], axis=1)
    preact = jnp.dot(aggregated, weight_ref[...], preferred_element_type=F32) + bias_ref[...]
    sigmoid_part = jax.nn.sigmoid(preact)
    act_ref[...] = (preact * sigmoid_part).astype(BF16)
    grad = cot_ref[...].astype(F32) * sigmoid_part * (1.0 + preact * (1.0 - sigmoid_part))
    rounded = grad.astype(BF16)
    rest = (grad - rounded.astype(F32)).astype(BF16)
    over_nodes = (((0,), (0,)), ((), ()))
    grads_ref[:, :width] = lax.dot_general(
        aggregated, rounded, over_nodes, preferred_element_type=F32
    ).astype(BF16)
    ones = jnp.ones((grad.shape[0], LANES), BF16)
    column = lax.dot_general(rounded, ones, over_nodes, preferred_element_type=F32)
    column = column + lax.dot_general(rest, ones, over_nodes, preferred_element_type=F32)
    grads_ref[:, width:] = split_column(column)


def sum_kernel(parts_ref, out_ref):
    width = parts_ref.shape[2] - LANES
    total = parts_ref[0].astype(F32)
    for part in range(1, parts_ref.shape[0]):
        total = total + parts_ref[part].astype(F32)
    main = total[:, :width].astype(BF16)
    column = total[:, width : width + 1] + total[:, width + 1 : width + 2]
    side = split_column(jnp.broadcast_to(column, (column.shape[0], LANES)))
    for copy in range(out_ref.shape[0]):
        out_ref[copy, :, :width] = main
        out_ref[copy, :, width:] = side


def sum_parts(parts, copies):
    return pl.pallas_call(
        sum_kernel,
        out_shape=jax.ShapeDtypeStruct((copies,) + parts.shape[1:], BF16),
        in_specs=[VMEM],
        out_specs=VMEM,
        compiler_params=PARAMS,
    )(parts)


def last_kernel(parts_ref, weight_ref, bias_ref):
    width = weight_ref.shape[1]
    weight_ref[...] = parts_ref[:, :width].astype(F32)
    side = jnp.transpose(parts_ref[:, width:].astype(F32))
    bias_ref[...] = side[0:1] + side[1:2]


def call(kernel, out, *args):
    shapes = jax.tree.map(lambda o: jax.ShapeDtypeStruct(*o), out, is_leaf=lambda o: isinstance(o[0], tuple) and not isinstance(o[1], tuple))
    specs = jax.tree.map(lambda o: VMEM, shapes)
    return pl.pallas_call(
        kernel, out_shape=shapes, in_specs=[VMEM] * len(args), out_specs=specs, compiler_params=PARAMS
    )(*args)


def swap(array, axis):
    return lax.ppermute(array, axis, [(0, 1), (1, 0)])


def per_device(
    features, weight, bias_term, cotangent, tile_values, tile_rows, tile_cols, tile_count
):
    nodes, width = features.shape
    _, _, slots, size, _ = tile_values.shape
    n_z, n_x = lax.axis_size("z_lo"), lax.axis_size("x")
    n_rest = lax.axis_size(REST)
    tiles = tile_values[0, 0]
    tiles_y = swap(tiles, "y_odd")
    tiles_core = swap(tiles, "core")
    tiles_both = swap(tiles_y, "core")
    ints = [tile_rows[0, 0], tile_cols[0, 0], jnp.broadcast_to(tile_count[0], (slots,))]
    side = jnp.pad(jnp.stack(ints), ((0, SIDE - 3), (0, LANES - slots))).astype(BF16)
    quarters = call(quarter_kernel, ((4, nodes + SIDE, LANES), BF16), features, side)
    quarters = lax.all_to_all(quarters, QUAD, 0, 0)
    meta = quarters[:, nodes : nodes + 3, :slots].astype(jnp.int32)
    near = lax.all_gather(quarters[:, :nodes], "z_lo", axis=0)
    blocks = lax.all_to_all(jnp.broadcast_to(near[None], (n_x,) + near.shape), "x", 0, 0)
    place = jnp.stack([lax.axis_index(axis) for axis in QUAD]).astype(jnp.int32)
    term = pl.pallas_call(
        tile_kernel,
        out_shape=jax.ShapeDtypeStruct((n_rest, 2, size, LANES), BF16),
        in_specs=[SMEM, SMEM] + [ANY] * 4 + [VMEM],
        out_specs=VMEM,
        scratch_shapes=[
            pltpu.VMEM((4, slots, size, size), BF16),
            pltpu.VMEM((2, n_rest, size, LANES), F32),
            pltpu.SemaphoreType.DMA((4, slots)),
        ],
        compiler_params=PARAMS,
    )(place, meta, tiles, tiles_y, tiles_core, tiles_both, blocks)
    shares = lax.all_to_all(term, REST, 0, 0)
    shares = call(add_kernel, ((2, size, LANES), BF16), shares)
    shares = lax.all_to_all(shares.reshape(4, nodes, LANES), QUAD, 0, 0)
    activations, grads = call(
        node_kernel,
        (((nodes, width), BF16), ((width, width + LANES), BF16)),
        shares,
        weight,
        bias_term[None, :],
        cotangent,
    )
    n_plane, n_depth = lax.axis_size(PLANE), lax.axis_size(DEPTH)
    grads = lax.all_to_all(grads.reshape(n_plane, width // n_plane, width + LANES), PLANE, 0, 0)
    grads = lax.all_to_all(sum_parts(grads, n_depth), DEPTH, 0, 0)
    grads = lax.all_to_all(sum_parts(grads, n_plane), PLANE, 0, 0)
    weight_grad, bias_grad = call(
        last_kernel,
        (((width, width), F32), ((1, width), F32)),
        grads.reshape(width, width + LANES),
    )
    return activations, weight_grad, bias_grad[0]


def solution(mesh):
    cut = Mesh(mesh.devices.reshape(SIZES), AXES)
    everywhere = P(AXES, None)
    return jax.shard_map(
        per_device,
        mesh=cut,
        in_specs=(
            everywhere,
            P(),
            P(),
            everywhere,
            P(ROW, COL, None, None, None),
            P(ROW, COL, None),
            P(ROW, COL, None),
            P(ROW, COL),
        ),
        out_specs=(everywhere, P(), P()),
        check_vma=False,
    )
```

time: 231 us -> 209 us (0.905)
  waiting for transfers between devices: 74.2 us -> 16.9 us
  blocking collectives: 132 us -> 165 us
  starting transfers between devices: 0.04 us -> 14.4 us
  between operations: 14.7 us -> 1.38 us
  Pallas kernels: 2.68 us -> 6.12 us
  local copies, waits for them, and re-layouts: 5.99 us -> 3.58 us
    all_gather x1 -> x0, waiting for transfers between devices: 73.5 us -> none  [per_device(): gathered = lax.all_gather(features, 'row', axis=0, tiled=True)]
    all_gather x0 -> x1, blocking collectives: none -> 16.9 us  [per_device(): near = lax.all_gather(quarters[:, :nodes], 'z_lo', axis=0)]
    all_to_all x0 -> x1, waiting for transfers between devices: none -> 16.7 us  [per_device(): lax.all_to_all(jnp.broadcast_to(near[None], (n_x,) + near.shape), 'x', 0, 0)]
    all_to_all x4 -> x6, blocking collectives: 132 us -> 148 us  [the longest x1 37 us: per_device(): shares = lax.all_to_all(term, REST, 0, 0)]
    ppermute x0 -> x3, starting transfers between devices: none -> 10.3 us  [swap(): return lax.ppermute(array, axis, [(0, 1), (1, 0)])]
    all_to_all x0 -> x1, starting transfers between devices: none -> 4.14 us  [per_device(): lax.all_to_all(jnp.broadcast_to(near[None], (n_x,) + near.shape), 'x', 0, 0)]
    pallas_call x2 -> x5, Pallas kernels: 2.32 us -> 5.74 us  [the longest x1 3.56 us: per_device(): pl.pallas_call(tile_kernel, out_shape=jax.ShapeDtypeStruct((n_rest, 2, si...]
    unnamed x14 -> x12, local copies, waits for them, and re-layouts: 4.88 us -> 1.59 us
  transfers between devices with their start and end apart: 1 -> 4, of which waited for: 1 -> 2; matrix products, arithmetic and copies ran while one was open for 0% -> 2% of each run, Pallas kernels for 0% -> 0%
where the time goes in v3:
time: 209 us
  blocking collectives  165 us (79%)
  waiting for transfers between devices  16.9 us (8%)
  starting transfers between devices  14.4 us (7%)
  Pallas kernels  6.12 us (3%)
  local copies, waits for them, and re-layouts  3.58 us (2%)
    all_to_all x1, blocking collectives, per_device(): shares = lax.all_to_all(term, REST, 0, 0)  37 us
    all_to_all x1, blocking collectives, per_device(): quarters = lax.all_to_all(quarters, QUAD, 0, 0)  31.4 us
    all_to_all x1, blocking collectives, per_device(): grads = lax.all_to_all(sum_parts(grads, n_plane), PLANE, 0, 0)  27.5 us
    all_to_all x1, blocking collectives, per_device(): lax.all_to_all(grads.reshape(n_plane, width // n_plane, width + LANES), P...  24.5 us
    all_to_all x1, blocking collectives, per_device(): shares = lax.all_to_all(shares.reshape(4, nodes, LANES), QUAD, 0, 0)  18.6 us
    all_gather x1, blocking collectives, per_device(): near = lax.all_gather(quarters[:, :nodes], 'z_lo', axis=0)  16.9 us
    all_to_all x1, waiting for transfers between devices, per_device(): lax.all_to_all(jnp.broadcast_to(near[None], (n_x,) + near.shape), 'x', 0, 0)  16.7 us
    ppermute x3, starting transfers between devices, swap(): return lax.ppermute(array, axis, [(0, 1), (1, 0)])  10.3 us
  transfers between devices with their start and end apart: 4, of which 2 were waited for; matrix products, arithmetic and copies ran while one was open for 2% of the time, Pallas kernels for 0%

profile of v3, /device:TPU:1, one launch (start us, length us, event | category | flops | bytes accessed | tf_op | source)
XLA Modules:
  0.0 208.9 jit_solution(1004998403098698245)
XLA Ops:
  0.6 4.0 %collective-permute-start = (bf16[11,256,256]{2,1,0:T(8,128)(2,1)}, bf16[11,256,256]{2,1,0:T(8,128)(2,1)}, u32[]{:S(2)}, u32[]{:S(2)}) collective-permute-start(bf16[11,256,256]{2,1,0:T(8,128)(2,1)} %bitcast.17), channel_id=1, source_target_pairs={{0,1},{1,0},{2,3},{3,2},{4,5},{5,4},{6,7},{7,6},{8,9},{9,8},{10,11... | collective-permute-start | bytes 4325384 | tf_op jit(solution)/shard_map/ppermute | solution.py:149
  5.3 0.1 pad.8.clone
  5.4 0.7 convert_bitcast_fusion
  6.1 0.1 maximum_maximum_fusion
  6.2 0.0 copy-start.2
  6.2 0.9 copy-done.2
  7.1 31.4 %all_to_all.35 = bf16[4,144,128]{2,1,0:T(8,128)(2,1)S(1)} all-to-all(bf16[4,144,128]{2,1,0:T(8,128)(2,1)S(1)} %shard_map.103), channel_id=1, replica_groups=mesh['z_lo'=4,'x'=4,'core'=2,'z_hi'=2,'y_pair'=4,'y_odd'=2] {'core','y_o..., dimensions={0} | all-to-all | bytes 294912 | tf_op jit(solution)/shard_map/all_to_all | solution.py:166
  38.5 0.0 copy-start.5
  38.5 0.7 copy-done.5
  39.2 16.9 %all-gather = bf16[16,128,128]{2,1,0:T(8,128)(2,1)S(1)} all-gather(bf16[4,128,128]{2,1,0:T(8,128)(2,1)S(1)} %slice.9), channel_id=2, replica_groups=mesh['z_lo'=4,'x'=4,'core'=2,'z_hi'=2,'y_pair'=4,'y_odd'=2] {'z_lo'}, dimensions={0}, use_global_device_ids=true | all-gather | bytes 655360 | tf_op jit(solution)/shard_map/all_gather | solution.py:168
  56.1 1.9 broadcast_in_dim.4
  58.0 0.0 copy-start
  58.0 4.1 %all-to-all-start.1 = ((bf16[4,4,4,128,128]{4,3,2,1,0:T(8,128)(2,1)}), bf16[4,4,4,128,128]{4,3,2,1,0:T(8,128)(2,1)S(1)}, u32[]{:S(2)}, u32[]{:S(2)}) async-start(bf16[4,4,4,128,128]{4,3,2,1,0:T(8,128)(2,1)} %broadcast_in_dim.4), calls=%async_computation.1 | async-start | bytes 4194304 | tf_op jit(solution)/shard_map/all_to_all | solution.py:169
  62.1 0.0 copy-done
  62.1 4.3 %collective-permute-start.1 = (bf16[11,256,256]{2,1,0:T(8,128)(2,1)S(1)}, bf16[11,256,256]{2,1,0:T(8,128)(2,1)}, u32[]{:S(2)}, u32[]{:S(2)}) collective-permute-start(bf16[11,256,256]{2,1,0:T(8,128)(2,1)S(1)} %bitcast.18), channel_id=1, source_target_pairs={{0,16},{16,0},{1,17},{17,1},{2,18},{18,2},{3,19},{19,3},{4,20},{20... | collective-permute-start | bytes 4325384 | tf_op jit(solution)/shard_map/ppermute | solution.py:149
  66.5 0.0 collective-permute-done.refs_1_
  66.5 1.9 collective-permute-start.2
  68.4 0.1 pad_add_fusion.place_ref
  68.5 0.7 slice_convert_fusion.meta_ref
  69.2 0.2 collective-permute-done.1.refs_2_
  69.4 16.7 %all-to-all-done.1.refs_4_ = bf16[4,4,4,128,128]{4,3,2,1,0:T(8,128)(2,1)S(1)} async-done(((bf16[4,4,4,128,128]{4,3,2,1,0:T(8,128)(2,1)}), bf16[4,4,4,128,128]{4,3,2,1,0:T(8,128)(2,1)S(1)}, u32[]{:S(2)}, u32[]{:S(2)}) %all-to-all-start.1) | async-done | bytes 2097184 | tf_op jit(solution)/shard_map/all_to_all | solution.py:169
  86.1 0.0 collective-permute-done.2.refs_3_
  86.1 3.6 %shard_map.104 = bf16[8,2,256,128]{3,2,1,0:T(8,128)(2,1)S(1)} custom-call(s32[2]{0:T(128)S(1)} %pad_add_fusion.place_ref, s32[4,3,11]{2,1,0:T(4,128)S(1)} %slice_convert_fusion.meta_ref, bf16[11,256,256]{2,1,0:T(8,128)(2,1)S(1)} %bitcast.19, bf16[11,256,256]{2,1,0:T(8,128)(2,1)} %collective-permute-done.refs_1_, ...), custom_call_target="tpu_custom_call" | custom-call | tf_op jit(solution)/shard_map/pallas_call | solution.py:171
  89.6 0.0 copy-start.1
  89.7 0.0 copy-start.3
  89.7 0.0 copy-start.4
  89.7 37.0 %all_to_all.36.parts_ref = bf16[8,2,256,128]{3,2,1,0:T(8,128)(2,1)S(1)} all-to-all(bf16[8,2,256,128]{3,2,1,0:T(8,128)(2,1)S(1)} %shard_map.104), channel_id=1, replica_groups=mesh['z_lo'=4,'x'=4,'core'=2,'z_hi'=2,'y_pair'=4,'y_odd'=2] {'z_hi','y_p..., dimensions={0} | all-to-all | bytes 2097152 | tf_op jit(solution)/shard_map/all_to_all | solution.py:183
  126.6 0.1 shard_map.105
  126.8 18.6 %all_to_all.37.shares_ref = bf16[4,128,128]{2,1,0:T(8,128)(2,1)S(1)} all-to-all(bf16[4,128,128]{2,1,0:T(8,128)(2,1)S(1)} %bitcast.21), channel_id=1, replica_groups=mesh['z_lo'=4,'x'=4,'core'=2,'z_hi'=2,'y_pair'=4,'y_odd'=2] {'core','y_o..., dimensions={0} | all-to-all | bytes 262144 | tf_op jit(solution)/shard_map/all_to_all | solution.py:185
  145.4 0.0 copy-done.1
  145.4 0.0 copy-done.3
  145.4 0.0 copy-done.4
  145.4 1.0 shard_map.106
  146.4 24.5 %all_to_all.38.parts_ref = bf16[64,8,640]{2,1,0:T(8,128)(2,1)S(1)} all-to-all(bf16[64,8,640]{2,1,0:T(8,128)(2,1)S(1)} %bitcast.20), channel_id=1, replica_groups=mesh['z_lo'=4,'x'=4,'core'=2,'z_hi'=2,'y_pair'=4,'y_odd'=2] {'x','core',..., dimensions={0} | all-to-all | bytes 1310720 | tf_op jit(solution)/shard_map/all_to_all | solution.py:195
  170.9 0.2 shard_map.107
  171.1 9.0 %all_to_all.39.parts_ref = bf16[8,8,640]{2,1,0:T(8,128)(2,1)S(1)} all-to-all(bf16[8,8,640]{2,1,0:T(8,128)(2,1)S(1)} %shard_map.107), channel_id=1, replica_groups=mesh['z_lo'=4,'x'=4,'core'=2,'z_hi'=2,'y_pair'=4,'y_odd'=2] {'z_lo','z_hi'}, dimensions={0} | all-to-all | bytes 163840 | tf_op jit(solution)/shard_map/all_to_all | solution.py:196
  180.1 0.2 shard_map.108
  180.3 27.5 %all_to_all.40 = bf16[64,8,640]{2,1,0:T(8,128)(2,1)S(1)} all-to-all(bf16[64,8,640]{2,1,0:T(8,128)(2,1)S(1)} %shard_map.108), channel_id=1, replica_groups=mesh['z_lo'=4,'x'=4,'core'=2,'z_hi'=2,'y_pair'=4,'y_odd'=2] {'x','core',..., dimensions={0} | all-to-all | bytes 1310720 | tf_op jit(solution)/shard_map/all_to_all | solution.py:197
  207.8 1.1 shard_map.109
  (3 shorter events, 0.0 us)
Async XLA Ops:
  0.6 65.8 %collective-permute-start = (bf16[11,256,256]{2,1,0:T(8,128)(2,1)}, bf16[11,256,256]{2,1,0:T(8,128)(2,1)}, u32[]{:S(2)}, u32[]{:S(2)}) collective-permute-start(bf16[11,256,256]{2,1,0:T(8,128)(2,1)} %bitcast.17), channel_id=1, source_target_pairs={{0,1},{1,0},{2,3},{3,2},{4,5},{5,4},{6,7},{7,6},{8,9},{9,8},{10,11... | collective-permute-start | bytes 4325384 | tf_op jit(solution)/shard_map/ppermute | solution.py:149
  6.2 0.9 copy-start.2
  38.5 0.7 copy-start.5
  58.0 4.1 %copy-start = (bf16[1,1,11,256,256]{4,3,2,1,0:T(8,128)(2,1)S(1)}, bf16[1,1,11,256,256]{4,3,2,1,0:T(8,128)(2,1)}, u32[]{:S(2)}) copy-start(bf16[1,1,11,256,256]{4,3,2,1,0:T(8,128)(2,1)} %param.12) | copy-start | bytes 4325380
  58.0 28.1 %all-to-all-start.1 = ((bf16[4,4,4,128,128]{4,3,2,1,0:T(8,128)(2,1)}), bf16[4,4,4,128,128]{4,3,2,1,0:T(8,128)(2,1)S(1)}, u32[]{:S(2)}, u32[]{:S(2)}) async-start(bf16[4,4,4,128,128]{4,3,2,1,0:T(8,128)(2,1)} %broadcast_in_dim.4), calls=%async_computation.1 | async-start | bytes 4194304 | tf_op jit(solution)/shard_map/all_to_all | solution.py:169
  62.1 7.3 %collective-permute-start.1 = (bf16[11,256,256]{2,1,0:T(8,128)(2,1)S(1)}, bf16[11,256,256]{2,1,0:T(8,128)(2,1)}, u32[]{:S(2)}, u32[]{:S(2)}) collective-permute-start(bf16[11,256,256]{2,1,0:T(8,128)(2,1)S(1)} %bitcast.18), channel_id=1, source_target_pairs={{0,16},{16,0},{1,17},{17,1},{2,18},{18,2},{3,19},{19,3},{4,20},{20... | collective-permute-start | bytes 4325384 | tf_op jit(solution)/shard_map/ppermute | solution.py:149
  66.5 19.6 %collective-permute-start.2 = (bf16[11,256,256]{2,1,0:T(8,128)(2,1)}, bf16[11,256,256]{2,1,0:T(8,128)(2,1)}, u32[]{:S(2)}, u32[]{:S(2)}) collective-permute-start(bf16[11,256,256]{2,1,0:T(8,128)(2,1)} %collective-permute-done.refs_1_), channel_id=1, source_target_pairs={{0,16},{16,0},{1,17},{17,1},{2,18},{18,2},{3,19},{19,3},{4,20},{20... | collective-permute-start | bytes 4325384 | tf_op jit(solution)/shard_map/ppermute | solution.py:149
  89.6 55.8 %copy-start.1 = (bf16[512,512]{1,0:T(8,128)(2,1)S(1)}, bf16[512,512]{1,0:T(8,128)(2,1)}, u32[]{:S(2)}) copy-start(bf16[512,512]{1,0:T(8,128)(2,1)} %weight_ref.1) | copy-start | bytes 1572868
  89.7 55.8 %copy-start.3 = (bf16[128,512]{1,0:T(8,128)(2,1)S(1)}, bf16[128,512]{1,0:T(8,128)(2,1)}, u32[]{:S(2)}) copy-start(bf16[128,512]{1,0:T(8,128)(2,1)} %cot_ref.1) | copy-start | bytes 393220
  89.7 55.7 %copy-start.4 = (f32[512]{0:T(512)S(1)}, f32[512]{0:T(512)}, u32[]{:S(2)}) copy-start(f32[512]{0:T(512)} %param.10) | copy-start | bytes 6148

commit v4 on v3

--- a/solution.py
+++ b/solution.py
@@ -17,7 +17,7 @@
 COL = ("z_hi", "y_pair", "y_odd")
 QUAD = ("core", "y_odd")
 REST = ("z_hi", "y_pair")
-PLANE = ("x", "core", "y_pair", "y_odd")
+PLANE = ("x", "y_pair")
 DEPTH = ("z_lo", "z_hi")
 SIZES = (4, 4, 2, 2, 4, 2)
 SIDE = 16
@@ -157,13 +157,14 @@
     n_z, n_x = lax.axis_size("z_lo"), lax.axis_size("x")
     n_rest = lax.axis_size(REST)
     tiles = tile_values[0, 0]
-    tiles_y = swap(tiles, "y_odd")
-    tiles_core = swap(tiles, "core")
-    tiles_both = swap(tiles_y, "core")
     ints = [tile_rows[0, 0], tile_cols[0, 0], jnp.broadcast_to(tile_count[0], (slots,))]
     side = jnp.pad(jnp.stack(ints), ((0, SIDE - 3), (0, LANES - slots))).astype(BF16)
     quarters = call(quarter_kernel, ((4, nodes + SIDE, LANES), BF16), features, side)
     quarters = lax.all_to_all(quarters, QUAD, 0, 0)
+    quarters, tiles = lax.optimization_barrier((quarters, tiles))
+    tiles_y = swap(tiles, "y_odd")
+    tiles_core = swap(tiles, "core")
+    tiles_both = swap(tiles_y, "core")
     meta = quarters[:, nodes : nodes + 3, :slots].astype(jnp.int32)
     near = lax.all_gather(quarters[:, :nodes], "z_lo", axis=0)
     blocks = lax.all_to_all(jnp.broadcast_to(near[None], (n_x,) + near.shape), "x", 0, 0)
@@ -192,13 +193,17 @@
         cotangent,
     )
     n_plane, n_depth = lax.axis_size(PLANE), lax.axis_size(DEPTH)
-    grads = lax.all_to_all(grads.reshape(n_plane, width // n_plane, width + LANES), PLANE, 0, 0)
-    grads = lax.all_to_all(sum_parts(grads, n_depth), DEPTH, 0, 0)
-    grads = lax.all_to_all(sum_parts(grads, n_plane), PLANE, 0, 0)
+    wide = width + LANES
+    grads = sum_parts(lax.all_to_all(grads.reshape(4, width // 4, wide), QUAD, 0, 0), 1)
+    grads = grads.reshape(n_plane, width // 4 // n_plane, wide)
+    grads = sum_parts(lax.all_to_all(grads, PLANE, 0, 0), n_depth)
+    grads = sum_parts(lax.all_to_all(grads, DEPTH, 0, 0), n_plane)
+    grads = lax.all_to_all(grads, PLANE, 0, 0).reshape(1, width // 4, wide)
+    grads = lax.all_to_all(jnp.broadcast_to(grads, (4,) + grads.shape[1:]), QUAD, 0, 0)
     weight_grad, bias_grad = call(
         last_kernel,
         (((width, width), F32), ((1, width), F32)),
-        grads.reshape(width, width + LANES),
+        grads.reshape(width, wide),
     )
     return activations, weight_grad, bias_grad[0]
 

time: 209 us -> 184 us (0.88)
  blocking collectives: 165 us -> 143 us
  waiting for transfers between devices: 16.9 us -> 11.6 us
    all_to_all x1, blocking collectives: 31.4 us -> 13.6 us  [per_device(): quarters = lax.all_to_all(quarters, QUAD, 0, 0)]
    all_to_all x1, waiting for transfers between devices: 16.7 us -> 3 us  [per_device(): lax.all_to_all(jnp.broadcast_to(near[None], (n_x,) + near.shape), 'x', 0, 0)]
    all_to_all x1, blocking collectives: 18.6 us -> 8.08 us  [per_device(): shares = lax.all_to_all(shares.reshape(4, nodes, LANES), QUAD, 0, 0)]
    ppermute x3, waiting for transfers between devices: 0.24 us -> 8.61 us  [swap(): return lax.ppermute(array, axis, [(0, 1), (1, 0)])]
    all_to_all x1, blocking collectives: 37 us -> 44.7 us  [per_device(): shares = lax.all_to_all(term, REST, 0, 0)]
    all_gather x1, blocking collectives: 16.9 us -> 12.2 us  [per_device(): near = lax.all_gather(quarters[:, :nodes], 'z_lo', axis=0)]
    all_to_all x3 -> x5, blocking collectives: 61 us -> 64.4 us  [the longest x1 16 us: per_device(): lax.all_to_all(jnp.broadcast_to(grads, (4,) + grads.shape[1:]), QUAD, 0, 0)]
  transfers between devices with their start and end apart: 4 -> 4, of which waited for: 2 -> 2; matrix products, arithmetic and copies ran while one was open for 2% -> 1% of each run, Pallas kernels for 0% -> 0%
where the time goes in v4:
time: 184 us
  blocking collectives  143 us (78%)
  starting transfers between devices  15.3 us (8%)
  waiting for transfers between devices  11.6 us (6%)
  Pallas kernels  7.72 us (4%)
  local copies, waits for them, and re-layouts  2.97 us (2%)
    all_to_all x1, blocking collectives, per_device(): shares = lax.all_to_all(term, REST, 0, 0)  44.7 us
    all_to_all x1, blocking collectives, per_device(): lax.all_to_all(jnp.broadcast_to(grads, (4,) + grads.shape[1:]), QUAD, 0, 0)  16 us
    all_to_all x1, blocking collectives, per_device(): quarters = lax.all_to_all(quarters, QUAD, 0, 0)  13.6 us
    all_to_all x1, blocking collectives, per_device(): grads = sum_parts(lax.all_to_all(grads, PLANE, 0, 0), n_depth)  13.5 us
    all_to_all x1, blocking collectives, per_device(): grads = lax.all_to_all(grads, PLANE, 0, 0).reshape(1, width // 4, wide)  12.7 us
    all_to_all x1, blocking collectives, per_device(): lax.all_to_all(grads.reshape(4, width // 4, wide), QUAD, 0, 0)  12.6 us
    all_gather x1, blocking collectives, per_device(): near = lax.all_gather(quarters[:, :nodes], 'z_lo', axis=0)  12.2 us
    ppermute x3, starting transfers between devices, swap(): return lax.ppermute(array, axis, [(0, 1), (1, 0)])  11.6 us
  transfers between devices with their start and end apart: 4, of which 2 were waited for; matrix products, arithmetic and copies ran while one was open for 1% of the time, Pallas kernels for 0%

profile of v4, /device:TPU:1, one launch (start us, length us, event | category | flops | bytes accessed | tf_op | source)
XLA Modules:
  0.0 183.5 jit_solution(13713500241785130277)
XLA Ops:
  1.3 0.1 pad.8.clone
  1.4 0.7 convert_bitcast_fusion
  2.0 0.1 maximum_maximum_fusion
  2.1 0.0 copy-start.2
  2.1 0.9 copy-done.2
  3.0 13.6 %all_to_all.45 = bf16[4,144,128]{2,1,0:T(8,128)(2,1)S(1)} all-to-all(bf16[4,144,128]{2,1,0:T(8,128)(2,1)S(1)} %shard_map.103), channel_id=1, replica_groups=mesh['z_lo'=4,'x'=4,'core'=2,'z_hi'=2,'y_pair'=4,'y_odd'=2] {'core','y_o..., dimensions={0} | all-to-all | bytes 294912 | tf_op jit(solution)/shard_map/all_to_all | solution.py:163
  16.6 0.0 copy-start.5
  16.6 2.0 %collective-permute-start = (bf16[11,256,256]{2,1,0:T(8,128)(2,1)}, bf16[11,256,256]{2,1,0:T(8,128)(2,1)}, u32[]{:S(2)}, u32[]{:S(2)}) collective-permute-start(bf16[11,256,256]{2,1,0:T(8,128)(2,1)} %bitcast.19), channel_id=1, source_target_pairs={{0,1},{1,0},{2,3},{3,2},{4,5},{5,4},{6,7},{7,6},{8,9},{9,8},{10,11... | collective-permute-start | bytes 4325384 | tf_op jit(solution)/shard_map/ppermute | solution.py:149
  18.6 0.0 copy-done.5
  18.7 12.2 %all-gather = bf16[16,128,128]{2,1,0:T(8,128)(2,1)S(1)} all-gather(bf16[4,128,128]{2,1,0:T(8,128)(2,1)S(1)} %slice.7), channel_id=2, replica_groups=mesh['z_lo'=4,'x'=4,'core'=2,'z_hi'=2,'y_pair'=4,'y_odd'=2] {'z_lo'}, dimensions={0}, use_global_device_ids=true | all-gather | bytes 655360 | tf_op jit(solution)/shard_map/all_gather | solution.py:169
  30.9 1.9 %broadcast_in_dim.16 = bf16[4,4,4,128,128]{4,3,2,1,0:T(8,128)(2,1)} broadcast(bf16[4,4,128,128]{3,2,1,0:T(8,128)(2,1)S(1)} %bitcast.26), dimensions={1,2,3,4} | broadcast | bytes 2621440 | tf_op jit(solution)/shard_map/broadcast_in_dim | solution.py:170
  32.8 0.0 copy-start
  32.8 3.7 %all-to-all-start.1 = ((bf16[4,4,4,128,128]{4,3,2,1,0:T(8,128)(2,1)}), bf16[4,4,4,128,128]{4,3,2,1,0:T(8,128)(2,1)S(1)}, u32[]{:S(2)}, u32[]{:S(2)}) async-start(bf16[4,4,4,128,128]{4,3,2,1,0:T(8,128)(2,1)} %broadcast_in_dim.16), calls=%async_computation.1 | async-start | bytes 4194304 | tf_op jit(solution)/shard_map/all_to_all | solution.py:170
  36.6 0.0 copy-done
  36.6 6.3 %collective-permute-start.1 = (bf16[11,256,256]{2,1,0:T(8,128)(2,1)S(1)}, bf16[11,256,256]{2,1,0:T(8,128)(2,1)}, u32[]{:S(2)}, u32[]{:S(2)}) collective-permute-start(bf16[11,256,256]{2,1,0:T(8,128)(2,1)S(1)} %bitcast.20), channel_id=1, source_target_pairs={{0,16},{16,0},{1,17},{17,1},{2,18},{18,2},{3,19},{19,3},{4,20},{20... | collective-permute-start | bytes 4325384 | tf_op jit(solution)/shard_map/ppermute | solution.py:149
  42.9 8.6 %collective-permute-done.refs_1_ = bf16[11,256,256]{2,1,0:T(8,128)(2,1)} collective-permute-done((bf16[11,256,256]{2,1,0:T(8,128)(2,1)}, bf16[11,256,256]{2,1,0:T(8,128)(2,1)}, u32[]{:S(2)}, u32[]{:S(2)}) %collective-permute-start) | collective-permute-done | bytes 1441824 | tf_op jit(solution)/shard_map/ppermute | solution.py:149
  51.5 3.2 %collective-permute-start.2 = (bf16[11,256,256]{2,1,0:T(8,128)(2,1)}, bf16[11,256,256]{2,1,0:T(8,128)(2,1)}, u32[]{:S(2)}, u32[]{:S(2)}) collective-permute-start(bf16[11,256,256]{2,1,0:T(8,128)(2,1)} %collective-permute-done.refs_1_), channel_id=1, source_target_pairs={{0,16},{16,0},{1,17},{17,1},{2,18},{18,2},{3,19},{19,3},{4,20},{20... | collective-permute-start | bytes 4325384 | tf_op jit(solution)/shard_map/ppermute | solution.py:149
  54.7 0.1 pad_add_fusion.place_ref
  54.8 0.7 slice_convert_fusion.meta_ref
  55.5 0.0 collective-permute-done.1.refs_2_
  55.5 3.0 %all-to-all-done.1.refs_4_ = bf16[4,4,4,128,128]{4,3,2,1,0:T(8,128)(2,1)S(1)} async-done(((bf16[4,4,4,128,128]{4,3,2,1,0:T(8,128)(2,1)}), bf16[4,4,4,128,128]{4,3,2,1,0:T(8,128)(2,1)S(1)}, u32[]{:S(2)}, u32[]{:S(2)}) %all-to-all-start.1) | async-done | bytes 2097184 | tf_op jit(solution)/shard_map/all_to_all | solution.py:170
  58.5 0.0 collective-permute-done.2.refs_3_
  58.5 5.0 %shard_map.104 = bf16[8,2,256,128]{3,2,1,0:T(8,128)(2,1)S(1)} custom-call(s32[2]{0:T(128)S(1)} %pad_add_fusion.place_ref, s32[4,3,11]{2,1,0:T(4,128)S(1)} %slice_convert_fusion.meta_ref, bf16[11,256,256]{2,1,0:T(8,128)(2,1)S(1)} %bitcast.21, bf16[11,256,256]{2,1,0:T(8,128)(2,1)} %collective-permute-done.refs_1_, ...), custom_call_target="tpu_custom_call" | custom-call | tf_op jit(solution)/shard_map/pallas_call | solution.py:172
  63.5 0.0 copy-start.1
  63.6 0.0 copy-start.3
  63.6 0.0 copy-start.4
  63.6 44.7 %all_to_all.46.parts_ref = bf16[8,2,256,128]{3,2,1,0:T(8,128)(2,1)S(1)} all-to-all(bf16[8,2,256,128]{3,2,1,0:T(8,128)(2,1)S(1)} %shard_map.104), channel_id=1, replica_groups=mesh['z_lo'=4,'x'=4,'core'=2,'z_hi'=2,'y_pair'=4,'y_odd'=2] {'z_hi','y_p..., dimensions={0} | all-to-all | bytes 2097152 | tf_op jit(solution)/shard_map/all_to_all | solution.py:184
  108.3 0.1 shard_map.105
  108.5 8.1 %all_to_all.47.shares_ref = bf16[4,128,128]{2,1,0:T(8,128)(2,1)S(1)} all-to-all(bf16[4,128,128]{2,1,0:T(8,128)(2,1)S(1)} %bitcast.24), channel_id=1, replica_groups=mesh['z_lo'=4,'x'=4,'core'=2,'z_hi'=2,'y_pair'=4,'y_odd'=2] {'core','y_o..., dimensions={0} | all-to-all | bytes 262144 | tf_op jit(solution)/shard_map/all_to_all | solution.py:186
  116.5 0.0 copy-done.1
  116.5 0.0 copy-done.3
  116.5 0.0 copy-done.4
  116.6 1.0 shard_map.106
  117.5 12.6 %all_to_all.48.parts_ref = bf16[4,128,640]{2,1,0:T(8,128)(2,1)S(1)} all-to-all(bf16[4,128,640]{2,1,0:T(8,128)(2,1)S(1)} %bitcast.22), channel_id=1, replica_groups=mesh['z_lo'=4,'x'=4,'core'=2,'z_hi'=2,'y_pair'=4,'y_odd'=2] {'core','y_o..., dimensions={0} | all-to-all | bytes 1310720 | tf_op jit(solution)/shard_map/all_to_all | solution.py:197
  130.2 0.2 shard_map.107
  130.3 13.5 %all_to_all.49.parts_ref = bf16[16,8,640]{2,1,0:T(8,128)(2,1)S(1)} all-to-all(bf16[16,8,640]{2,1,0:T(8,128)(2,1)S(1)} %bitcast.23), channel_id=1, replica_groups=mesh['z_lo'=4,'x'=4,'core'=2,'z_hi'=2,'y_pair'=4,'y_odd'=2] {'x','y_pair'}, dimensions={0} | all-to-all | bytes 327680 | tf_op jit(solution)/shard_map/all_to_all | solution.py:199
  143.8 0.2 shard_map.108
  144.0 9.6 %all_to_all.50.parts_ref = bf16[8,8,640]{2,1,0:T(8,128)(2,1)S(1)} all-to-all(bf16[8,8,640]{2,1,0:T(8,128)(2,1)S(1)} %shard_map.108), channel_id=1, replica_groups=mesh['z_lo'=4,'x'=4,'core'=2,'z_hi'=2,'y_pair'=4,'y_odd'=2] {'z_lo','z_hi'}, dimensions={0} | all-to-all | bytes 163840 | tf_op jit(solution)/shard_map/all_to_all | solution.py:200
  153.5 0.2 shard_map.109
  153.7 12.7 %all_to_all.51 = bf16[16,8,640]{2,1,0:T(8,128)(2,1)S(1)} all-to-all(bf16[16,8,640]{2,1,0:T(8,128)(2,1)S(1)} %shard_map.109), channel_id=1, replica_groups=mesh['z_lo'=4,'x'=4,'core'=2,'z_hi'=2,'y_pair'=4,'y_odd'=2] {'x','y_pair'}, dimensions={0} | all-to-all | bytes 327680 | tf_op jit(solution)/shard_map/all_to_all | solution.py:201
  166.4 0.1 broadcast_in_dim.19
  166.4 16.0 %all_to_all.52 = bf16[4,128,640]{2,1,0:T(8,128)(2,1)S(1)} all-to-all(bf16[4,128,640]{2,1,0:T(8,128)(2,1)S(1)} %broadcast_in_dim.19), channel_id=1, replica_groups=mesh['z_lo'=4,'x'=4,'core'=2,'z_hi'=2,'y_pair'=4,'y_odd'=2] {'core','y_o..., dimensions={0} | all-to-all | bytes 1310720 | tf_op jit(solution)/shard_map/all_to_all | solution.py:202
  182.4 1.1 shard_map.110
  (3 shorter events, 0.0 us)
Async XLA Ops:
  2.1 0.9 copy-start.2
  16.6 2.0 %copy-start.5 = (bf16[4,144,128]{2,1,0:T(8,128)(2,1)}, bf16[4,144,128]{2,1,0:T(8,128)(2,1)S(1)}, u32[]{:S(2)}) copy-start(bf16[4,144,128]{2,1,0:T(8,128)(2,1)S(1)} %all_to_all.45) | copy-start | bytes 442372
  16.6 34.9 %collective-permute-start = (bf16[11,256,256]{2,1,0:T(8,128)(2,1)}, bf16[11,256,256]{2,1,0:T(8,128)(2,1)}, u32[]{:S(2)}, u32[]{:S(2)}) collective-permute-start(bf16[11,256,256]{2,1,0:T(8,128)(2,1)} %bitcast.19), channel_id=1, source_target_pairs={{0,1},{1,0},{2,3},{3,2},{4,5},{5,4},{6,7},{7,6},{8,9},{9,8},{10,11... | collective-permute-start | bytes 4325384 | tf_op jit(solution)/shard_map/ppermute | solution.py:149
  32.8 3.8 %copy-start = (bf16[1,1,11,256,256]{4,3,2,1,0:T(8,128)(2,1)S(1)}, bf16[1,1,11,256,256]{4,3,2,1,0:T(8,128)(2,1)}, u32[]{:S(2)}) copy-start(bf16[1,1,11,256,256]{4,3,2,1,0:T(8,128)(2,1)} %param.12) | copy-start | bytes 4325380
  32.8 25.7 %all-to-all-start.1 = ((bf16[4,4,4,128,128]{4,3,2,1,0:T(8,128)(2,1)}), bf16[4,4,4,128,128]{4,3,2,1,0:T(8,128)(2,1)S(1)}, u32[]{:S(2)}, u32[]{:S(2)}) async-start(bf16[4,4,4,128,128]{4,3,2,1,0:T(8,128)(2,1)} %broadcast_in_dim.16), calls=%async_computation.1 | async-start | bytes 4194304 | tf_op jit(solution)/shard_map/all_to_all | solution.py:170
  36.6 18.9 %collective-permute-start.1 = (bf16[11,256,256]{2,1,0:T(8,128)(2,1)S(1)}, bf16[11,256,256]{2,1,0:T(8,128)(2,1)}, u32[]{:S(2)}, u32[]{:S(2)}) collective-permute-start(bf16[11,256,256]{2,1,0:T(8,128)(2,1)S(1)} %bitcast.20), channel_id=1, source_target_pairs={{0,16},{16,0},{1,17},{17,1},{2,18},{18,2},{3,19},{19,3},{4,20},{20... | collective-permute-start | bytes 4325384 | tf_op jit(solution)/shard_map/ppermute | solution.py:149
  51.5 7.0 %collective-permute-start.2 = (bf16[11,256,256]{2,1,0:T(8,128)(2,1)}, bf16[11,256,256]{2,1,0:T(8,128)(2,1)}, u32[]{:S(2)}, u32[]{:S(2)}) collective-permute-start(bf16[11,256,256]{2,1,0:T(8,128)(2,1)} %collective-permute-done.refs_1_), channel_id=1, source_target_pairs={{0,16},{16,0},{1,17},{17,1},{2,18},{18,2},{3,19},{19,3},{4,20},{20... | collective-permute-start | bytes 4325384 | tf_op jit(solution)/shard_map/ppermute | solution.py:149
  63.5 53.0 %copy-start.1 = (bf16[512,512]{1,0:T(8,128)(2,1)S(1)}, bf16[512,512]{1,0:T(8,128)(2,1)}, u32[]{:S(2)}) copy-start(bf16[512,512]{1,0:T(8,128)(2,1)} %weight_ref.1) | copy-start | bytes 1572868
  63.6 53.0 %copy-start.3 = (bf16[128,512]{1,0:T(8,128)(2,1)S(1)}, bf16[128,512]{1,0:T(8,128)(2,1)}, u32[]{:S(2)}) copy-start(bf16[128,512]{1,0:T(8,128)(2,1)} %cot_ref.1) | copy-start | bytes 393220
  63.6 53.0 %copy-start.4 = (f32[512]{0:T(512)S(1)}, f32[512]{0:T(512)}, u32[]{:S(2)}) copy-start(f32[512]{0:T(512)} %param.10) | copy-start | bytes 6148

commit v5 on v4

v5 whole, which is shorter than its diff:
```python
import jax
import jax.numpy as jnp
from jax import lax
from jax.experimental import pallas as pl
from jax.experimental.pallas import tpu as pltpu
from jax.sharding import Mesh, PartitionSpec as P

F32 = jnp.float32
BF16 = jnp.bfloat16
LANES = 128
VMEM = pl.BlockSpec(memory_space=pltpu.VMEM)
SMEM = pl.BlockSpec(memory_space=pltpu.SMEM)
ANY = pl.BlockSpec(memory_space=pl.ANY)
PARAMS = pltpu.CompilerParams(vmem_limit_bytes=40 * 1024 * 1024)
AXES = ("z_lo", "x", "core", "z_hi", "y_pair", "y_odd")
ROW = ("z_lo", "x", "core")
COL = ("z_hi", "y_pair", "y_odd")
QUAD = ("core", "y_odd")
PLANE = ("x", "y_pair")
DEPTH = ("z_lo", "z_hi")
SIZES = (4, 4, 2, 2, 4, 2)
SIDE = 16


def quarter_kernel(features_ref, cot_ref, side_ref, out_ref):
    nodes = features_ref.shape[0]
    for part in range(out_ref.shape[0]):
        lanes = slice(part * LANES, (part + 1) * LANES)
        out_ref[part, :nodes, :] = features_ref[:, lanes]
        out_ref[part, nodes : 2 * nodes, :] = cot_ref[:, lanes]
        out_ref[part, 2 * nodes :, :] = side_ref[...]


def tile_kernel(place_ref, meta_ref, *refs):
    given, block_ref, out_ref, tiles, total, sems = refs[:4], refs[4], refs[5], refs[6], refs[7], refs[8]
    _, slots, size, _ = tiles.shape
    n_x = block_ref.shape[0]
    core, odd = place_ref[0], place_ref[1]

    def tile_copy(which, slot):
        return pltpu.make_async_copy(
            given[which].at[slot], tiles.at[which, slot], sems.at[which, slot]
        )

    def cell_of(which):
        cell_core, cell_odd = (core + which // 2) % 2, (odd + which % 2) % 2
        return cell_core, cell_odd, cell_core * 2 + cell_odd

    for which in range(4):

        def fetch(slot, carry):
            tile_copy(which, slot).start()
            return carry

        lax.fori_loop(0, meta_ref[cell_of(which)[2], 2, 0], fetch, 0)
    total[...] = jnp.zeros_like(total)
    for which in range(4):
        cell_core, cell_odd, cell = cell_of(which)

        def step(slot, carry):
            tile_copy(which, slot).wait()
            chip = meta_ref[cell, 1, slot]
            z, x = chip // n_x, lax.rem(chip, n_x)
            window = jnp.concatenate(
                [block_ref[x, z, cell_odd], block_ref[x, z, 2 + cell_odd]], axis=0
            )
            total[cell_core, meta_ref[cell, 0, slot]] += jnp.dot(
                tiles[which, slot], window, preferred_element_type=F32
            )
            return carry

        lax.fori_loop(0, meta_ref[cell, 2, 0], step, 0)
    n_pair = out_ref.shape[0]
    for row in range(total.shape[1]):
        for cell_core in range(2):
            out_ref[row % n_pair, row // n_pair, cell_core] = total[cell_core, row].astype(BF16)


def add(ref):
    total = ref[0].astype(F32)
    for part in range(1, ref.shape[0]):
        total = total + ref[part].astype(F32)
    return total


def pair_kernel(place_ref, parts_ref, keep_ref, send_ref):
    mine = place_ref[2]
    keep_ref[...] = add(parts_ref.at[:, mine])
    send_ref[...] = add(parts_ref.at[:, 1 - mine]).astype(BF16)


def spread_kernel(keep_ref, given_ref, out_ref):
    total = (keep_ref[...] + given_ref[...].astype(F32)).astype(BF16)
    for copy in range(out_ref.shape[0]):
        out_ref[copy] = total


def split_rows(row):
    high = row.astype(BF16)
    low = (row - high.astype(F32)).astype(BF16)
    tall = (SIDE, row.shape[1])
    place = lax.broadcasted_iota(jnp.int32, tall, 0)
    high = jnp.broadcast_to(high.astype(F32), tall)
    low = jnp.broadcast_to(low.astype(F32), tall)
    return jnp.where(place == 0, high, jnp.where(place == 1, low, 0.0)).astype(BF16)


def node_kernel(place_ref, shares_ref, quarters_ref, weight_ref, bias_ref, act_ref, grads_ref):
    quad, nodes = shares_ref.shape[0], shares_ref.shape[2]
    me = place_ref[0] * 2 + place_ref[1]
    aggregated = jnp.concatenate(
        [
            jnp.concatenate([shares_ref[part, group] for part in range(quad)], axis=1)
            for group in range(quad)
        ],
        axis=0,
    )
    own = jnp.concatenate([shares_ref[part, me] for part in range(quad)], axis=1)
    preact = jnp.dot(own, weight_ref[...], preferred_element_type=F32) + bias_ref[...]
    act_ref[...] = (preact * jax.nn.sigmoid(preact)).astype(BF16)
    lanes = pl.ds(pl.multiple_of(me * LANES, LANES), LANES)
    preact = jnp.dot(aggregated, weight_ref[:, lanes], preferred_element_type=F32) + bias_ref[:, lanes]
    sigmoid_part = jax.nn.sigmoid(preact)
    cot = jnp.concatenate([quarters_ref[group, nodes : 2 * nodes] for group in range(quad)], axis=0)
    grad = cot.astype(F32) * sigmoid_part * (1.0 + preact * (1.0 - sigmoid_part))
    product = lax.dot_general(
        aggregated, grad.astype(BF16), (((0,), (0,)), ((), ())), preferred_element_type=F32
    ).astype(BF16)
    side = split_rows(jnp.sum(grad, axis=0, keepdims=True))
    n_chunks, tall, _ = grads_ref.shape
    depth = tall - SIDE
    for chunk in range(n_chunks):
        grads_ref[chunk, :depth] = product[chunk * depth : (chunk + 1) * depth]
        grads_ref[chunk, depth:] = side


def sum_kernel(parts_ref, out_ref):
    total = add(parts_ref)
    depth = total.shape[0] - SIDE
    main = total[:depth].astype(BF16)
    side = split_rows(total[depth : depth + 1] + total[depth + 1 : depth + 2])
    for copy in range(out_ref.shape[0]):
        out_ref[copy, :depth] = main
        out_ref[copy, depth:] = side


def copy_kernel(given_ref, out_ref):
    n_chunks, tall, _ = given_ref.shape
    depth = tall - SIDE
    for copy in range(out_ref.shape[0]):
        for chunk in range(n_chunks):
            out_ref[copy, chunk * depth : (chunk + 1) * depth] = given_ref[chunk, :depth]
        out_ref[copy, n_chunks * depth :] = given_ref[0, depth:]


def last_kernel(parts_ref, weight_ref, bias_ref):
    width = weight_ref.shape[0]
    for part in range(parts_ref.shape[0]):
        lanes = slice(part * LANES, (part + 1) * LANES)
        weight_ref[:, lanes] = parts_ref[part, :width].astype(F32)
        side = parts_ref[part, width:].astype(F32)
        bias_ref[:, lanes] = side[0:1] + side[1:2]


def call(kernel, out, *args, scalars=0):
    shapes = jax.tree.map(lambda o: jax.ShapeDtypeStruct(*o), out, is_leaf=lambda o: isinstance(o[0], tuple) and not isinstance(o[1], tuple))
    specs = jax.tree.map(lambda o: VMEM, shapes)
    return pl.pallas_call(
        kernel, out_shape=shapes, in_specs=[SMEM] * scalars + [VMEM] * (len(args) - scalars), out_specs=specs, compiler_params=PARAMS
    )(*args)


def swap(array, axis):
    return lax.ppermute(array, axis, [(0, 1), (1, 0)])


def per_device(
    features, weight, bias_term, cotangent, tile_values, tile_rows, tile_cols, tile_count
):
    nodes, width = features.shape
    _, _, slots, size, _ = tile_values.shape
    n_z, n_x = lax.axis_size("z_lo"), lax.axis_size("x")
    n_pair = lax.axis_size("y_pair")
    tiles = tile_values[0, 0]
    ints = [tile_rows[0, 0], tile_cols[0, 0], jnp.broadcast_to(tile_count[0], (slots,))]
    side = jnp.pad(jnp.stack(ints), ((0, SIDE - 3), (0, LANES - slots))).astype(BF16)
    quarters = call(
        quarter_kernel, ((4, 2 * nodes + SIDE, LANES), BF16), features, cotangent, side
    )
    quarters = lax.all_to_all(quarters, QUAD, 0, 0)
    quarters, tiles = lax.optimization_barrier((quarters, tiles))
    tiles_y = swap(tiles, "y_odd")
    tiles_core = swap(tiles, "core")
    tiles_both = swap(tiles_y, "core")
    meta = quarters[:, 2 * nodes : 2 * nodes + 3, :slots].astype(jnp.int32)
    near = lax.all_gather(quarters[:, :nodes], "z_lo", axis=0)
    blocks = lax.all_to_all(jnp.broadcast_to(near[None], (n_x,) + near.shape), "x", 0, 0)
    place = jnp.stack([lax.axis_index(axis) for axis in QUAD + ("z_hi",)]).astype(jnp.int32)
    term = pl.pallas_call(
        tile_kernel,
        out_shape=jax.ShapeDtypeStruct((n_pair, 2, 2, size, LANES), BF16),
        in_specs=[SMEM, SMEM] + [ANY] * 4 + [VMEM],
        out_specs=VMEM,
        scratch_shapes=[
            pltpu.VMEM((4, slots, size, size), BF16),
            pltpu.VMEM((2, 2 * n_pair, size, LANES), F32),
            pltpu.SemaphoreType.DMA((4, slots)),
        ],
        compiler_params=PARAMS,
    )(place, meta, tiles, tiles_y, tiles_core, tiles_both, blocks)
    shares = lax.all_to_all(term, "y_pair", 0, 0)
    block = (2, size, LANES)
    keep, send = call(pair_kernel, ((block, F32), (block, BF16)), place, shares, scalars=1)
    shares = call(spread_kernel, ((4,) + block, BF16), keep, swap(send, "z_hi"))
    shares = lax.all_to_all(shares.reshape(4, 4, nodes, LANES), QUAD, 0, 0)
    n_plane, n_depth = lax.axis_size(PLANE), lax.axis_size(DEPTH)
    chunk = (width // n_plane + SIDE, LANES)
    activations, grads = call(
        node_kernel,
        (((nodes, width), BF16), ((n_plane,) + chunk, BF16)),
        place,
        shares,
        quarters,
        weight,
        bias_term[None, :],
        scalars=1,
    )
    grads = lax.all_to_all(grads, PLANE, 0, 0)
    grads = call(sum_kernel, ((n_depth,) + chunk, BF16), grads)
    grads = lax.all_to_all(grads, DEPTH, 0, 0)
    grads = call(sum_kernel, ((n_plane,) + chunk, BF16), grads)
    grads = lax.all_to_all(grads, PLANE, 0, 0)
    grads = call(copy_kernel, ((4, width + SIDE, LANES), BF16), grads)
    grads = lax.all_to_all(grads, QUAD, 0, 0)
    weight_grad, bias_grad = call(
        last_kernel, (((width, width), F32), ((1, width), F32)), grads
    )
    return activations, weight_grad, bias_grad[0]


def solution(mesh):
    cut = Mesh(mesh.devices.reshape(SIZES), AXES)
    everywhere = P(AXES, None)
    return jax.shard_map(
        per_device,
        mesh=cut,
        in_specs=(
            everywhere,
            P(),
            P(),
            everywhere,
            P(ROW, COL, None, None, None),
            P(ROW, COL, None),
            P(ROW, COL, None),
            P(ROW, COL),
        ),
        out_specs=(everywhere, P(), P()),
        check_vma=False,
    )
```

time: 184 us -> 186 us (1.011)
  blocking collectives: 143 us -> 132 us
  starting transfers between devices: 15.3 us -> 21.6 us
  waiting for transfers between devices: 11.6 us -> 16.6 us
  local copies, waits for them, and re-layouts: 2.97 us -> 5.18 us
    all_to_all x7 -> x6, blocking collectives: 117 us -> 105 us  [the longest x1 34.7 us: per_device(): shares = lax.all_to_all(term, 'y_pair', 0, 0)]
    ppermute x3 -> x4, starting transfers between devices: 11.6 us -> 18 us  [swap(): return lax.ppermute(array, axis, [(0, 1), (1, 0)])]
    ppermute x3 -> x4, waiting for transfers between devices: 8.61 us -> 13.1 us  [swap(): return lax.ppermute(array, axis, [(0, 1), (1, 0)])]
    unnamed x12 -> x10, local copies, waits for them, and re-layouts: 0.93 us -> 3.18 us
    pallas_call x8 -> x9, Pallas kernels: 7.72 us -> 8.18 us  [the longest x1 4.5 us: per_device(): pl.pallas_call(tile_kernel, out_shape=jax.ShapeDtypeStruct((n_pair, 2, 2,...]
  transfers between devices with their start and end apart: 4 -> 5, of which waited for: 2 -> 3; matrix products, arithmetic and copies ran while one was open for 1% -> 1% of each run, Pallas kernels for 0% -> 0%
where the time goes in v5:
time: 186 us
  blocking collectives  132 us (71%)
  starting transfers between devices  21.6 us (12%)
  waiting for transfers between devices  16.6 us (9%)
  Pallas kernels  8.18 us (4%)
  local copies, waits for them, and re-layouts  5.18 us (3%)
    all_to_all x1, blocking collectives, per_device(): shares = lax.all_to_all(term, 'y_pair', 0, 0)  34.7 us
    all_to_all x2, blocking collectives, per_device(): grads = lax.all_to_all(grads, PLANE, 0, 0)  29.6 us
    ppermute x4, starting transfers between devices, swap(): return lax.ppermute(array, axis, [(0, 1), (1, 0)])  18 us
    all_to_all x1, blocking collectives, per_device(): grads = lax.all_to_all(grads, QUAD, 0, 0)  15.7 us
    all_to_all x1, blocking collectives, per_device(): quarters = lax.all_to_all(quarters, QUAD, 0, 0)  15 us
    ppermute x4, waiting for transfers between devices, swap(): return lax.ppermute(array, axis, [(0, 1), (1, 0)])  13.1 us
    all_to_all x1, blocking collectives, per_device(): shares = lax.all_to_all(shares.reshape(4, 4, nodes, LANES), QUAD, 0, 0)  12.5 us
    all_gather x1, blocking collectives, per_device(): near = lax.all_gather(quarters[:, :nodes], 'z_lo', axis=0)  12.2 us
  transfers between devices with their start and end apart: 5, of which 3 were waited for; matrix products, arithmetic and copies ran while one was open for 1% of the time, Pallas kernels for 0%

profile of v5, /device:TPU:1, one launch (start us, length us, event | category | flops | bytes accessed | tf_op | source)
XLA Modules:
  0.0 185.5 jit_solution(2457552843425986931)
XLA Ops:
  1.3 0.7 convert_bitcast_fusion
  2.0 0.1 pad.8.clone
  2.0 0.1 maximum_maximum_fusion
  2.1 0.0 copy-start.2
  2.1 0.9 copy-done.2
  3.0 0.0 copy-start.3
  3.0 0.9 copy-done.3
  4.0 15.0 %all_to_all.40.quarters_ref = bf16[4,272,128]{2,1,0:T(8,128)(2,1)S(1)} all-to-all(bf16[4,272,128]{2,1,0:T(8,128)(2,1)S(1)} %shard_map.103), channel_id=1, replica_groups=mesh['z_lo'=4,'x'=4,'core'=2,'z_hi'=2,'y_pair'=4,'y_odd'=2] {'core','y_o..., dimensions={0} | all-to-all | bytes 557056 | tf_op jit(solution)/shard_map/all_to_all | solution.py:190
  18.9 2.0 %collective-permute-start = (bf16[11,256,256]{2,1,0:T(8,128)(2,1)}, bf16[11,256,256]{2,1,0:T(8,128)(2,1)}, u32[]{:S(2)}, u32[]{:S(2)}) collective-permute-start(bf16[11,256,256]{2,1,0:T(8,128)(2,1)} %bitcast.16), channel_id=1, source_target_pairs={{0,1},{1,0},{2,3},{3,2},{4,5},{5,4},{6,7},{7,6},{8,9},{9,8},{10,11... | collective-permute-start | bytes 4325384 | tf_op jit(solution)/shard_map/ppermute | solution.py:174
  21.0 12.2 %all-gather = bf16[16,128,128]{2,1,0:T(8,128)(2,1)S(1)} all-gather(bf16[4,128,128]{2,1,0:T(8,128)(2,1)S(1)} %slice.7), channel_id=2, replica_groups=mesh['z_lo'=4,'x'=4,'core'=2,'z_hi'=2,'y_pair'=4,'y_odd'=2] {'z_lo'}, dimensions={0}, use_global_device_ids=true | all-gather | bytes 655360 | tf_op jit(solution)/shard_map/all_gather | solution.py:196
  33.2 1.9 %broadcast_in_dim.4 = bf16[4,4,4,128,128]{4,3,2,1,0:T(8,128)(2,1)} broadcast(bf16[4,4,128,128]{3,2,1,0:T(8,128)(2,1)S(1)} %bitcast.20), dimensions={1,2,3,4} | broadcast | bytes 2621440 | tf_op jit(solution)/shard_map/broadcast_in_dim | solution.py:197
  35.1 3.6 %all-to-all-start.1 = ((bf16[4,4,4,128,128]{4,3,2,1,0:T(8,128)(2,1)}), bf16[4,4,4,128,128]{4,3,2,1,0:T(8,128)(2,1)S(1)}, u32[]{:S(2)}, u32[]{:S(2)}) async-start(bf16[4,4,4,128,128]{4,3,2,1,0:T(8,128)(2,1)} %broadcast_in_dim.4), calls=%async_computation.1 | async-start | bytes 4194304 | tf_op jit(solution)/shard_map/all_to_all | solution.py:197
  38.8 6.3 %collective-permute-start.1 = (bf16[11,256,256]{2,1,0:T(8,128)(2,1)}, bf16[11,256,256]{2,1,0:T(8,128)(2,1)}, u32[]{:S(2)}, u32[]{:S(2)}) collective-permute-start(bf16[11,256,256]{2,1,0:T(8,128)(2,1)} %bitcast.17), channel_id=1, source_target_pairs={{0,16},{16,0},{1,17},{17,1},{2,18},{18,2},{3,19},{19,3},{4,20},{20... | collective-permute-start | bytes 4325384 | tf_op jit(solution)/shard_map/ppermute | solution.py:174
  45.1 8.7 %collective-permute-done.refs_1_ = bf16[11,256,256]{2,1,0:T(8,128)(2,1)} collective-permute-done((bf16[11,256,256]{2,1,0:T(8,128)(2,1)}, bf16[11,256,256]{2,1,0:T(8,128)(2,1)}, u32[]{:S(2)}, u32[]{:S(2)}) %collective-permute-start) | collective-permute-done | bytes 1441824 | tf_op jit(solution)/shard_map/ppermute | solution.py:174
  53.8 3.2 %collective-permute-start.2 = (bf16[11,256,256]{2,1,0:T(8,128)(2,1)}, bf16[11,256,256]{2,1,0:T(8,128)(2,1)}, u32[]{:S(2)}, u32[]{:S(2)}) collective-permute-start(bf16[11,256,256]{2,1,0:T(8,128)(2,1)} %collective-permute-done.refs_1_), channel_id=1, source_target_pairs={{0,16},{16,0},{1,17},{17,1},{2,18},{18,2},{3,19},{19,3},{4,20},{20... | collective-permute-start | bytes 4325384 | tf_op jit(solution)/shard_map/ppermute | solution.py:174
  57.1 0.1 pad_add_fusion.place_ref
  57.1 0.0 collective-permute-done.1.refs_2_
  57.1 3.5 %all-to-all-done.1.refs_4_ = bf16[4,4,4,128,128]{4,3,2,1,0:T(8,128)(2,1)S(1)} async-done(((bf16[4,4,4,128,128]{4,3,2,1,0:T(8,128)(2,1)}), bf16[4,4,4,128,128]{4,3,2,1,0:T(8,128)(2,1)S(1)}, u32[]{:S(2)}, u32[]{:S(2)}) %all-to-all-start.1) | async-done | bytes 2097184 | tf_op jit(solution)/shard_map/all_to_all | solution.py:197
  60.7 0.0 collective-permute-done.2.refs_3_
  60.7 0.0 copy-start
  60.7 1.4 copy-done
  62.0 4.5 %shard_map.104 = bf16[4,2,2,256,128]{4,3,2,1,0:T(8,128)(2,1)S(1)} custom-call(s32[3]{0:T(128)S(1)} %pad_add_fusion.place_ref, s32[4,3,11]{2,1,0:T(4,128)S(1)} %slice_convert_fusion.meta_ref, bf16[11,256,256]{2,1,0:T(8,128)(2,1)S(1)} %bitcast.18, bf16[11,256,256]{2,1,0:T(8,128)(2,1)} %collective-permute-done.refs_1_, ...), custom_call_target="tpu_custom_call" | custom-call | tf_op jit(solution)/shard_map/pallas_call | solution.py:199
  66.5 34.7 %all_to_all.41.parts_ref = bf16[4,2,2,256,128]{4,3,2,1,0:T(8,128)(2,1)S(1)} all-to-all(bf16[4,2,2,256,128]{4,3,2,1,0:T(8,128)(2,1)S(1)} %shard_map.104), channel_id=1, replica_groups=mesh['z_lo'=4,'x'=4,'core'=2,'z_hi'=2,'y_pair'=4,'y_odd'=2] {'y_pair'}, dimensions={0} | all-to-all | bytes 2097152 | tf_op jit(solution)/shard_map/all_to_all | solution.py:211
  101.3 0.0 copy-start.1
  101.3 0.0 copy-start.4
  101.3 0.7 shard_map.105
  101.9 6.4 %collective-permute-start.3 = (bf16[2,256,128]{2,1,0:T(8,128)(2,1)S(1)}, bf16[2,256,128]{2,1,0:T(8,128)(2,1)S(1)}, u32[]{:S(2)}, u32[]{:S(2)}) collective-permute-start(bf16[2,256,128]{2,1,0:T(8,128)(2,1)S(1)} %get-tuple-element.14), channel_id=1, source_target_pairs={{0,8},{8,0},{1,9},{9,1},{2,10},{10,2},{3,11},{11,3},{4,12},{12,4},... | collective-permute-start | bytes 393224 | tf_op jit(solution)/shard_map/ppermute | solution.py:174
  108.4 4.3 %collective-permute-done.3.given_ref = bf16[2,256,128]{2,1,0:T(8,128)(2,1)S(1)} collective-permute-done((bf16[2,256,128]{2,1,0:T(8,128)(2,1)S(1)}, bf16[2,256,128]{2,1,0:T(8,128)(2,1)S(1)}, u32[]{:S(2)}, u32[]{:S(2)}) %collective-permute-start.3) | collective-permute-done | bytes 131104 | tf_op jit(solution)/shard_map/ppermute | solution.py:174
  112.7 12.5 %all_to_all.42.shares_ref = bf16[4,4,128,128]{3,2,1,0:T(8,128)(2,1)S(1)} all-to-all(bf16[4,4,128,128]{3,2,1,0:T(8,128)(2,1)S(1)} %bitcast.15), channel_id=1, replica_groups=mesh['z_lo'=4,'x'=4,'core'=2,'z_hi'=2,'y_pair'=4,'y_odd'=2] {'core','y_o..., dimensions={0} | all-to-all | bytes 1048576 | tf_op jit(solution)/shard_map/all_to_all | solution.py:215
  125.2 0.0 copy-done.1
  125.2 0.0 copy-done.4
  125.2 1.7 shard_map.107
  126.9 16.7 %all_to_all.43.parts_ref = bf16[16,48,128]{2,1,0:T(8,128)(2,1)S(1)} all-to-all(bf16[16,48,128]{2,1,0:T(8,128)(2,1)S(1)} %get-tuple-element.16), channel_id=1, replica_groups=mesh['z_lo'=4,'x'=4,'core'=2,'z_hi'=2,'y_pair'=4,'y_odd'=2] {'x','y_pair'}, dimensions={0} | all-to-all | bytes 393216 | tf_op jit(solution)/shard_map/all_to_all | solution.py:228
  143.7 12.1 %all_to_all.44.parts_ref = bf16[8,48,128]{2,1,0:T(8,128)(2,1)S(1)} all-to-all(bf16[8,48,128]{2,1,0:T(8,128)(2,1)S(1)} %shard_map.108), channel_id=1, replica_groups=mesh['z_lo'=4,'x'=4,'core'=2,'z_hi'=2,'y_pair'=4,'y_odd'=2] {'z_lo','z_hi'}, dimensions={0} | all-to-all | bytes 196608 | tf_op jit(solution)/shard_map/all_to_all | solution.py:230
  155.8 12.8 %all_to_all.45.given_ref = bf16[16,48,128]{2,1,0:T(8,128)(2,1)S(1)} all-to-all(bf16[16,48,128]{2,1,0:T(8,128)(2,1)S(1)} %shard_map.109), channel_id=1, replica_groups=mesh['z_lo'=4,'x'=4,'core'=2,'z_hi'=2,'y_pair'=4,'y_odd'=2] {'x','y_pair'}, dimensions={0} | all-to-all | bytes 393216 | tf_op jit(solution)/shard_map/all_to_all | solution.py:232
  168.7 0.1 shard_map.110
  168.8 15.7 %all_to_all.46.parts_ref = bf16[4,528,128]{2,1,0:T(8,128)(2,1)S(1)} all-to-all(bf16[4,528,128]{2,1,0:T(8,128)(2,1)S(1)} %shard_map.110), channel_id=1, replica_groups=mesh['z_lo'=4,'x'=4,'core'=2,'z_hi'=2,'y_pair'=4,'y_odd'=2] {'core','y_o..., dimensions={0} | all-to-all | bytes 1081344 | tf_op jit(solution)/shard_map/all_to_all | solution.py:234
  184.4 1.1 shard_map.111
  (7 shorter events, 0.2 us)
Async XLA Ops:
  2.1 0.9 copy-start.2
  3.0 0.9 copy-start.3
  18.9 34.9 %collective-permute-start = (bf16[11,256,256]{2,1,0:T(8,128)(2,1)}, bf16[11,256,256]{2,1,0:T(8,128)(2,1)}, u32[]{:S(2)}, u32[]{:S(2)}) collective-permute-start(bf16[11,256,256]{2,1,0:T(8,128)(2,1)} %bitcast.16), channel_id=1, source_target_pairs={{0,1},{1,0},{2,3},{3,2},{4,5},{5,4},{6,7},{7,6},{8,9},{9,8},{10,11... | collective-permute-start | bytes 4325384 | tf_op jit(solution)/shard_map/ppermute | solution.py:174
  35.1 25.5 %all-to-all-start.1 = ((bf16[4,4,4,128,128]{4,3,2,1,0:T(8,128)(2,1)}), bf16[4,4,4,128,128]{4,3,2,1,0:T(8,128)(2,1)S(1)}, u32[]{:S(2)}, u32[]{:S(2)}) async-start(bf16[4,4,4,128,128]{4,3,2,1,0:T(8,128)(2,1)} %broadcast_in_dim.4), calls=%async_computation.1 | async-start | bytes 4194304 | tf_op jit(solution)/shard_map/all_to_all | solution.py:197
  38.8 18.4 %collective-permute-start.1 = (bf16[11,256,256]{2,1,0:T(8,128)(2,1)}, bf16[11,256,256]{2,1,0:T(8,128)(2,1)}, u32[]{:S(2)}, u32[]{:S(2)}) collective-permute-start(bf16[11,256,256]{2,1,0:T(8,128)(2,1)} %bitcast.17), channel_id=1, source_target_pairs={{0,16},{16,0},{1,17},{17,1},{2,18},{18,2},{3,19},{19,3},{4,20},{20... | collective-permute-start | bytes 4325384 | tf_op jit(solution)/shard_map/ppermute | solution.py:174
  53.8 6.9 %collective-permute-start.2 = (bf16[11,256,256]{2,1,0:T(8,128)(2,1)}, bf16[11,256,256]{2,1,0:T(8,128)(2,1)}, u32[]{:S(2)}, u32[]{:S(2)}) collective-permute-start(bf16[11,256,256]{2,1,0:T(8,128)(2,1)} %collective-permute-done.refs_1_), channel_id=1, source_target_pairs={{0,16},{16,0},{1,17},{17,1},{2,18},{18,2},{3,19},{19,3},{4,20},{20... | collective-permute-start | bytes 4325384 | tf_op jit(solution)/shard_map/ppermute | solution.py:174
  60.7 1.4 copy-start
  101.3 24.0 %copy-start.1 = (bf16[512,512]{1,0:T(8,128)(2,1)S(1)}, bf16[512,512]{1,0:T(8,128)(2,1)}, u32[]{:S(2)}) copy-start(bf16[512,512]{1,0:T(8,128)(2,1)} %weight_ref.1) | copy-start | bytes 1572868
  101.3 24.0 %copy-start.4 = (f32[512]{0:T(512)S(1)}, f32[512]{0:T(512)}, u32[]{:S(2)}) copy-start(f32[512]{0:T(512)} %param.10) | copy-start | bytes 6148
  101.9 10.8 %collective-permute-start.3 = (bf16[2,256,128]{2,1,0:T(8,128)(2,1)S(1)}, bf16[2,256,128]{2,1,0:T(8,128)(2,1)S(1)}, u32[]{:S(2)}, u32[]{:S(2)}) collective-permute-start(bf16[2,256,128]{2,1,0:T(8,128)(2,1)S(1)} %get-tuple-element.14), channel_id=1, source_target_pairs={{0,8},{8,0},{1,9},{9,1},{2,10},{10,2},{3,11},{11,3},{4,12},{12,4},... | collective-permute-start | bytes 393224 | tf_op jit(solution)/shard_map/ppermute | solution.py:174

commit v6 on v5

--- a/solution.py
+++ b/solution.py
@@ -10,25 +10,58 @@
 LANES = 128
 VMEM = pl.BlockSpec(memory_space=pltpu.VMEM)
 SMEM = pl.BlockSpec(memory_space=pltpu.SMEM)
-ANY = pl.BlockSpec(memory_space=pl.ANY)
+HBM = pl.BlockSpec(memory_space=pltpu.HBM)
 PARAMS = pltpu.CompilerParams(vmem_limit_bytes=40 * 1024 * 1024)
 AXES = ("z_lo", "x", "core", "z_hi", "y_pair", "y_odd")
 ROW = ("z_lo", "x", "core")
 COL = ("z_hi", "y_pair", "y_odd")
 QUAD = ("core", "y_odd")
-PLANE = ("x", "y_pair")
+FIRST = ("z_lo", "core", "y_odd")
 DEPTH = ("z_lo", "z_hi")
+Y = ("y_pair", "y_odd")
+PLANE = ("x", "y_pair", "y_odd")
 SIZES = (4, 4, 2, 2, 4, 2)
+ROLES = ((0, 2, 5, 7), (1, 3, 4, 6))
+PLANE_ROLES = tuple(tuple(x * 8 + y for x in range(4) for y in role) for role in ROLES)
 SIDE = 16
 
 
-def quarter_kernel(features_ref, cot_ref, side_ref, out_ref):
+def quarter_of(part, flip):
+    return part // 2 * 2 + lax.rem(part % 2 + flip, 2)
+
+
+def lanes_of(quarter):
+    return pl.ds(pl.multiple_of(quarter * LANES, LANES), LANES)
+
+
+def quarter_kernel(place_ref, rows_ref, cols_ref, count_ref, features_ref, out_ref, side, sems):
     nodes = features_ref.shape[0]
-    for part in range(out_ref.shape[0]):
-        lanes = slice(part * LANES, (part + 1) * LANES)
-        out_ref[part, :nodes, :] = features_ref[:, lanes]
-        out_ref[part, nodes : 2 * nodes, :] = cot_ref[:, lanes]
-        out_ref[part, 2 * nodes :, :] = side_ref[...]
+    copies = []
+    for place in range(out_ref.shape[0]):
+        lanes = lanes_of(quarter_of(place % 4, place_ref[3]))
+        copies.append(
+            pltpu.make_async_copy(
+                features_ref.at[:, lanes], out_ref.at[place, pl.ds(0, nodes)], sems.at[0, place]
+            )
+        )
+        copies[-1].start()
+    row = lax.broadcasted_iota(jnp.int32, side.shape, 0)
+    lane = lax.broadcasted_iota(jnp.int32, side.shape, 1)
+    values = jnp.where(row == 2, count_ref[0], 0)
+    for slot in range(rows_ref.shape[0]):
+        for kind, ref in enumerate((rows_ref, cols_ref)):
+            here = jnp.logical_and(row == kind, lane == slot)
+            values = jnp.where(here, ref[slot], values)
+    side[...] = values.astype(F32).astype(BF16)
+    for place in range(out_ref.shape[0]):
+        copies.append(
+            pltpu.make_async_copy(
+                side, out_ref.at[place, pl.ds(nodes, SIDE)], sems.at[1, place]
+            )
+        )
+        copies[-1].start()
+    for copy in copies:
+        copy.wait()
 
 
 def tile_kernel(place_ref, meta_ref, *refs):
@@ -89,10 +122,11 @@
     send_ref[...] = add(parts_ref.at[:, 1 - mine]).astype(BF16)
 
 
-def spread_kernel(keep_ref, given_ref, out_ref):
+def spread_kernel(place_ref, keep_ref, given_ref, cot_ref, out_ref):
     total = (keep_ref[...] + given_ref[...].astype(F32)).astype(BF16)
-    for copy in range(out_ref.shape[0]):
-        out_ref[copy] = total
+    for part in range(out_ref.shape[0]):
+        out_ref[part, : total.shape[0]] = total
+        out_ref[part, total.shape[0]] = cot_ref[:, lanes_of(quarter_of(part, place_ref[3]))]
 
 
 def split_rows(row):
@@ -105,23 +139,22 @@
     return jnp.where(place == 0, high, jnp.where(place == 1, low, 0.0)).astype(BF16)
 
 
-def node_kernel(place_ref, shares_ref, quarters_ref, weight_ref, bias_ref, act_ref, grads_ref):
-    quad, nodes = shares_ref.shape[0], shares_ref.shape[2]
-    me = place_ref[0] * 2 + place_ref[1]
-    aggregated = jnp.concatenate(
-        [
-            jnp.concatenate([shares_ref[part, group] for part in range(quad)], axis=1)
-            for group in range(quad)
-        ],
-        axis=0,
-    )
-    own = jnp.concatenate([shares_ref[part, me] for part in range(quad)], axis=1)
-    preact = jnp.dot(own, weight_ref[...], preferred_element_type=F32) + bias_ref[...]
+def node_kernel(place_ref, shares_ref, weight_ref, bias_ref, act_ref, grads_ref):
+    quad = shares_ref.shape[0]
+    me, flip = place_ref[0] * 2 + place_ref[1], place_ref[3]
+
+    def rows_of(group):
+        return jnp.concatenate(
+            [shares_ref[quarter_of(part, flip), group] for part in range(quad)], axis=1
+        )
+
+    aggregated = jnp.concatenate([rows_of(group) for group in range(quad)], axis=0)
+    preact = jnp.dot(rows_of(me), weight_ref[...], preferred_element_type=F32) + bias_ref[...]
     act_ref[...] = (preact * jax.nn.sigmoid(preact)).astype(BF16)
-    lanes = pl.ds(pl.multiple_of(me * LANES, LANES), LANES)
+    lanes = lanes_of(quarter_of(me, flip))
     preact = jnp.dot(aggregated, weight_ref[:, lanes], preferred_element_type=F32) + bias_ref[:, lanes]
     sigmoid_part = jax.nn.sigmoid(preact)
-    cot = jnp.concatenate([quarters_ref[group, nodes : 2 * nodes] for group in range(quad)], axis=0)
+    cot = jnp.concatenate([shares_ref[group, quad] for group in range(quad)], axis=0)
     grad = cot.astype(F32) * sigmoid_part * (1.0 + preact * (1.0 - sigmoid_part))
     product = lax.dot_general(
         aggregated, grad.astype(BF16), (((0,), (0,)), ((), ())), preferred_element_type=F32
@@ -153,10 +186,11 @@
         out_ref[copy, n_chunks * depth :] = given_ref[0, depth:]
 
 
-def last_kernel(parts_ref, weight_ref, bias_ref):
+def last_kernel(place_ref, parts_ref, weight_ref, bias_ref):
     width = weight_ref.shape[0]
-    for part in range(parts_ref.shape[0]):
-        lanes = slice(part * LANES, (part + 1) * LANES)
+    for quarter in range(parts_ref.shape[0]):
+        part = quarter_of(quarter, place_ref[3])
+        lanes = slice(quarter * LANES, (quarter + 1) * LANES)
         weight_ref[:, lanes] = parts_ref[part, :width].astype(F32)
         side = parts_ref[part, width:].astype(F32)
         bias_ref[:, lanes] = side[0:1] + side[1:2]
@@ -179,27 +213,33 @@
 ):
     nodes, width = features.shape
     _, _, slots, size, _ = tile_values.shape
-    n_z, n_x = lax.axis_size("z_lo"), lax.axis_size("x")
-    n_pair = lax.axis_size("y_pair")
-    tiles = tile_values[0, 0]
-    ints = [tile_rows[0, 0], tile_cols[0, 0], jnp.broadcast_to(tile_count[0], (slots,))]
-    side = jnp.pad(jnp.stack(ints), ((0, SIDE - 3), (0, LANES - slots))).astype(BF16)
-    quarters = call(
-        quarter_kernel, ((4, 2 * nodes + SIDE, LANES), BF16), features, cotangent, side
-    )
-    quarters = lax.all_to_all(quarters, QUAD, 0, 0)
-    quarters, tiles = lax.optimization_barrier((quarters, tiles))
+    n_x, n_pair = lax.axis_size("x"), lax.axis_size("y_pair")
+    places = [lax.axis_index(axis) for axis in QUAD + ("z_hi",)]
+    places.append(lax.axis_index("y_pair") // (n_pair // 2))
+    place = jnp.stack(places).astype(jnp.int32)
+    n_first = lax.axis_size(FIRST)
+    quarters = pl.pallas_call(
+        quarter_kernel,
+        out_shape=jax.ShapeDtypeStruct((n_first, nodes + SIDE, LANES), BF16),
+        in_specs=[SMEM] * 4 + [HBM],
+        out_specs=HBM,
+        scratch_shapes=[pltpu.VMEM((SIDE, LANES), BF16), pltpu.SemaphoreType.DMA((2, n_first))],
+        compiler_params=PARAMS,
+    )(place, tile_rows[0, 0], tile_cols[0, 0], tile_count[0], features)
+    quarters = lax.all_to_all(quarters, FIRST, 0, 0)
+    quarters, tiles = lax.optimization_barrier((quarters, tile_values[0, 0]))
     tiles_y = swap(tiles, "y_odd")
     tiles_core = swap(tiles, "core")
     tiles_both = swap(tiles_y, "core")
-    meta = quarters[:, 2 * nodes : 2 * nodes + 3, :slots].astype(jnp.int32)
-    near = lax.all_gather(quarters[:, :nodes], "z_lo", axis=0)
+    quarters = quarters.reshape(-1, 4, nodes + SIDE, LANES)
+    meta = lax.dynamic_index_in_dim(quarters, lax.axis_index("z_lo"), 0, keepdims=False)
+    meta = meta[:, nodes : nodes + 3, :slots].astype(jnp.int32)
+    near = quarters[:, :, :nodes]
     blocks = lax.all_to_all(jnp.broadcast_to(near[None], (n_x,) + near.shape), "x", 0, 0)
-    place = jnp.stack([lax.axis_index(axis) for axis in QUAD + ("z_hi",)]).astype(jnp.int32)
     term = pl.pallas_call(
         tile_kernel,
         out_shape=jax.ShapeDtypeStruct((n_pair, 2, 2, size, LANES), BF16),
-        in_specs=[SMEM, SMEM] + [ANY] * 4 + [VMEM],
+        in_specs=[SMEM, SMEM] + [HBM] * 4 + [VMEM],
         out_specs=VMEM,
         scratch_shapes=[
             pltpu.VMEM((4, slots, size, size), BF16),
@@ -208,32 +248,45 @@
         ],
         compiler_params=PARAMS,
     )(place, meta, tiles, tiles_y, tiles_core, tiles_both, blocks)
-    shares = lax.all_to_all(term, "y_pair", 0, 0)
-    block = (2, size, LANES)
-    keep, send = call(pair_kernel, ((block, F32), (block, BF16)), place, shares, scalars=1)
-    shares = call(spread_kernel, ((4,) + block, BF16), keep, swap(send, "z_hi"))
-    shares = lax.all_to_all(shares.reshape(4, 4, nodes, LANES), QUAD, 0, 0)
-    n_plane, n_depth = lax.axis_size(PLANE), lax.axis_size(DEPTH)
+    shares = lax.all_to_all(term, Y, 0, 0, axis_index_groups=ROLES)
+    block = (4, nodes, LANES)
+    keep, send = call(
+        pair_kernel,
+        ((block, F32), (block, BF16)),
+        place,
+        shares.reshape((n_pair, 2) + block),
+        scalars=1,
+    )
+    shares = call(
+        spread_kernel,
+        ((4, 5, nodes, LANES), BF16),
+        place,
+        keep,
+        swap(send, "z_hi"),
+        cotangent,
+        scalars=1,
+    )
+    shares = lax.all_to_all(shares, QUAD, 0, 0)
+    n_plane, n_depth = len(PLANE_ROLES[0]), lax.axis_size(DEPTH)
     chunk = (width // n_plane + SIDE, LANES)
     activations, grads = call(
         node_kernel,
         (((nodes, width), BF16), ((n_plane,) + chunk, BF16)),
         place,
         shares,
-        quarters,
         weight,
         bias_term[None, :],
         scalars=1,
     )
-    grads = lax.all_to_all(grads, PLANE, 0, 0)
+    grads = lax.all_to_all(grads, PLANE, 0, 0, axis_index_groups=PLANE_ROLES)
     grads = call(sum_kernel, ((n_depth,) + chunk, BF16), grads)
     grads = lax.all_to_all(grads, DEPTH, 0, 0)
     grads = call(sum_kernel, ((n_plane,) + chunk, BF16), grads)
-    grads = lax.all_to_all(grads, PLANE, 0, 0)
+    grads = lax.all_to_all(grads, PLANE, 0, 0, axis_index_groups=PLANE_ROLES)
     grads = call(copy_kernel, ((4, width + SIDE, LANES), BF16), grads)
     grads = lax.all_to_all(grads, QUAD, 0, 0)
     weight_grad, bias_grad = call(
-        last_kernel, (((width, width), F32), ((1, width), F32)), grads
+        last_kernel, (((width, width), F32), ((1, width), F32)), place, grads, scalars=1
     )
     return activations, weight_grad, bias_grad[0]
 

time: 186 us -> 200 us (1.075)
  waiting for transfers between devices: 16.6 us -> 31.7 us
  blocking collectives: 132 us -> 127 us
  Pallas kernels: 8.18 us -> 10.8 us
    ppermute x4, waiting for transfers between devices: 13.1 us -> 31.7 us  [swap(): return lax.ppermute(array, axis, [(0, 1), (1, 0)])]
    all_gather x1 -> x0, blocking collectives: 12.2 us -> none  [per_device(): near = lax.all_gather(quarters[:, :nodes], 'z_lo', axis=0)]
    all_to_all x5, blocking collectives: 91.8 us -> 96.2 us  [the longest x1 33.2 us: per_device(): shares = lax.all_to_all(term, Y, 0, 0, axis_index_groups=ROLES)]
    all_to_all x1, waiting for transfers between devices: 3.53 us -> 0.01 us  [per_device(): lax.all_to_all(jnp.broadcast_to(near[None], (n_x,) + near.shape), 'x', 0, 0)]
    pallas_call x8 -> x7, Pallas kernels: 3.69 us -> 4.74 us  [call(): pl.pallas_call(kernel, out_shape=shapes, in_specs=[SMEM] * scalars + [VME...]
where the time goes in v6:
time: 200 us; the launch traced here: 199 us
  blocking collectives  127 us (64%)
  waiting for transfers between devices  31.7 us (16%)
  starting transfers between devices  22.5 us (11%)
  Pallas kernels  10.8 us (5%)
  local copies, waits for them, and re-layouts  5.05 us (3%)
    all_to_all x1, blocking collectives, per_device(): shares = lax.all_to_all(term, Y, 0, 0, axis_index_groups=ROLES)  33.2 us
    ppermute x4, waiting for transfers between devices, swap(): return lax.ppermute(array, axis, [(0, 1), (1, 0)])  31.7 us
    all_to_all x1, blocking collectives, per_device(): quarters = lax.all_to_all(quarters, FIRST, 0, 0)  25.9 us
    all_to_all x2, blocking collectives, per_device(): grads = lax.all_to_all(grads, PLANE, 0, 0, axis_index_groups=PLANE_ROLES)  24.9 us
    ppermute x4, starting transfers between devices, swap(): return lax.ppermute(array, axis, [(0, 1), (1, 0)])  18.5 us
    all_to_all x1, blocking collectives, per_device(): grads = lax.all_to_all(grads, QUAD, 0, 0)  17.1 us
    all_to_all x1, blocking collectives, per_device(): grads = lax.all_to_all(grads, DEPTH, 0, 0)  14 us
    all_to_all x1, blocking collectives, per_device(): shares = lax.all_to_all(shares, QUAD, 0, 0)  12.3 us
  transfers between devices with their start and end apart: 5, of which 3 were waited for; matrix products, arithmetic and copies ran while one was open for 1% of the time, Pallas kernels for 0%

profile of v6, /device:TPU:1, one launch (start us, length us, event | category | flops | bytes accessed | tf_op | source)
XLA Modules:
  0.0 199.0 jit_solution(3613464167208292785)
XLA Ops:
  0.6 0.0 copy-start
  1.4 0.1 pad_add_fusion.place_ref
  1.5 0.0 copy-start.3
  1.5 0.9 copy-done.3
  2.4 0.0 copy-start.5
  2.4 0.7 copy-done.5
  3.1 0.0 copy-start.6
  3.1 0.7 copy-done.6
  3.7 1.2 shard_map.103
  5.0 25.9 %all_to_all.40 = bf16[16,144,128]{2,1,0:T(8,128)(2,1)S(1)} all-to-all(bf16[16,144,128]{2,1,0:T(8,128)(2,1)S(1)} %shard_map.103), channel_id=1, replica_groups=mesh['z_lo'=4,'x'=4,'core'=2,'z_hi'=2,'y_pair'=4,'y_odd'=2] {'z_lo','cor..., dimensions={0} | all-to-all | bytes 1179648 | tf_op jit(solution)/shard_map/all_to_all | solution.py:229
  30.8 0.0 copy-start.7
  30.8 0.0 copy-done
  30.8 3.1 %collective-permute-start = (bf16[11,256,256]{2,1,0:T(8,128)(2,1)S(1)}, bf16[11,256,256]{2,1,0:T(8,128)(2,1)}, u32[]{:S(2)}, u32[]{:S(2)}) collective-permute-start(bf16[11,256,256]{2,1,0:T(8,128)(2,1)S(1)} %bitcast.16), channel_id=1, source_target_pairs={{0,1},{1,0},{2,3},{3,2},{4,5},{5,4},{6,7},{7,6},{8,9},{9,8},{10,11... | collective-permute-start | bytes 4325384 | tf_op jit(solution)/shard_map/ppermute | solution.py:208
  33.9 0.0 copy-done.7
  34.0 1.8 broadcast_in_dim.4
  35.8 4.0 %all-to-all-start.1 = ((bf16[4,4,4,128,128]{4,3,2,1,0:T(8,128)(2,1)}), bf16[4,4,4,128,128]{4,3,2,1,0:T(8,128)(2,1)S(1)}, u32[]{:S(2)}, u32[]{:S(2)}) async-start(bf16[4,4,4,128,128]{4,3,2,1,0:T(8,128)(2,1)} %broadcast_in_dim.4), calls=%async_computation.1 | async-start | bytes 4194304 | tf_op jit(solution)/shard_map/all_to_all | solution.py:238
  39.8 2.9 %collective-permute-start.1 = (bf16[11,256,256]{2,1,0:T(8,128)(2,1)S(1)}, bf16[11,256,256]{2,1,0:T(8,128)(2,1)}, u32[]{:S(2)}, u32[]{:S(2)}) collective-permute-start(bf16[11,256,256]{2,1,0:T(8,128)(2,1)S(1)} %bitcast.17), channel_id=1, source_target_pairs={{0,16},{16,0},{1,17},{17,1},{2,18},{18,2},{3,19},{19,3},{4,20},{20... | collective-permute-start | bytes 4325384 | tf_op jit(solution)/shard_map/ppermute | solution.py:208
  42.7 22.9 %collective-permute-done.refs_1_ = bf16[11,256,256]{2,1,0:T(8,128)(2,1)} collective-permute-done((bf16[11,256,256]{2,1,0:T(8,128)(2,1)S(1)}, bf16[11,256,256]{2,1,0:T(8,128)(2,1)}, u32[]{:S(2)}, u32[]{:S(2)}) %collective-permute-start) | collective-permute-done | bytes 1441824 | tf_op jit(solution)/shard_map/ppermute | solution.py:208
  65.6 3.1 %collective-permute-start.2 = (bf16[11,256,256]{2,1,0:T(8,128)(2,1)}, bf16[11,256,256]{2,1,0:T(8,128)(2,1)}, u32[]{:S(2)}, u32[]{:S(2)}) collective-permute-start(bf16[11,256,256]{2,1,0:T(8,128)(2,1)} %collective-permute-done.refs_1_), channel_id=1, source_target_pairs={{0,16},{16,0},{1,17},{17,1},{2,18},{18,2},{3,19},{19,3},{4,20},{20... | collective-permute-start | bytes 4325384 | tf_op jit(solution)/shard_map/ppermute | solution.py:208
  68.7 0.9 dynamic-slice_bitcast_fusion
  69.7 0.0 collective-permute-done.1.refs_2_
  69.7 0.0 all-to-all-done.1.refs_4_
  69.7 2.2 %collective-permute-done.2.refs_3_ = bf16[11,256,256]{2,1,0:T(8,128)(2,1)} collective-permute-done((bf16[11,256,256]{2,1,0:T(8,128)(2,1)}, bf16[11,256,256]{2,1,0:T(8,128)(2,1)}, u32[]{:S(2)}, u32[]{:S(2)}) %collective-permute-start.2) | collective-permute-done | bytes 1441824 | tf_op jit(solution)/shard_map/ppermute | solution.py:208
  71.9 4.9 %shard_map.104 = bf16[4,2,2,256,128]{4,3,2,1,0:T(8,128)(2,1)S(1)} custom-call(s32[4]{0:T(128)S(1)} %pad_add_fusion.place_ref, s32[4,3,11]{2,1,0:T(4,128)S(1)} %slice_convert_fusion.meta_ref, bf16[11,256,256]{2,1,0:T(8,128)(2,1)S(1)} %bitcast.18, bf16[11,256,256]{2,1,0:T(8,128)(2,1)} %collective-permute-done.refs_1_, ...), custom_call_target="tpu_custom_call" | custom-call | tf_op jit(solution)/shard_map/pallas_call | solution.py:239
  76.7 0.0 copy-start.2
  76.8 33.2 %all_to_all.41 = bf16[4,2,2,256,128]{4,3,2,1,0:T(8,128)(2,1)S(1)} all-to-all(bf16[4,2,2,256,128]{4,3,2,1,0:T(8,128)(2,1)S(1)} %shard_map.104), channel_id=1, replica_groups={{0,2,5,7},{1,3,4,6},{8,10,13,15},{9,11,12,14},{16,18,21,23},{17,19,20,2..., dimensions={0} | all-to-all | bytes 2097152 | tf_op jit(solution)/shard_map/all_to_all | solution.py:251
  109.9 0.7 shard_map.105
  110.6 0.0 copy-start.1
  110.6 0.0 copy-start.4
  110.6 9.4 %collective-permute-start.3 = (bf16[4,128,128]{2,1,0:T(8,128)(2,1)S(1)}, bf16[4,128,128]{2,1,0:T(8,128)(2,1)S(1)}, u32[]{:S(2)}, u32[]{:S(2)}) collective-permute-start(bf16[4,128,128]{2,1,0:T(8,128)(2,1)S(1)} %get-tuple-element.14), channel_id=1, source_target_pairs={{0,8},{8,0},{1,9},{9,1},{2,10},{10,2},{3,11},{11,3},{4,12},{12,4},... | collective-permute-start | bytes 393224 | tf_op jit(solution)/shard_map/ppermute | solution.py:208
  120.1 6.6 %collective-permute-done.3.given_ref = bf16[4,128,128]{2,1,0:T(8,128)(2,1)S(1)} collective-permute-done((bf16[4,128,128]{2,1,0:T(8,128)(2,1)S(1)}, bf16[4,128,128]{2,1,0:T(8,128)(2,1)S(1)}, u32[]{:S(2)}, u32[]{:S(2)}) %collective-permute-start.3) | collective-permute-done | bytes 131104 | tf_op jit(solution)/shard_map/ppermute | solution.py:208
  126.6 0.0 copy-done.2
  126.7 0.6 shard_map.106
  127.3 12.3 %all_to_all.42.shares_ref = bf16[4,5,128,128]{3,2,1,0:T(8,128)(2,1)S(1)} all-to-all(bf16[4,5,128,128]{3,2,1,0:T(8,128)(2,1)S(1)} %shard_map.106), channel_id=1, replica_groups=mesh['z_lo'=4,'x'=4,'core'=2,'z_hi'=2,'y_pair'=4,'y_odd'=2] {'core','y_o..., dimensions={0} | all-to-all | bytes 1310720 | tf_op jit(solution)/shard_map/all_to_all | solution.py:269
  139.5 0.0 copy-done.1
  139.5 0.0 copy-done.4
  139.5 1.7 shard_map.107
  141.2 13.6 %all_to_all.43.parts_ref = bf16[16,48,128]{2,1,0:T(8,128)(2,1)S(1)} all-to-all(bf16[16,48,128]{2,1,0:T(8,128)(2,1)S(1)} %get-tuple-element.16), channel_id=1, replica_groups={{0,2,5,7,32,34,37,39,64,66,69,71,96,98,101,103},{1,3,4,6,33,35,36,38,65..., dimensions={0} | all-to-all | bytes 393216 | tf_op jit(solution)/shard_map/all_to_all | solution.py:281
  154.9 14.0 %all_to_all.44.parts_ref = bf16[8,48,128]{2,1,0:T(8,128)(2,1)S(1)} all-to-all(bf16[8,48,128]{2,1,0:T(8,128)(2,1)S(1)} %shard_map.108), channel_id=1, replica_groups=mesh['z_lo'=4,'x'=4,'core'=2,'z_hi'=2,'y_pair'=4,'y_odd'=2] {'z_lo','z_hi'}, dimensions={0} | all-to-all | bytes 196608 | tf_op jit(solution)/shard_map/all_to_all | solution.py:283
  168.9 11.3 %all_to_all.45.given_ref = bf16[16,48,128]{2,1,0:T(8,128)(2,1)S(1)} all-to-all(bf16[16,48,128]{2,1,0:T(8,128)(2,1)S(1)} %shard_map.109), channel_id=1, replica_groups={{0,2,5,7,32,34,37,39,64,66,69,71,96,98,101,103},{1,3,4,6,33,35,36,38,65..., dimensions={0} | all-to-all | bytes 393216 | tf_op jit(solution)/shard_map/all_to_all | solution.py:285
  180.2 0.1 shard_map.110
  180.2 17.1 %all_to_all.46.parts_ref = bf16[4,528,128]{2,1,0:T(8,128)(2,1)S(1)} all-to-all(bf16[4,528,128]{2,1,0:T(8,128)(2,1)S(1)} %shard_map.110), channel_id=1, replica_groups=mesh['z_lo'=4,'x'=4,'core'=2,'z_hi'=2,'y_pair'=4,'y_odd'=2] {'core','y_o..., dimensions={0} | all-to-all | bytes 1081344 | tf_op jit(solution)/shard_map/all_to_all | solution.py:287
  197.4 1.7 shard_map.111
  (4 shorter events, 0.1 us)
Async XLA Ops:
  0.6 30.2 %copy-start = (bf16[1,1,11,256,256]{4,3,2,1,0:T(8,128)(2,1)S(1)}, bf16[1,1,11,256,256]{4,3,2,1,0:T(8,128)(2,1)}, u32[]{:S(2)}) copy-start(bf16[1,1,11,256,256]{4,3,2,1,0:T(8,128)(2,1)} %param.12) | copy-start | bytes 4325380
  1.5 0.9 copy-start.3
  2.4 0.7 copy-start.5
  3.1 0.7 copy-start.6
  30.8 3.1 %copy-start.7 = (bf16[16,144,128]{2,1,0:T(8,128)(2,1)}, bf16[16,144,128]{2,1,0:T(8,128)(2,1)S(1)}, u32[]{:S(2)}) copy-start(bf16[16,144,128]{2,1,0:T(8,128)(2,1)S(1)} %all_to_all.40) | copy-start | bytes 1769476
  30.8 34.8 %collective-permute-start = (bf16[11,256,256]{2,1,0:T(8,128)(2,1)S(1)}, bf16[11,256,256]{2,1,0:T(8,128)(2,1)}, u32[]{:S(2)}, u32[]{:S(2)}) collective-permute-start(bf16[11,256,256]{2,1,0:T(8,128)(2,1)S(1)} %bitcast.16), channel_id=1, source_target_pairs={{0,1},{1,0},{2,3},{3,2},{4,5},{5,4},{6,7},{7,6},{8,9},{9,8},{10,11... | collective-permute-start | bytes 4325384 | tf_op jit(solution)/shard_map/ppermute | solution.py:208
  35.8 33.9 %all-to-all-start.1 = ((bf16[4,4,4,128,128]{4,3,2,1,0:T(8,128)(2,1)}), bf16[4,4,4,128,128]{4,3,2,1,0:T(8,128)(2,1)S(1)}, u32[]{:S(2)}, u32[]{:S(2)}) async-start(bf16[4,4,4,128,128]{4,3,2,1,0:T(8,128)(2,1)} %broadcast_in_dim.4), calls=%async_computation.1 | async-start | bytes 4194304 | tf_op jit(solution)/shard_map/all_to_all | solution.py:238
  39.8 29.8 %collective-permute-start.1 = (bf16[11,256,256]{2,1,0:T(8,128)(2,1)S(1)}, bf16[11,256,256]{2,1,0:T(8,128)(2,1)}, u32[]{:S(2)}, u32[]{:S(2)}) collective-permute-start(bf16[11,256,256]{2,1,0:T(8,128)(2,1)S(1)} %bitcast.17), channel_id=1, source_target_pairs={{0,16},{16,0},{1,17},{17,1},{2,18},{18,2},{3,19},{19,3},{4,20},{20... | collective-permute-start | bytes 4325384 | tf_op jit(solution)/shard_map/ppermute | solution.py:208
  65.6 6.3 %collective-permute-start.2 = (bf16[11,256,256]{2,1,0:T(8,128)(2,1)}, bf16[11,256,256]{2,1,0:T(8,128)(2,1)}, u32[]{:S(2)}, u32[]{:S(2)}) collective-permute-start(bf16[11,256,256]{2,1,0:T(8,128)(2,1)} %collective-permute-done.refs_1_), channel_id=1, source_target_pairs={{0,16},{16,0},{1,17},{17,1},{2,18},{18,2},{3,19},{19,3},{4,20},{20... | collective-permute-start | bytes 4325384 | tf_op jit(solution)/shard_map/ppermute | solution.py:208
  76.7 49.9 %copy-start.2 = (bf16[128,512]{1,0:T(8,128)(2,1)S(1)}, bf16[128,512]{1,0:T(8,128)(2,1)}, u32[]{:S(2)}) copy-start(bf16[128,512]{1,0:T(8,128)(2,1)} %cot_ref.1) | copy-start | bytes 393220
  110.6 28.9 %copy-start.1 = (bf16[512,512]{1,0:T(8,128)(2,1)S(1)}, bf16[512,512]{1,0:T(8,128)(2,1)}, u32[]{:S(2)}) copy-start(bf16[512,512]{1,0:T(8,128)(2,1)} %weight_ref.1) | copy-start | bytes 1572868
  110.6 28.9 %copy-start.4 = (f32[512]{0:T(512)S(1)}, f32[512]{0:T(512)}, u32[]{:S(2)}) copy-start(f32[512]{0:T(512)} %param.10) | copy-start | bytes 6148
  110.6 16.0 %collective-permute-start.3 = (bf16[4,128,128]{2,1,0:T(8,128)(2,1)S(1)}, bf16[4,128,128]{2,1,0:T(8,128)(2,1)S(1)}, u32[]{:S(2)}, u32[]{:S(2)}) collective-permute-start(bf16[4,128,128]{2,1,0:T(8,128)(2,1)S(1)} %get-tuple-element.14), channel_id=1, source_target_pairs={{0,8},{8,0},{1,9},{9,1},{2,10},{10,2},{3,11},{11,3},{4,12},{12,4},... | collective-permute-start | bytes 393224 | tf_op jit(solution)/shard_map/ppermute | solution.py:208

commit v7 on v5

v7 whole, which is shorter than its diff:
```python
import jax
import jax.numpy as jnp
from jax import lax
from jax.experimental import pallas as pl
from jax.experimental.pallas import tpu as pltpu
from jax.sharding import Mesh, PartitionSpec as P

F32 = jnp.float32
BF16 = jnp.bfloat16
LANES = 128
VMEM = pl.BlockSpec(memory_space=pltpu.VMEM)
SMEM = pl.BlockSpec(memory_space=pltpu.SMEM)
HBM = pl.BlockSpec(memory_space=pltpu.HBM)
PARAMS = pltpu.CompilerParams(vmem_limit_bytes=40 * 1024 * 1024)
AXES = ("z_lo", "x", "core", "z_hi", "y_pair", "y_odd")
ROW = ("z_lo", "x", "core")
COL = ("z_hi", "y_pair", "y_odd")
QUAD = ("core", "y_odd")
PLANE = ("x", "y_pair")
DEPTH = ("z_lo", "z_hi", "core", "y_odd")
SIZES = (4, 4, 2, 2, 4, 2)
SIDE = 16
PAIR = 8


def lanes_of(part):
    return slice(part * LANES, (part + 1) * LANES)


def quarter_kernel(features_ref, side_ref, out_ref):
    nodes = features_ref.shape[0]
    for part in range(out_ref.shape[0]):
        out_ref[part, :nodes, :] = features_ref[:, lanes_of(part)]
        out_ref[part, nodes:, :] = side_ref[...]


def tile_kernel(place_ref, meta_ref, *refs):
    given, block_ref = refs[:4], refs[4]
    first_ref, keep_ref, send_ref, tiles, total, sems = refs[5:]
    _, slots, size, _ = tiles.shape
    n_x = block_ref.shape[0]
    core, odd = place_ref[0], place_ref[1]

    def tile_copy(which, slot):
        return pltpu.make_async_copy(
            given[which].at[slot], tiles.at[which, slot], sems.at[which, slot]
        )

    def cell_of(which):
        cell_core, cell_odd = (core + which // 2) % 2, (odd + which % 2) % 2
        return cell_core, cell_odd, cell_core * 2 + cell_odd

    for which in range(4):

        def fetch(slot, carry):
            tile_copy(which, slot).start()
            return carry

        lax.fori_loop(0, meta_ref[cell_of(which)[2], 2, 0], fetch, 0)
    total[...] = jnp.zeros_like(total)
    for which in range(4):
        cell_core, cell_odd, cell = cell_of(which)

        def step(slot, carry):
            tile_copy(which, slot).wait()
            chip = meta_ref[cell, 1, slot]
            z, x = chip // n_x, lax.rem(chip, n_x)
            window = jnp.concatenate(
                [block_ref[x, z, cell_odd], block_ref[x, z, 2 + cell_odd]], axis=0
            )
            total[cell_core, meta_ref[cell, 0, slot]] += jnp.dot(
                tiles[which, slot], window, preferred_element_type=F32
            )
            return carry

        lax.fori_loop(0, meta_ref[cell, 2, 0], step, 0)
    n_pair, mine = first_ref.shape[0], place_ref[2]
    for pair in range(n_pair):
        for high in range(2):
            first_ref[pair, high] = total[0, high * n_pair + pair].astype(BF16)
        keep_ref[pair] = total[1, mine * n_pair + pair]
        send_ref[pair] = total[1, (1 - mine) * n_pair + pair].astype(BF16)


def add(ref):
    total = ref[0].astype(F32)
    for part in range(1, ref.shape[0]):
        total = total + ref[part].astype(F32)
    return total


def pair_kernel(place_ref, parts_ref, keep_ref, send_ref):
    mine = place_ref[2]
    keep_ref[...] = add(parts_ref.at[:, mine])
    send_ref[...] = add(parts_ref.at[:, 1 - mine]).astype(BF16)


def join_kernel(keep_ref, given_ref, out_ref):
    out_ref[...] = (keep_ref[...] + given_ref[...].astype(F32)).astype(BF16)


def spread_kernel(keep_ref, given_ref, parts_ref, cot_ref, out_ref):
    nodes = cot_ref.shape[0]
    first = (keep_ref[...] + given_ref[...].astype(F32)).astype(BF16)
    second = add(parts_ref).astype(BF16)
    for part in range(out_ref.shape[0]):
        for half in range(2):
            out_ref[part, half] = first[half * nodes : (half + 1) * nodes]
            out_ref[part, 2 + half] = second[half * nodes : (half + 1) * nodes]
        out_ref[part, 4] = cot_ref[:, lanes_of(part)]


def split_rows(row):
    high = row.astype(BF16)
    low = (row - high.astype(F32)).astype(BF16)
    tall = (PAIR, row.shape[1])
    place = lax.broadcasted_iota(jnp.int32, tall, 0)
    high = jnp.broadcast_to(high.astype(F32), tall)
    low = jnp.broadcast_to(low.astype(F32), tall)
    return jnp.where(place == 0, high, jnp.where(place == 1, low, 0.0))


def node_kernel(place_ref, shares_ref, weight_ref, bias_ref, act_ref, grads_ref):
    quad = shares_ref.shape[0]
    me = place_ref[0] * 2 + place_ref[1]
    aggregated = jnp.concatenate(
        [
            jnp.concatenate([shares_ref[part, group] for part in range(quad)], axis=1)
            for group in range(quad)
        ],
        axis=0,
    )
    own = jnp.concatenate([shares_ref[part, me] for part in range(quad)], axis=1)
    preact = jnp.dot(own, weight_ref[...], preferred_element_type=F32) + bias_ref[...]
    act_ref[...] = (preact * jax.nn.sigmoid(preact)).astype(BF16)
    lanes = pl.ds(pl.multiple_of(me * LANES, LANES), LANES)
    preact = jnp.dot(aggregated, weight_ref[:, lanes], preferred_element_type=F32) + bias_ref[:, lanes]
    sigmoid_part = jax.nn.sigmoid(preact)
    cot = jnp.concatenate([shares_ref[group, quad] for group in range(quad)], axis=0)
    grad = cot.astype(F32) * sigmoid_part * (1.0 + preact * (1.0 - sigmoid_part))
    product = lax.dot_general(
        aggregated, grad.astype(BF16), (((0,), (0,)), ((), ())), preferred_element_type=F32
    ).astype(BF16)
    side = split_rows(jnp.sum(grad, axis=0, keepdims=True)).astype(BF16)
    n_chunks, tall, _ = grads_ref.shape
    depth = tall - PAIR
    for chunk in range(n_chunks):
        grads_ref[chunk, :depth] = product[chunk * depth : (chunk + 1) * depth]
        grads_ref[chunk, depth:] = side


def sum_kernel(parts_ref, out_ref):
    total = add(parts_ref)
    depth = total.shape[0] - PAIR
    main = total[:depth].astype(BF16)
    side = split_rows(total[depth : depth + 1] + total[depth + 1 : depth + 2]).astype(BF16)
    for copy in range(out_ref.shape[0]):
        out_ref[copy, :depth] = main
        out_ref[copy, depth:] = side


def depth_kernel(parts_ref, out_ref):
    n_z, quad, tall, lanes = parts_ref.shape
    depth = tall - PAIR
    place = lax.broadcasted_iota(jnp.int32, (PAIR, lanes), 0)
    side = jnp.zeros((PAIR, lanes), F32)
    mains = []
    for part in range(quad):
        total = parts_ref[0, part].astype(F32)
        for z in range(1, n_z):
            total = total + parts_ref[z, part].astype(F32)
        mains.append(total[:depth].astype(BF16))
        row = total[depth : depth + 1] + total[depth + 1 : depth + 2]
        high = row.astype(BF16).astype(F32)
        low = row - high
        high, low = (jnp.broadcast_to(part_row, side.shape) for part_row in (high, low))
        side = jnp.where(place == 2 * part, high, jnp.where(place == 2 * part + 1, low, side))
    side = side.astype(BF16)
    for copy in range(out_ref.shape[0]):
        for part in range(quad):
            out_ref[copy, part * depth : (part + 1) * depth] = mains[part]
        out_ref[copy, quad * depth :] = side


def last_kernel(parts_ref, weight_ref, bias_ref):
    n_chunks, tall, lanes = parts_ref.shape
    quad = weight_ref.shape[1] // lanes
    depth = (tall - PAIR) // quad
    for chunk in range(n_chunks):
        for part in range(quad):
            rows = slice(chunk * depth, (chunk + 1) * depth)
            weight_ref[rows, lanes_of(part)] = parts_ref[
                chunk, part * depth : (part + 1) * depth
            ].astype(F32)
    side = parts_ref[0, tall - PAIR :].astype(F32)
    for part in range(quad):
        bias_ref[:, lanes_of(part)] = side[2 * part : 2 * part + 1] + side[2 * part + 1 : 2 * part + 2]


def call(kernel, out, *args, scalars=0):
    shapes = jax.tree.map(lambda o: jax.ShapeDtypeStruct(*o), out, is_leaf=lambda o: isinstance(o[0], tuple) and not isinstance(o[1], tuple))
    specs = jax.tree.map(lambda o: VMEM, shapes)
    return pl.pallas_call(
        kernel, out_shape=shapes, in_specs=[SMEM] * scalars + [VMEM] * (len(args) - scalars), out_specs=specs, compiler_params=PARAMS
    )(*args)


def swap(array, axis):
    return lax.ppermute(array, axis, [(0, 1), (1, 0)])


def per_device(
    features, weight, bias_term, cotangent, tile_values, tile_rows, tile_cols, tile_count
):
    nodes, width = features.shape
    _, _, slots, size, _ = tile_values.shape
    n_z, n_x = lax.axis_size("z_lo"), lax.axis_size("x")
    n_pair = lax.axis_size("y_pair")
    tiles = tile_values[0, 0]
    ints = [tile_rows[0, 0], tile_cols[0, 0], jnp.broadcast_to(tile_count[0], (slots,))]
    side = jnp.pad(jnp.stack(ints), ((0, SIDE - 3), (0, LANES - slots))).astype(BF16)
    quarters = call(quarter_kernel, ((4, nodes + SIDE, LANES), BF16), features, side)
    quarters = lax.all_to_all(quarters, QUAD, 0, 0)
    quarters, tiles = lax.optimization_barrier((quarters, tiles))
    tiles_y = swap(tiles, "y_odd")
    tiles_core = swap(tiles, "core")
    tiles_both = swap(tiles_y, "core")
    meta = quarters[:, nodes : nodes + 3, :slots].astype(jnp.int32)
    near = lax.all_gather(quarters[:, :nodes], "z_lo", axis=0)
    blocks = lax.all_to_all(jnp.broadcast_to(near[None], (n_x,) + near.shape), "x", 0, 0)
    place = jnp.stack([lax.axis_index(axis) for axis in QUAD + ("z_hi",)]).astype(jnp.int32)
    block = (size, LANES)
    first, keep, send = pl.pallas_call(
        tile_kernel,
        out_shape=(
            jax.ShapeDtypeStruct((n_pair, 2) + block, BF16),
            jax.ShapeDtypeStruct((n_pair,) + block, F32),
            jax.ShapeDtypeStruct((n_pair,) + block, BF16),
        ),
        in_specs=[SMEM, SMEM] + [HBM] * 4 + [VMEM],
        out_specs=(VMEM, VMEM, VMEM),
        scratch_shapes=[
            pltpu.VMEM((4, slots, size, size), BF16),
            pltpu.VMEM((2, 2 * n_pair) + block, F32),
            pltpu.SemaphoreType.DMA((4, slots)),
        ],
        compiler_params=PARAMS,
    )(place, meta, tiles, tiles_y, tiles_core, tiles_both, blocks)
    first = lax.all_to_all(first, "y_pair", 0, 0)
    second = call(join_kernel, ((n_pair,) + block, BF16), keep, swap(send, "z_hi"))
    second = lax.all_to_all(second, "y_pair", 0, 0)
    keep, send = call(pair_kernel, ((block, F32), (block, BF16)), place, first, scalars=1)
    shares = call(
        spread_kernel, ((4, 5, nodes, LANES), BF16), keep, swap(send, "z_hi"), second, cotangent
    )
    shares = lax.all_to_all(shares, QUAD, 0, 0)
    n_plane, n_depth = lax.axis_size(PLANE), lax.axis_size(DEPTH)
    depth = width // n_plane
    activations, grads = call(
        node_kernel,
        (((nodes, width), BF16), ((n_plane, depth + PAIR, LANES), BF16)),
        place,
        shares,
        weight,
        bias_term[None, :],
        scalars=1,
    )
    grads = lax.all_to_all(grads, PLANE, 0, 0)
    grads = call(sum_kernel, ((n_depth, depth + PAIR, LANES), BF16), grads)
    grads = lax.all_to_all(grads, DEPTH, 0, 0).reshape(-1, 4, depth + PAIR, LANES)
    grads = call(depth_kernel, ((n_plane, 4 * depth + PAIR, LANES), BF16), grads)
    grads = lax.all_to_all(grads, PLANE, 0, 0)
    weight_grad, bias_grad = call(
        last_kernel, (((width, width), F32), ((1, width), F32)), grads
    )
    return activations, weight_grad, bias_grad[0]


def solution(mesh):
    cut = Mesh(mesh.devices.reshape(SIZES), AXES)
    everywhere = P(AXES, None)
    return jax.shard_map(
        per_device,
        mesh=cut,
        in_specs=(
            everywhere,
            P(),
            P(),
            everywhere,
            P(ROW, COL, None, None, None),
            P(ROW, COL, None),
            P(ROW, COL, None),
            P(ROW, COL),
        ),
        out_specs=(everywhere, P(), P()),
        check_vma=False,
    )
```

time: 186 us -> 191 us (1.027)
  the two profiles are of different devices: /device:TPU:1 before, /device:TPU:64 now
where the time goes in v7:
time: 191 us; the launch traced here: 190 us
  blocking collectives  101 us (53%)
  starting transfers between devices  40.9 us (21%)
  waiting for transfers between devices  29.6 us (15%)
  Pallas kernels  9.19 us (5%)
  local copies, waits for them, and re-layouts  6.25 us (3%)
    all_to_all x2, blocking collectives, per_device(): grads = lax.all_to_all(grads, PLANE, 0, 0)  42.3 us
    all_to_all x1, blocking collectives, per_device(): lax.all_to_all(grads, DEPTH, 0, 0).reshape(-1, 4, depth + PAIR, LANES)  21.5 us
    ppermute x5, starting transfers between devices, swap(): return lax.ppermute(array, axis, [(0, 1), (1, 0)])  21.4 us
    all_gather x1, blocking collectives, per_device(): near = lax.all_gather(quarters[:, :nodes], 'z_lo', axis=0)  16.8 us
    ppermute x5, waiting for transfers between devices, swap(): return lax.ppermute(array, axis, [(0, 1), (1, 0)])  16.7 us
    all_to_all x1, blocking collectives, per_device(): shares = lax.all_to_all(shares, QUAD, 0, 0)  12.7 us
    all_to_all x1, waiting for transfers between devices, per_device(): lax.all_to_all(jnp.broadcast_to(near[None], (n_x,) + near.shape), 'x', 0, 0)  11.7 us
    all_to_all x1, blocking collectives, per_device(): quarters = lax.all_to_all(quarters, QUAD, 0, 0)  7.45 us
  transfers between devices with their start and end apart: 8, of which 5 were waited for; matrix products, arithmetic and copies ran while one was open for 1% of the time, Pallas kernels for 1%

profile of v7, /device:TPU:64, one launch (start us, length us, event | category | flops | bytes accessed | tf_op | source)
XLA Modules:
  0.0 189.7 jit_solution(14738936983546803018)
XLA Ops:
  1.3 0.1 pad.8.clone
  1.4 0.7 convert_bitcast_fusion
  2.0 0.1 maximum_maximum_fusion
  2.1 0.0 copy-start.6
  2.1 0.9 copy-done.6
  3.0 7.5 %all_to_all.40 = bf16[4,144,128]{2,1,0:T(8,128)(2,1)S(1)} all-to-all(bf16[4,144,128]{2,1,0:T(8,128)(2,1)S(1)} %shard_map.103), channel_id=1, replica_groups=mesh['z_lo'=4,'x'=4,'core'=2,'z_hi'=2,'y_pair'=4,'y_odd'=2] {'core','y_o..., dimensions={0} | all-to-all | bytes 294912 | tf_op jit(solution)/shard_map/all_to_all | solution.py:223
  10.5 0.0 copy-start.9
  10.5 2.2 %collective-permute-start = (bf16[11,256,256]{2,1,0:T(8,128)(2,1)}, bf16[11,256,256]{2,1,0:T(8,128)(2,1)}, u32[]{:S(2)}, u32[]{:S(2)}) collective-permute-start(bf16[11,256,256]{2,1,0:T(8,128)(2,1)} %bitcast.15), channel_id=1, source_target_pairs={{0,1},{1,0},{2,3},{3,2},{4,5},{5,4},{6,7},{7,6},{8,9},{9,8},{10,11... | collective-permute-start | bytes 4325384 | tf_op jit(solution)/shard_map/ppermute | solution.py:209
  12.7 0.0 copy-done.9
  12.8 16.8 %all-gather = bf16[16,128,128]{2,1,0:T(8,128)(2,1)S(1)} all-gather(bf16[4,128,128]{2,1,0:T(8,128)(2,1)S(1)} %slice.7), channel_id=2, replica_groups=mesh['z_lo'=4,'x'=4,'core'=2,'z_hi'=2,'y_pair'=4,'y_odd'=2] {'z_lo'}, dimensions={0}, use_global_device_ids=true | all-gather | bytes 655360 | tf_op jit(solution)/shard_map/all_gather | solution.py:229
  29.6 1.9 %broadcast_in_dim.4 = bf16[4,4,4,128,128]{4,3,2,1,0:T(8,128)(2,1)} broadcast(bf16[4,4,128,128]{3,2,1,0:T(8,128)(2,1)S(1)} %bitcast.20), dimensions={1,2,3,4} | broadcast | bytes 2621440 | tf_op jit(solution)/shard_map/broadcast_in_dim | solution.py:230
  31.5 5.6 %all-to-all-start.1 = ((bf16[4,4,4,128,128]{4,3,2,1,0:T(8,128)(2,1)}), bf16[4,4,4,128,128]{4,3,2,1,0:T(8,128)(2,1)S(1)}, u32[]{:S(2)}, u32[]{:S(2)}) async-start(bf16[4,4,4,128,128]{4,3,2,1,0:T(8,128)(2,1)} %broadcast_in_dim.4), calls=%async_computation.1 | async-start | bytes 4194304 | tf_op jit(solution)/shard_map/all_to_all | solution.py:230
  37.2 0.0 copy-done
  37.2 1.9 %collective-permute-start.1 = (bf16[11,256,256]{2,1,0:T(8,128)(2,1)S(1)}, bf16[11,256,256]{2,1,0:T(8,128)(2,1)}, u32[]{:S(2)}, u32[]{:S(2)}) collective-permute-start(bf16[11,256,256]{2,1,0:T(8,128)(2,1)S(1)} %bitcast.16), channel_id=1, source_target_pairs={{0,16},{16,0},{1,17},{17,1},{2,18},{18,2},{3,19},{19,3},{4,20},{20... | collective-permute-start | bytes 4325384 | tf_op jit(solution)/shard_map/ppermute | solution.py:209
  39.1 7.1 %collective-permute-done.refs_1_ = bf16[11,256,256]{2,1,0:T(8,128)(2,1)} collective-permute-done((bf16[11,256,256]{2,1,0:T(8,128)(2,1)}, bf16[11,256,256]{2,1,0:T(8,128)(2,1)}, u32[]{:S(2)}, u32[]{:S(2)}) %collective-permute-start) | collective-permute-done | bytes 1441824 | tf_op jit(solution)/shard_map/ppermute | solution.py:209
  46.2 1.9 %collective-permute-start.2 = (bf16[11,256,256]{2,1,0:T(8,128)(2,1)}, bf16[11,256,256]{2,1,0:T(8,128)(2,1)}, u32[]{:S(2)}, u32[]{:S(2)}) collective-permute-start(bf16[11,256,256]{2,1,0:T(8,128)(2,1)} %collective-permute-done.refs_1_), channel_id=1, source_target_pairs={{0,16},{16,0},{1,17},{17,1},{2,18},{18,2},{3,19},{19,3},{4,20},{20... | collective-permute-start | bytes 4325384 | tf_op jit(solution)/shard_map/ppermute | solution.py:209
  48.2 0.1 pad_add_fusion.place_ref
  48.2 0.7 slice_convert_fusion.meta_ref
  48.9 0.0 collective-permute-done.1.refs_2_
  48.9 11.7 %all-to-all-done.1.refs_4_ = bf16[4,4,4,128,128]{4,3,2,1,0:T(8,128)(2,1)S(1)} async-done(((bf16[4,4,4,128,128]{4,3,2,1,0:T(8,128)(2,1)}), bf16[4,4,4,128,128]{4,3,2,1,0:T(8,128)(2,1)S(1)}, u32[]{:S(2)}, u32[]{:S(2)}) %all-to-all-start.1) | async-done | bytes 2097184 | tf_op jit(solution)/shard_map/all_to_all | solution.py:230
  60.6 0.0 collective-permute-done.2.refs_3_
  60.7 4.9 %shard_map.104 = (bf16[4,2,256,128]{3,2,1,0:T(8,128)(2,1)S(1)}, f32[4,256,128]{2,1,0:T(8,128)S(1)}, bf16[4,256,128]{2,1,0:T(8,128)(2,1)S(1)}) custom-call(s32[3]{0:T(128)S(1)} %pad_add_fusion.place_ref, s32[4,3,11]{2,1,0:T(4,128)S(1)} %slice_convert_fusion.meta_ref, bf16[11,256,256]{2,1,0:T(8,128)(2,1)S(1)} %bitcast.17, ...), custom_call_target="tpu_custom_call" | custom-call | tf_op jit(solution)/shard_map/pallas_call | solution.py:233
  65.6 0.0 copy-start.2
  65.6 0.8 copy-done.2
  66.4 0.8 copy-done.3
  67.2 0.7 copy-done.8
  67.9 6.6 %all-to-all-start.2 = ((bf16[4,2,256,128]{3,2,1,0:T(8,128)(2,1)}), bf16[4,2,256,128]{3,2,1,0:T(8,128)(2,1)S(1)}, u32[]{:S(2)}, u32[]{:S(2)}) async-start(bf16[4,2,256,128]{3,2,1,0:T(8,128)(2,1)} %copy-done.2), calls=%async_computation.2 | async-start | bytes 1048576 | tf_op jit(solution)/shard_map/all_to_all | solution.py:249
  74.5 8.0 %collective-permute-start.4 = (bf16[4,256,128]{2,1,0:T(8,128)(2,1)}, bf16[4,256,128]{2,1,0:T(8,128)(2,1)S(1)}, u32[]{:S(2)}, u32[]{:S(2)}) collective-permute-start(bf16[4,256,128]{2,1,0:T(8,128)(2,1)} %copy-done.8), channel_id=1, source_target_pairs={{0,8},{8,0},{1,9},{9,1},{2,10},{10,2},{3,11},{11,3},{4,12},{12,4},... | collective-permute-start | bytes 786440 | tf_op jit(solution)/shard_map/ppermute | solution.py:209
  82.5 7.4 %collective-permute-done.4.given_ref = bf16[4,256,128]{2,1,0:T(8,128)(2,1)S(1)} collective-permute-done((bf16[4,256,128]{2,1,0:T(8,128)(2,1)}, bf16[4,256,128]{2,1,0:T(8,128)(2,1)S(1)}, u32[]{:S(2)}, u32[]{:S(2)}) %collective-permute-start.4) | collective-permute-done | bytes 262176 | tf_op jit(solution)/shard_map/ppermute | solution.py:209
  89.9 1.0 copy-done.4
  90.9 0.7 shard_map.106
  91.7 0.0 all-to-all-done.2.parts_ref
  91.7 7.3 %all-to-all-start.3 = ((bf16[4,256,128]{2,1,0:T(8,128)(2,1)}), bf16[4,256,128]{2,1,0:T(8,128)(2,1)S(1)}, u32[]{:S(2)}, u32[]{:S(2)}) async-start(bf16[4,256,128]{2,1,0:T(8,128)(2,1)} %shard_map.106), calls=%async_computation.3 | async-start | bytes 524288 | tf_op jit(solution)/shard_map/all_to_all | solution.py:251
  99.0 0.6 shard_map.105
  99.6 7.3 %collective-permute-start.3 = (bf16[256,128]{1,0:T(8,128)(2,1)S(1)}, bf16[256,128]{1,0:T(8,128)(2,1)S(1)}, u32[]{:S(2)}, u32[]{:S(2)}) collective-permute-start(bf16[256,128]{1,0:T(8,128)(2,1)S(1)} %get-tuple-element.18), channel_id=1, source_target_pairs={{0,8},{8,0},{1,9},{9,1},{2,10},{10,2},{3,11},{11,3},{4,12},{12,4},... | collective-permute-start | bytes 196616 | tf_op jit(solution)/shard_map/ppermute | solution.py:209
  106.9 1.3 all-to-all-done.3.parts_ref
  108.2 2.1 %collective-permute-done.3.given_ref = bf16[256,128]{1,0:T(8,128)(2,1)S(1)} collective-permute-done((bf16[256,128]{1,0:T(8,128)(2,1)S(1)}, bf16[256,128]{1,0:T(8,128)(2,1)S(1)}, u32[]{:S(2)}, u32[]{:S(2)}) %collective-permute-start.3) | collective-permute-done | bytes 65568 | tf_op jit(solution)/shard_map/ppermute | solution.py:209
  110.3 0.0 copy-done.5
  110.3 0.1 shard_map.107
  110.4 12.7 %all_to_all.41.shares_ref = bf16[4,5,128,128]{3,2,1,0:T(8,128)(2,1)S(1)} all-to-all(bf16[4,5,128,128]{3,2,1,0:T(8,128)(2,1)S(1)} %shard_map.107), channel_id=1, replica_groups=mesh['z_lo'=4,'x'=4,'core'=2,'z_hi'=2,'y_pair'=4,'y_odd'=2] {'core','y_o..., dimensions={0} | all-to-all | bytes 1310720 | tf_op jit(solution)/shard_map/all_to_all | solution.py:256
  123.0 0.0 copy-done.1
  123.0 0.0 copy-done.7
  123.0 1.7 shard_map.108
  124.7 19.5 %all_to_all.42.parts_ref = bf16[16,40,128]{2,1,0:T(8,128)(2,1)S(1)} all-to-all(bf16[16,40,128]{2,1,0:T(8,128)(2,1)S(1)} %get-tuple-element.22), channel_id=1, replica_groups=mesh['z_lo'=4,'x'=4,'core'=2,'z_hi'=2,'y_pair'=4,'y_odd'=2] {'x','y_pair'}, dimensions={0} | all-to-all | bytes 327680 | tf_op jit(solution)/shard_map/all_to_all | solution.py:268
  144.3 21.5 %all_to_all.43 = bf16[32,40,128]{2,1,0:T(8,128)(2,1)S(1)} all-to-all(bf16[32,40,128]{2,1,0:T(8,128)(2,1)S(1)} %shard_map.109), channel_id=1, replica_groups=mesh['z_lo'=4,'x'=4,'core'=2,'z_hi'=2,'y_pair'=4,'y_odd'=2] {'z_lo','z_h..., dimensions={0} | all-to-all | bytes 655360 | tf_op jit(solution)/shard_map/all_to_all | solution.py:270
  165.8 0.1 shard_map.110
  165.9 22.8 %all_to_all.44.parts_ref = bf16[16,136,128]{2,1,0:T(8,128)(2,1)S(1)} all-to-all(bf16[16,136,128]{2,1,0:T(8,128)(2,1)S(1)} %shard_map.110), channel_id=1, replica_groups=mesh['z_lo'=4,'x'=4,'core'=2,'z_hi'=2,'y_pair'=4,'y_odd'=2] {'x','y_pair'}, dimensions={0} | all-to-all | bytes 1114112 | tf_op jit(solution)/shard_map/all_to_all | solution.py:272
  188.7 1.0 shard_map.111
  (11 shorter events, 0.1 us)
Async XLA Ops:
  2.1 0.9 copy-start.6
  10.5 2.2 %copy-start.9 = (bf16[4,144,128]{2,1,0:T(8,128)(2,1)}, bf16[4,144,128]{2,1,0:T(8,128)(2,1)S(1)}, u32[]{:S(2)}) copy-start(bf16[4,144,128]{2,1,0:T(8,128)(2,1)S(1)} %all_to_all.40) | copy-start | bytes 442372
  10.5 35.7 %collective-permute-start = (bf16[11,256,256]{2,1,0:T(8,128)(2,1)}, bf16[11,256,256]{2,1,0:T(8,128)(2,1)}, u32[]{:S(2)}, u32[]{:S(2)}) collective-permute-start(bf16[11,256,256]{2,1,0:T(8,128)(2,1)} %bitcast.15), channel_id=1, source_target_pairs={{0,1},{1,0},{2,3},{3,2},{4,5},{5,4},{6,7},{7,6},{8,9},{9,8},{10,11... | collective-permute-start | bytes 4325384 | tf_op jit(solution)/shard_map/ppermute | solution.py:209
  31.5 5.7 %copy-start = (bf16[1,1,11,256,256]{4,3,2,1,0:T(8,128)(2,1)S(1)}, bf16[1,1,11,256,256]{4,3,2,1,0:T(8,128)(2,1)}, u32[]{:S(2)}) copy-start(bf16[1,1,11,256,256]{4,3,2,1,0:T(8,128)(2,1)} %param.12) | copy-start | bytes 4325380
  31.5 29.1 %all-to-all-start.1 = ((bf16[4,4,4,128,128]{4,3,2,1,0:T(8,128)(2,1)}), bf16[4,4,4,128,128]{4,3,2,1,0:T(8,128)(2,1)S(1)}, u32[]{:S(2)}, u32[]{:S(2)}) async-start(bf16[4,4,4,128,128]{4,3,2,1,0:T(8,128)(2,1)} %broadcast_in_dim.4), calls=%async_computation.1 | async-start | bytes 4194304 | tf_op jit(solution)/shard_map/all_to_all | solution.py:230
  37.2 11.8 %collective-permute-start.1 = (bf16[11,256,256]{2,1,0:T(8,128)(2,1)S(1)}, bf16[11,256,256]{2,1,0:T(8,128)(2,1)}, u32[]{:S(2)}, u32[]{:S(2)}) collective-permute-start(bf16[11,256,256]{2,1,0:T(8,128)(2,1)S(1)} %bitcast.16), channel_id=1, source_target_pairs={{0,16},{16,0},{1,17},{17,1},{2,18},{18,2},{3,19},{19,3},{4,20},{20... | collective-permute-start | bytes 4325384 | tf_op jit(solution)/shard_map/ppermute | solution.py:209
  46.2 14.4 %collective-permute-start.2 = (bf16[11,256,256]{2,1,0:T(8,128)(2,1)}, bf16[11,256,256]{2,1,0:T(8,128)(2,1)}, u32[]{:S(2)}, u32[]{:S(2)}) collective-permute-start(bf16[11,256,256]{2,1,0:T(8,128)(2,1)} %collective-permute-done.refs_1_), channel_id=1, source_target_pairs={{0,16},{16,0},{1,17},{17,1},{2,18},{18,2},{3,19},{19,3},{4,20},{20... | collective-permute-start | bytes 4325384 | tf_op jit(solution)/shard_map/ppermute | solution.py:209
  65.6 0.8 copy-start.2
  66.4 0.8 copy-start.3
  67.2 0.7 copy-start.8
  67.9 42.4 %copy-start.5 = (bf16[128,512]{1,0:T(8,128)(2,1)S(1)}, bf16[128,512]{1,0:T(8,128)(2,1)}, u32[]{:S(2)}) copy-start(bf16[128,512]{1,0:T(8,128)(2,1)} %cot_ref.1) | copy-start | bytes 393220
  67.9 23.8 %all-to-all-start.2 = ((bf16[4,2,256,128]{3,2,1,0:T(8,128)(2,1)}), bf16[4,2,256,128]{3,2,1,0:T(8,128)(2,1)S(1)}, u32[]{:S(2)}, u32[]{:S(2)}) async-start(bf16[4,2,256,128]{3,2,1,0:T(8,128)(2,1)} %copy-done.2), calls=%async_computation.2 | async-start | bytes 1048576 | tf_op jit(solution)/shard_map/all_to_all | solution.py:249
  74.5 15.4 %collective-permute-start.4 = (bf16[4,256,128]{2,1,0:T(8,128)(2,1)}, bf16[4,256,128]{2,1,0:T(8,128)(2,1)S(1)}, u32[]{:S(2)}, u32[]{:S(2)}) collective-permute-start(bf16[4,256,128]{2,1,0:T(8,128)(2,1)} %copy-done.8), channel_id=1, source_target_pairs={{0,8},{8,0},{1,9},{9,1},{2,10},{10,2},{3,11},{11,3},{4,12},{12,4},... | collective-permute-start | bytes 786440 | tf_op jit(solution)/shard_map/ppermute | solution.py:209
  89.9 1.0 copy-start.4
  91.7 16.5 %all-to-all-start.3 = ((bf16[4,256,128]{2,1,0:T(8,128)(2,1)}), bf16[4,256,128]{2,1,0:T(8,128)(2,1)S(1)}, u32[]{:S(2)}, u32[]{:S(2)}) async-start(bf16[4,256,128]{2,1,0:T(8,128)(2,1)} %shard_map.106), calls=%async_computation.3 | async-start | bytes 524288 | tf_op jit(solution)/shard_map/all_to_all | solution.py:251
  99.0 24.1 %copy-start.1 = (bf16[512,512]{1,0:T(8,128)(2,1)S(1)}, bf16[512,512]{1,0:T(8,128)(2,1)}, u32[]{:S(2)}) copy-start(bf16[512,512]{1,0:T(8,128)(2,1)} %weight_ref.1) | copy-start | bytes 1572868
  99.0 24.1 %copy-start.7 = (f32[512]{0:T(512)S(1)}, f32[512]{0:T(512)}, u32[]{:S(2)}) copy-start(f32[512]{0:T(512)} %param.10) | copy-start | bytes 6148
  99.6 10.7 %collective-permute-start.3 = (bf16[256,128]{1,0:T(8,128)(2,1)S(1)}, bf16[256,128]{1,0:T(8,128)(2,1)S(1)}, u32[]{:S(2)}, u32[]{:S(2)}) collective-permute-start(bf16[256,128]{1,0:T(8,128)(2,1)S(1)} %get-tuple-element.18), channel_id=1, source_target_pairs={{0,8},{8,0},{1,9},{9,1},{2,10},{10,2},{3,11},{11,3},{4,12},{12,4},... | collective-permute-start | bytes 196616 | tf_op jit(solution)/shard_map/ppermute | solution.py:209

commit v8 on v4

v8 whole, which is shorter than its diff:
```python
import jax
import jax.numpy as jnp
from jax import lax
from jax.experimental import pallas as pl
from jax.experimental.pallas import tpu as pltpu
from jax.sharding import Mesh, PartitionSpec as P

F32 = jnp.float32
BF16 = jnp.bfloat16
LANES = 128
VMEM = pl.BlockSpec(memory_space=pltpu.VMEM)
SMEM = pl.BlockSpec(memory_space=pltpu.SMEM)
HBM = pl.BlockSpec(memory_space=pltpu.HBM)
PARAMS = pltpu.CompilerParams(vmem_limit_bytes=40 * 1024 * 1024)
AXES = ("z_lo", "x", "core", "z_hi", "y_pair", "y_odd")
ROW = ("z_lo", "x", "core")
COL = ("z_hi", "y_pair", "y_odd")
QUAD = ("core", "y_odd")
HOME = ("core", "z_hi", "y_pair", "y_odd")
NEAR = ("x", "core")
Y = ("y_pair", "y_odd")
Z = ("z_lo", "z_hi")
SIZES = (4, 4, 2, 2, 4, 2)
SIDE = 16
PAIR = 8


def lanes_of(part):
    return slice(part * LANES, (part + 1) * LANES)


def quarter_kernel(features_ref, side_ref, out_ref):
    nodes = features_ref.shape[0]
    for part in range(out_ref.shape[0]):
        out_ref[part, :nodes, :] = features_ref[:, lanes_of(part)]
        out_ref[part, nodes:, :] = side_ref[...]


def tile_kernel(place_ref, meta_ref, *refs):
    given, block_ref, out_ref, tiles, total, sems = refs[:4], refs[4], refs[5], refs[6], refs[7], refs[8]
    _, slots, size, _ = tiles.shape
    n_x = block_ref.shape[0]
    core, odd = place_ref[0], place_ref[1]

    def tile_copy(which, slot):
        return pltpu.make_async_copy(
            given[which].at[slot], tiles.at[which, slot], sems.at[which, slot]
        )

    def cell_of(which):
        cell_core, cell_odd = (core + which // 2) % 2, (odd + which % 2) % 2
        return cell_core, cell_odd, cell_core * 2 + cell_odd

    for which in range(4):

        def fetch(slot, carry):
            tile_copy(which, slot).start()
            return carry

        lax.fori_loop(0, meta_ref[cell_of(which)[2], 2, 0], fetch, 0)
    total[...] = jnp.zeros_like(total)
    for which in range(4):
        cell_core, cell_odd, cell = cell_of(which)

        def step(slot, carry):
            tile_copy(which, slot).wait()
            chip = meta_ref[cell, 1, slot]
            z, x = chip // n_x, lax.rem(chip, n_x)
            window = jnp.concatenate(
                [block_ref[x, z, cell_odd], block_ref[x, z, 2 + cell_odd]], axis=0
            )
            total[cell_core, meta_ref[cell, 0, slot]] += jnp.dot(
                tiles[which, slot], window, preferred_element_type=F32
            )
            return carry

        lax.fori_loop(0, meta_ref[cell, 2, 0], step, 0)
    out_ref[...] = total[...].astype(BF16)


def add(ref):
    total = ref[0].astype(F32)
    for part in range(1, ref.shape[0]):
        total = total + ref[part].astype(F32)
    return total


def with_bias(main, row):
    high = row.astype(BF16).astype(F32)
    tall = (PAIR, row.shape[1])
    place = lax.broadcasted_iota(jnp.int32, tall, 0)
    high, low = (jnp.broadcast_to(part, tall) for part in (high, row - high))
    side = jnp.where(place == 0, high, jnp.where(place == 1, low, 0.0))
    return jnp.concatenate([main, side], axis=0).astype(BF16)


def bias_of(total):
    depth = total.shape[0] - PAIR
    return total[depth : depth + 1] + total[depth + 1 : depth + 2]


def node_kernel(parts_ref, weight_ref, bias_ref, cot_ref, act_ref, grads_ref):
    n_high, n_odd = parts_ref.shape[1], parts_ref.shape[2]
    quarters = []
    for core in range(parts_ref.shape[0]):
        for odd in range(n_odd):
            total = parts_ref[core, 0, odd].astype(F32)
            for high in range(1, n_high):
                total = total + parts_ref[core, high, odd].astype(F32)
            quarters.append(total.astype(BF16))
    aggregated = jnp.concatenate(quarters, axis=1)
    preact = jnp.dot(aggregated, weight_ref[...], preferred_element_type=F32) + bias_ref[...]
    sigmoid_part = jax.nn.sigmoid(preact)
    act_ref[...] = (preact * sigmoid_part).astype(BF16)
    grad = cot_ref[...].astype(F32) * sigmoid_part * (1.0 + preact * (1.0 - sigmoid_part))
    product = lax.dot_general(
        aggregated, grad.astype(BF16), (((0,), (0,)), ((), ())), preferred_element_type=F32
    )
    row = jnp.sum(grad, axis=0, keepdims=True)
    depth = grads_ref.shape[1] - PAIR
    for chunk in range(grads_ref.shape[0]):
        grads_ref[chunk] = with_bias(product[chunk * depth : (chunk + 1) * depth], row)


def scatter_kernel(parts_ref, out_ref):
    total = add(parts_ref)
    depth = out_ref.shape[1] - PAIR
    for chunk in range(out_ref.shape[0]):
        out_ref[chunk] = with_bias(total[chunk * depth : (chunk + 1) * depth], bias_of(total))


def sum_kernel(parts_ref, out_ref):
    total = add(parts_ref)
    rounded = with_bias(total[: total.shape[0] - PAIR], bias_of(total))
    for copy in range(out_ref.shape[0]):
        out_ref[copy] = rounded


def copy_kernel(parts_ref, out_ref):
    depth = parts_ref.shape[1] - PAIR
    parts = [parts_ref[part].astype(F32) for part in range(parts_ref.shape[0])]
    rows = jnp.concatenate([part[:depth] for part in parts] + [parts[0][depth:]], axis=0).astype(BF16)
    for copy in range(out_ref.shape[0]):
        out_ref[copy] = rows


def last_kernel(parts_ref, weight_ref, bias_ref):
    depth = parts_ref.shape[1] - PAIR
    for chunk in range(parts_ref.shape[0]):
        rows = parts_ref[chunk].astype(F32)
        weight_ref[chunk * depth : (chunk + 1) * depth] = rows[:depth]
        if chunk == 0:
            bias_ref[...] = bias_of(rows)


def call(kernel, out, *args, scalars=0):
    shapes = jax.tree.map(lambda o: jax.ShapeDtypeStruct(*o), out, is_leaf=lambda o: isinstance(o[0], tuple) and not isinstance(o[1], tuple))
    specs = jax.tree.map(lambda o: VMEM, shapes)
    return pl.pallas_call(
        kernel, out_shape=shapes, in_specs=[SMEM] * scalars + [VMEM] * (len(args) - scalars), out_specs=specs, compiler_params=PARAMS
    )(*args)


def swap(array, axis):
    return lax.ppermute(array, axis, [(0, 1), (1, 0)])


def per_device(
    features, weight, bias_term, cotangent, tile_values, tile_rows, tile_cols, tile_count
):
    nodes, width = features.shape
    _, _, slots, size, _ = tile_values.shape
    n_z, n_x = lax.axis_size("z_lo"), lax.axis_size("x")
    n_pair = lax.axis_size("y_pair")
    tiles = tile_values[0, 0]
    ints = [tile_rows[0, 0], tile_cols[0, 0], jnp.broadcast_to(tile_count[0], (slots,))]
    side = jnp.pad(jnp.stack(ints), ((0, SIDE - 3), (0, LANES - slots))).astype(BF16)
    quarters = call(quarter_kernel, ((4, nodes + SIDE, LANES), BF16), features, side)
    quarters = lax.all_to_all(quarters, QUAD, 0, 0)
    quarters, tiles = lax.optimization_barrier((quarters, tiles))
    tiles_y = swap(tiles, "y_odd")
    tiles_core = swap(tiles, "core")
    tiles_both = swap(tiles_y, "core")
    meta = quarters[:, nodes : nodes + 3, :slots].astype(jnp.int32)
    near = lax.all_gather(quarters[:, :nodes], "z_lo", axis=0)
    blocks = lax.all_to_all(jnp.broadcast_to(near[None], (n_x,) + near.shape), "x", 0, 0)
    place = jnp.stack([lax.axis_index(axis) for axis in QUAD]).astype(jnp.int32)
    term = pl.pallas_call(
        tile_kernel,
        out_shape=jax.ShapeDtypeStruct((2, 2 * n_pair, size, LANES), BF16),
        in_specs=[SMEM, SMEM] + [HBM] * 4 + [VMEM],
        out_specs=VMEM,
        scratch_shapes=[
            pltpu.VMEM((4, slots, size, size), BF16),
            pltpu.VMEM((2, 2 * n_pair, size, LANES), F32),
            pltpu.SemaphoreType.DMA((4, slots)),
        ],
        compiler_params=PARAMS,
    )(place, meta, tiles, tiles_y, tiles_core, tiles_both, blocks)
    shares = lax.all_to_all(term.reshape(-1, nodes, LANES), HOME, 0, 0)
    n_near, n_y, n_deep = lax.axis_size(NEAR), lax.axis_size(Y), lax.axis_size(Z)
    depth = width // n_near
    tall, short = depth + PAIR, depth // n_y + PAIR
    activations, grads = call(
        node_kernel,
        (((nodes, width), BF16), ((n_near, tall, width), BF16)),
        shares.reshape(2, 2 * n_pair, 2, nodes, LANES),
        weight,
        bias_term[None, :],
        cotangent,
    )
    grads = lax.all_to_all(grads, NEAR, 0, 0)
    grads = call(scatter_kernel, ((n_y, short, width), BF16), grads)
    grads = lax.all_to_all(grads, Y, 0, 0)
    grads = call(sum_kernel, ((n_deep, short, width), BF16), grads)
    grads = lax.all_to_all(grads, Z, 0, 0)
    grads = call(sum_kernel, ((n_y, short, width), BF16), grads)
    grads = lax.all_to_all(grads, Y, 0, 0)
    grads = call(copy_kernel, ((n_near, tall, width), BF16), grads)
    grads = lax.all_to_all(grads, NEAR, 0, 0)
    weight_grad, bias_grad = call(
        last_kernel, (((width, width), F32), ((1, width), F32)), grads
    )
    return activations, weight_grad, bias_grad[0]


def solution(mesh):
    cut = Mesh(mesh.devices.reshape(SIZES), AXES)
    everywhere = P(AXES, None)
    return jax.shard_map(
        per_device,
        mesh=cut,
        in_specs=(
            everywhere,
            P(),
            P(),
            everywhere,
            P(ROW, COL, None, None, None),
            P(ROW, COL, None),
            P(ROW, COL, None),
            P(ROW, COL),
        ),
        out_specs=(everywhere, P(), P()),
        check_vma=False,
    )
```

time: 184 us -> 179 us (0.973)
  blocking collectives: 143 us -> 139 us
    all_to_all x7 -> x6, blocking collectives: 117 us -> 113 us  [the longest x1 50.1 us: per_device(): shares = lax.all_to_all(term.reshape(-1, nodes, LANES), HOME, 0, 0)]
where the time goes in v8:
time: 179 us; the launch traced here: 178 us
  blocking collectives  139 us (78%)
  starting transfers between devices  15.3 us (9%)
  waiting for transfers between devices  11.6 us (6%)
  Pallas kernels  6.19 us (3%)
  local copies, waits for them, and re-layouts  2.86 us (2%)
    all_to_all x1, blocking collectives, per_device(): shares = lax.all_to_all(term.reshape(-1, nodes, LANES), HOME, 0, 0)  50.1 us
    all_to_all x2, blocking collectives, per_device(): grads = lax.all_to_all(grads, NEAR, 0, 0)  31.5 us
    all_to_all x2, blocking collectives, per_device(): grads = lax.all_to_all(grads, Y, 0, 0)  22.3 us
    all_to_all x1, blocking collectives, per_device(): quarters = lax.all_to_all(quarters, QUAD, 0, 0)  13.6 us
    all_gather x1, blocking collectives, per_device(): near = lax.all_gather(quarters[:, :nodes], 'z_lo', axis=0)  12.2 us
    ppermute x3, starting transfers between devices, swap(): return lax.ppermute(array, axis, [(0, 1), (1, 0)])  11.6 us
    all_to_all x1, blocking collectives, per_device(): grads = lax.all_to_all(grads, Z, 0, 0)  9.65 us
    ppermute x3, waiting for transfers between devices, swap(): return lax.ppermute(array, axis, [(0, 1), (1, 0)])  8.67 us
  transfers between devices with their start and end apart: 4, of which 2 were waited for; matrix products, arithmetic and copies ran while one was open for 1% of the time, Pallas kernels for 0%

profile of v8, /device:TPU:1, one launch (start us, length us, event | category | flops | bytes accessed | tf_op | source)
XLA Modules:
  0.0 178.1 jit_solution(6358955816754356015)
XLA Ops:
  1.3 0.1 pad.8.clone
  1.4 0.7 convert_bitcast_fusion
  2.0 0.1 maximum_maximum_fusion
  2.1 0.0 copy-start.2
  2.1 0.9 copy-done.2
  3.0 13.6 %all_to_all.40 = bf16[4,144,128]{2,1,0:T(8,128)(2,1)S(1)} all-to-all(bf16[4,144,128]{2,1,0:T(8,128)(2,1)S(1)} %shard_map.103), channel_id=1, replica_groups=mesh['z_lo'=4,'x'=4,'core'=2,'z_hi'=2,'y_pair'=4,'y_odd'=2] {'core','y_o..., dimensions={0} | all-to-all | bytes 294912 | tf_op jit(solution)/shard_map/all_to_all | solution.py:179
  16.6 0.0 copy-start.5
  16.6 2.0 %collective-permute-start = (bf16[11,256,256]{2,1,0:T(8,128)(2,1)}, bf16[11,256,256]{2,1,0:T(8,128)(2,1)}, u32[]{:S(2)}, u32[]{:S(2)}) collective-permute-start(bf16[11,256,256]{2,1,0:T(8,128)(2,1)} %bitcast.17), channel_id=1, source_target_pairs={{0,1},{1,0},{2,3},{3,2},{4,5},{5,4},{6,7},{7,6},{8,9},{9,8},{10,11... | collective-permute-start | bytes 4325384 | tf_op jit(solution)/shard_map/ppermute | solution.py:165
  18.6 0.0 copy-done.5
  18.7 12.2 %all-gather = bf16[16,128,128]{2,1,0:T(8,128)(2,1)S(1)} all-gather(bf16[4,128,128]{2,1,0:T(8,128)(2,1)S(1)} %slice.7), channel_id=2, replica_groups=mesh['z_lo'=4,'x'=4,'core'=2,'z_hi'=2,'y_pair'=4,'y_odd'=2] {'z_lo'}, dimensions={0}, use_global_device_ids=true | all-gather | bytes 655360 | tf_op jit(solution)/shard_map/all_gather | solution.py:185
  30.9 1.8 %broadcast_in_dim.4 = bf16[4,4,4,128,128]{4,3,2,1,0:T(8,128)(2,1)} broadcast(bf16[4,4,128,128]{3,2,1,0:T(8,128)(2,1)S(1)} %bitcast.21), dimensions={1,2,3,4} | broadcast | bytes 2621440 | tf_op jit(solution)/shard_map/broadcast_in_dim | solution.py:186
  32.8 0.0 copy-start
  32.8 3.7 %all-to-all-start.1 = ((bf16[4,4,4,128,128]{4,3,2,1,0:T(8,128)(2,1)}), bf16[4,4,4,128,128]{4,3,2,1,0:T(8,128)(2,1)S(1)}, u32[]{:S(2)}, u32[]{:S(2)}) async-start(bf16[4,4,4,128,128]{4,3,2,1,0:T(8,128)(2,1)} %broadcast_in_dim.4), calls=%async_computation.1 | async-start | bytes 4194304 | tf_op jit(solution)/shard_map/all_to_all | solution.py:186
  36.5 0.0 copy-done
  36.5 6.3 %collective-permute-start.1 = (bf16[11,256,256]{2,1,0:T(8,128)(2,1)S(1)}, bf16[11,256,256]{2,1,0:T(8,128)(2,1)}, u32[]{:S(2)}, u32[]{:S(2)}) collective-permute-start(bf16[11,256,256]{2,1,0:T(8,128)(2,1)S(1)} %bitcast.18), channel_id=1, source_target_pairs={{0,16},{16,0},{1,17},{17,1},{2,18},{18,2},{3,19},{19,3},{4,20},{20... | collective-permute-start | bytes 4325384 | tf_op jit(solution)/shard_map/ppermute | solution.py:165
  42.8 8.7 %collective-permute-done.refs_1_ = bf16[11,256,256]{2,1,0:T(8,128)(2,1)} collective-permute-done((bf16[11,256,256]{2,1,0:T(8,128)(2,1)}, bf16[11,256,256]{2,1,0:T(8,128)(2,1)}, u32[]{:S(2)}, u32[]{:S(2)}) %collective-permute-start) | collective-permute-done | bytes 1441824 | tf_op jit(solution)/shard_map/ppermute | solution.py:165
  51.5 3.2 %collective-permute-start.2 = (bf16[11,256,256]{2,1,0:T(8,128)(2,1)}, bf16[11,256,256]{2,1,0:T(8,128)(2,1)}, u32[]{:S(2)}, u32[]{:S(2)}) collective-permute-start(bf16[11,256,256]{2,1,0:T(8,128)(2,1)} %collective-permute-done.refs_1_), channel_id=1, source_target_pairs={{0,16},{16,0},{1,17},{17,1},{2,18},{18,2},{3,19},{19,3},{4,20},{20... | collective-permute-start | bytes 4325384 | tf_op jit(solution)/shard_map/ppermute | solution.py:165
  54.7 0.1 pad_add_fusion.place_ref
  54.8 0.7 slice_convert_fusion.meta_ref
  55.5 0.0 collective-permute-done.1.refs_2_
  55.5 2.9 %all-to-all-done.1.refs_4_ = bf16[4,4,4,128,128]{4,3,2,1,0:T(8,128)(2,1)S(1)} async-done(((bf16[4,4,4,128,128]{4,3,2,1,0:T(8,128)(2,1)}), bf16[4,4,4,128,128]{4,3,2,1,0:T(8,128)(2,1)S(1)}, u32[]{:S(2)}, u32[]{:S(2)}) %all-to-all-start.1) | async-done | bytes 2097184 | tf_op jit(solution)/shard_map/all_to_all | solution.py:186
  58.4 0.0 collective-permute-done.2.refs_3_
  58.4 3.9 %shard_map.104 = bf16[2,8,256,128]{3,2,1,0:T(8,128)(2,1)S(1)} custom-call(s32[2]{0:T(128)S(1)} %pad_add_fusion.place_ref, s32[4,3,11]{2,1,0:T(4,128)S(1)} %slice_convert_fusion.meta_ref, bf16[11,256,256]{2,1,0:T(8,128)(2,1)S(1)} %bitcast.19, bf16[11,256,256]{2,1,0:T(8,128)(2,1)} %collective-permute-done.refs_1_, ...), custom_call_target="tpu_custom_call" | custom-call | tf_op jit(solution)/shard_map/pallas_call | solution.py:188
  62.4 0.0 copy-start.1
  62.4 0.0 copy-start.3
  62.4 0.0 copy-start.4
  62.4 50.1 %all_to_all.41 = bf16[32,128,128]{2,1,0:T(8,128)(2,1)S(1)} all-to-all(bf16[32,128,128]{2,1,0:T(8,128)(2,1)S(1)} %bitcast.16), channel_id=1, replica_groups=mesh['z_lo'=4,'x'=4,'core'=2,'z_hi'=2,'y_pair'=4,'y_odd'=2] {'core','z_h..., dimensions={0} | all-to-all | bytes 2097152 | tf_op jit(solution)/shard_map/all_to_all | solution.py:200
  112.5 0.0 copy-done.1
  112.5 0.0 copy-done.3
  112.5 0.0 copy-done.4
  112.5 1.0 shard_map.105
  113.5 13.5 %all_to_all.42.parts_ref = bf16[8,72,512]{2,1,0:T(8,128)(2,1)S(1)} all-to-all(bf16[8,72,512]{2,1,0:T(8,128)(2,1)S(1)} %get-tuple-element.12), channel_id=1, replica_groups=mesh['z_lo'=4,'x'=4,'core'=2,'z_hi'=2,'y_pair'=4,'y_odd'=2] {'x','core'}, dimensions={0} | all-to-all | bytes 1179648 | tf_op jit(solution)/shard_map/all_to_all | solution.py:212
  127.0 0.1 shard_map.106
  127.1 12.0 %all_to_all.43.parts_ref = bf16[8,16,512]{2,1,0:T(8,128)(2,1)S(1)} all-to-all(bf16[8,16,512]{2,1,0:T(8,128)(2,1)S(1)} %shard_map.106), channel_id=1, replica_groups=mesh['z_lo'=4,'x'=4,'core'=2,'z_hi'=2,'y_pair'=4,'y_odd'=2] {'y_pair','y..., dimensions={0} | all-to-all | bytes 262144 | tf_op jit(solution)/shard_map/all_to_all | solution.py:214
  139.1 9.6 %all_to_all.44.parts_ref = bf16[8,16,512]{2,1,0:T(8,128)(2,1)S(1)} all-to-all(bf16[8,16,512]{2,1,0:T(8,128)(2,1)S(1)} %shard_map.107), channel_id=1, replica_groups=mesh['z_lo'=4,'x'=4,'core'=2,'z_hi'=2,'y_pair'=4,'y_odd'=2] {'z_lo','z_hi'}, dimensions={0} | all-to-all | bytes 262144 | tf_op jit(solution)/shard_map/all_to_all | solution.py:216
  148.7 10.3 %all_to_all.45.parts_ref = bf16[8,16,512]{2,1,0:T(8,128)(2,1)S(1)} all-to-all(bf16[8,16,512]{2,1,0:T(8,128)(2,1)S(1)} %shard_map.108), channel_id=1, replica_groups=mesh['z_lo'=4,'x'=4,'core'=2,'z_hi'=2,'y_pair'=4,'y_odd'=2] {'y_pair','y..., dimensions={0} | all-to-all | bytes 262144 | tf_op jit(solution)/shard_map/all_to_all | solution.py:218
  159.1 18.0 %all_to_all.46.parts_ref = bf16[8,72,512]{2,1,0:T(8,128)(2,1)S(1)} all-to-all(bf16[8,72,512]{2,1,0:T(8,128)(2,1)S(1)} %shard_map.109), channel_id=1, replica_groups=mesh['z_lo'=4,'x'=4,'core'=2,'z_hi'=2,'y_pair'=4,'y_odd'=2] {'x','core'}, dimensions={0} | all-to-all | bytes 1179648 | tf_op jit(solution)/shard_map/all_to_all | solution.py:220
  177.1 1.0 shard_map.110
  (6 shorter events, 0.1 us)
Async XLA Ops:
  2.1 0.9 copy-start.2
  16.6 2.0 %copy-start.5 = (bf16[4,144,128]{2,1,0:T(8,128)(2,1)}, bf16[4,144,128]{2,1,0:T(8,128)(2,1)S(1)}, u32[]{:S(2)}) copy-start(bf16[4,144,128]{2,1,0:T(8,128)(2,1)S(1)} %all_to_all.40) | copy-start | bytes 442372
  16.6 34.9 %collective-permute-start = (bf16[11,256,256]{2,1,0:T(8,128)(2,1)}, bf16[11,256,256]{2,1,0:T(8,128)(2,1)}, u32[]{:S(2)}, u32[]{:S(2)}) collective-permute-start(bf16[11,256,256]{2,1,0:T(8,128)(2,1)} %bitcast.17), channel_id=1, source_target_pairs={{0,1},{1,0},{2,3},{3,2},{4,5},{5,4},{6,7},{7,6},{8,9},{9,8},{10,11... | collective-permute-start | bytes 4325384 | tf_op jit(solution)/shard_map/ppermute | solution.py:165
  32.8 3.8 %copy-start = (bf16[1,1,11,256,256]{4,3,2,1,0:T(8,128)(2,1)S(1)}, bf16[1,1,11,256,256]{4,3,2,1,0:T(8,128)(2,1)}, u32[]{:S(2)}) copy-start(bf16[1,1,11,256,256]{4,3,2,1,0:T(8,128)(2,1)} %param.12) | copy-start | bytes 4325380
  32.8 25.7 %all-to-all-start.1 = ((bf16[4,4,4,128,128]{4,3,2,1,0:T(8,128)(2,1)}), bf16[4,4,4,128,128]{4,3,2,1,0:T(8,128)(2,1)S(1)}, u32[]{:S(2)}, u32[]{:S(2)}) async-start(bf16[4,4,4,128,128]{4,3,2,1,0:T(8,128)(2,1)} %broadcast_in_dim.4), calls=%async_computation.1 | async-start | bytes 4194304 | tf_op jit(solution)/shard_map/all_to_all | solution.py:186
  36.5 19.0 %collective-permute-start.1 = (bf16[11,256,256]{2,1,0:T(8,128)(2,1)S(1)}, bf16[11,256,256]{2,1,0:T(8,128)(2,1)}, u32[]{:S(2)}, u32[]{:S(2)}) collective-permute-start(bf16[11,256,256]{2,1,0:T(8,128)(2,1)S(1)} %bitcast.18), channel_id=1, source_target_pairs={{0,16},{16,0},{1,17},{17,1},{2,18},{18,2},{3,19},{19,3},{4,20},{20... | collective-permute-start | bytes 4325384 | tf_op jit(solution)/shard_map/ppermute | solution.py:165
  51.5 7.0 %collective-permute-start.2 = (bf16[11,256,256]{2,1,0:T(8,128)(2,1)}, bf16[11,256,256]{2,1,0:T(8,128)(2,1)}, u32[]{:S(2)}, u32[]{:S(2)}) collective-permute-start(bf16[11,256,256]{2,1,0:T(8,128)(2,1)} %collective-permute-done.refs_1_), channel_id=1, source_target_pairs={{0,16},{16,0},{1,17},{17,1},{2,18},{18,2},{3,19},{19,3},{4,20},{20... | collective-permute-start | bytes 4325384 | tf_op jit(solution)/shard_map/ppermute | solution.py:165
  62.4 50.1 %copy-start.1 = (bf16[512,512]{1,0:T(8,128)(2,1)S(1)}, bf16[512,512]{1,0:T(8,128)(2,1)}, u32[]{:S(2)}) copy-start(bf16[512,512]{1,0:T(8,128)(2,1)} %weight_ref.1) | copy-start | bytes 1572868
  62.4 50.1 %copy-start.3 = (bf16[128,512]{1,0:T(8,128)(2,1)S(1)}, bf16[128,512]{1,0:T(8,128)(2,1)}, u32[]{:S(2)}) copy-start(bf16[128,512]{1,0:T(8,128)(2,1)} %cot_ref.1) | copy-start | bytes 393220
  62.4 50.1 %copy-start.4 = (f32[512]{0:T(512)S(1)}, f32[512]{0:T(512)}, u32[]{:S(2)}) copy-start(f32[512]{0:T(512)} %param.10) | copy-start | bytes 6148

commit v9 on v8

--- a/solution.py
+++ b/solution.py
@@ -16,7 +16,7 @@
 ROW = ("z_lo", "x", "core")
 COL = ("z_hi", "y_pair", "y_odd")
 QUAD = ("core", "y_odd")
-HOME = ("core", "z_hi", "y_pair", "y_odd")
+HOME = ("core", "y_pair", "y_odd")
 NEAR = ("x", "core")
 Y = ("y_pair", "y_odd")
 Z = ("z_lo", "z_hi")
@@ -62,20 +62,41 @@
     for which in range(4):
         cell_core, cell_odd, cell = cell_of(which)
 
-        def step(slot, carry):
-            tile_copy(which, slot).wait()
+        used = meta_ref[cell, 2, 0]
+
+        def product(slot):
             chip = meta_ref[cell, 1, slot]
             z, x = chip // n_x, lax.rem(chip, n_x)
             window = jnp.concatenate(
                 [block_ref[x, z, cell_odd], block_ref[x, z, 2 + cell_odd]], axis=0
             )
-            total[cell_core, meta_ref[cell, 0, slot]] += jnp.dot(
-                tiles[which, slot], window, preferred_element_type=F32
-            )
+            return jnp.dot(tiles[which, slot], window, preferred_element_type=F32)
+
+        def step(index, carry):
+            slot = 2 * index
+            both = slot + 1 < used
+            other = jnp.where(both, slot + 1, slot)
+            tile_copy(which, slot).wait()
+
+            @pl.when(both)
+            def _():
+                tile_copy(which, other).wait()
+
+            one, two = product(slot), product(other)
+            total[cell_core, meta_ref[cell, 0, slot]] += one
+            total[cell_core, meta_ref[cell, 0, other]] += jnp.where(both, two, 0.0)
             return carry
 
-        lax.fori_loop(0, meta_ref[cell, 2, 0], step, 0)
-    out_ref[...] = total[...].astype(BF16)
+        lax.fori_loop(0, (used + 1) // 2, step, 0)
+    n_pair, nodes = out_ref.shape[1], out_ref.shape[4]
+    for cell_core in range(2):
+        for pair in range(n_pair):
+            for high in range(2):
+                rows = total[cell_core, high * n_pair + pair].astype(BF16)
+                for cell_odd in range(2):
+                    out_ref[cell_core, pair, cell_odd, high] = rows[
+                        cell_odd * nodes : (cell_odd + 1) * nodes
+                    ]
 
 
 def add(ref):
@@ -83,6 +104,19 @@
     for part in range(1, ref.shape[0]):
         total = total + ref[part].astype(F32)
     return total
+
+
+def repeat_kernel(given_ref, out_ref):
+    for copy in range(out_ref.shape[0]):
+        out_ref[copy] = given_ref[...]
+
+
+def pair_kernel(place_ref, parts_ref, keep_ref, send_ref):
+    mine = place_ref[2]
+    for core in range(2):
+        for odd in range(2):
+            keep_ref[core * 2 + odd] = add(parts_ref.at[core, :, odd, mine])
+            send_ref[core * 2 + odd] = add(parts_ref.at[core, :, odd, 1 - mine]).astype(BF16)
 
 
 def with_bias(main, row):
@@ -99,15 +133,11 @@
     return total[depth : depth + 1] + total[depth + 1 : depth + 2]
 
 
-def node_kernel(parts_ref, weight_ref, bias_ref, cot_ref, act_ref, grads_ref):
-    n_high, n_odd = parts_ref.shape[1], parts_ref.shape[2]
-    quarters = []
-    for core in range(parts_ref.shape[0]):
-        for odd in range(n_odd):
-            total = parts_ref[core, 0, odd].astype(F32)
-            for high in range(1, n_high):
-                total = total + parts_ref[core, high, odd].astype(F32)
-            quarters.append(total.astype(BF16))
+def node_kernel(keep_ref, given_ref, weight_ref, bias_ref, cot_ref, act_ref, grads_ref):
+    quarters = [
+        (keep_ref[part] + given_ref[part].astype(F32)).astype(BF16)
+        for part in range(keep_ref.shape[0])
+    ]
     aggregated = jnp.concatenate(quarters, axis=1)
     preact = jnp.dot(aggregated, weight_ref[...], preferred_element_type=F32) + bias_ref[...]
     sigmoid_part = jax.nn.sigmoid(preact)
@@ -122,24 +152,39 @@
         grads_ref[chunk] = with_bias(product[chunk * depth : (chunk + 1) * depth], row)
 
 
+def beside_bias(main, bias):
+    high = bias.astype(BF16).astype(F32)
+    side = jnp.concatenate([high, bias - high], axis=0)
+    return jnp.concatenate([main, side], axis=1).astype(BF16)
+
+
 def scatter_kernel(parts_ref, out_ref):
     total = add(parts_ref)
-    depth = out_ref.shape[1] - PAIR
+    depth, width = out_ref.shape[1], parts_ref.shape[2]
+    row = bias_of(total)
+    bias = jnp.concatenate([row[:, lanes_of(part)] for part in range(width // LANES)], axis=0)
     for chunk in range(out_ref.shape[0]):
-        out_ref[chunk] = with_bias(total[chunk * depth : (chunk + 1) * depth], bias_of(total))
+        out_ref[chunk] = beside_bias(total[chunk * depth : (chunk + 1) * depth], bias)
 
 
 def sum_kernel(parts_ref, out_ref):
     total = add(parts_ref)
-    rounded = with_bias(total[: total.shape[0] - PAIR], bias_of(total))
+    width = total.shape[1] - LANES
+    side = total[:, width:]
+    half = side.shape[0] // 2
+    rounded = beside_bias(total[:, :width], side[:half] + side[half:])
     for copy in range(out_ref.shape[0]):
         out_ref[copy] = rounded
 
 
 def copy_kernel(parts_ref, out_ref):
-    depth = parts_ref.shape[1] - PAIR
+    width = out_ref.shape[2]
     parts = [parts_ref[part].astype(F32) for part in range(parts_ref.shape[0])]
-    rows = jnp.concatenate([part[:depth] for part in parts] + [parts[0][depth:]], axis=0).astype(BF16)
+    side = parts[0][:, width:]
+    half = side.shape[0] // 2
+    bias = side[:half] + side[half:]
+    row = jnp.concatenate([bias[part : part + 1] for part in range(half)], axis=1)
+    rows = with_bias(jnp.concatenate([part[:, :width] for part in parts], axis=0), row)
     for copy in range(out_ref.shape[0]):
         out_ref[copy] = rows
 
@@ -183,11 +228,12 @@
     tiles_both = swap(tiles_y, "core")
     meta = quarters[:, nodes : nodes + 3, :slots].astype(jnp.int32)
     near = lax.all_gather(quarters[:, :nodes], "z_lo", axis=0)
-    blocks = lax.all_to_all(jnp.broadcast_to(near[None], (n_x,) + near.shape), "x", 0, 0)
-    place = jnp.stack([lax.axis_index(axis) for axis in QUAD]).astype(jnp.int32)
+    near = call(repeat_kernel, ((n_x,) + near.shape, BF16), near)
+    blocks = lax.all_to_all(near, "x", 0, 0)
+    place = jnp.stack([lax.axis_index(axis) for axis in QUAD + ("z_hi",)]).astype(jnp.int32)
     term = pl.pallas_call(
         tile_kernel,
-        out_shape=jax.ShapeDtypeStruct((2, 2 * n_pair, size, LANES), BF16),
+        out_shape=jax.ShapeDtypeStruct((2, n_pair, 2, 2, nodes, LANES), BF16),
         in_specs=[SMEM, SMEM] + [HBM] * 4 + [VMEM],
         out_specs=VMEM,
         scratch_shapes=[
@@ -197,24 +243,33 @@
         ],
         compiler_params=PARAMS,
     )(place, meta, tiles, tiles_y, tiles_core, tiles_both, blocks)
-    shares = lax.all_to_all(term.reshape(-1, nodes, LANES), HOME, 0, 0)
+    shares = lax.all_to_all(term.reshape(-1, 2, nodes, LANES), HOME, 0, 0)
+    block = (4, nodes, LANES)
+    keep, send = call(
+        pair_kernel,
+        ((block, F32), (block, BF16)),
+        place,
+        shares.reshape(2, n_pair, 2, 2, nodes, LANES),
+        scalars=1,
+    )
     n_near, n_y, n_deep = lax.axis_size(NEAR), lax.axis_size(Y), lax.axis_size(Z)
     depth = width // n_near
-    tall, short = depth + PAIR, depth // n_y + PAIR
+    tall, wide = depth + PAIR, width + LANES
     activations, grads = call(
         node_kernel,
         (((nodes, width), BF16), ((n_near, tall, width), BF16)),
-        shares.reshape(2, 2 * n_pair, 2, nodes, LANES),
+        keep,
+        swap(send, "z_hi"),
         weight,
         bias_term[None, :],
         cotangent,
     )
     grads = lax.all_to_all(grads, NEAR, 0, 0)
-    grads = call(scatter_kernel, ((n_y, short, width), BF16), grads)
+    grads = call(scatter_kernel, ((n_y, depth // n_y, wide), BF16), grads)
     grads = lax.all_to_all(grads, Y, 0, 0)
-    grads = call(sum_kernel, ((n_deep, short, width), BF16), grads)
+    grads = call(sum_kernel, ((n_deep, depth // n_y, wide), BF16), grads)
     grads = lax.all_to_all(grads, Z, 0, 0)
-    grads = call(sum_kernel, ((n_y, short, width), BF16), grads)
+    grads = call(sum_kernel, ((n_y, depth // n_y, wide), BF16), grads)
     grads = lax.all_to_all(grads, Y, 0, 0)
     grads = call(copy_kernel, ((n_near, tall, width), BF16), grads)
     grads = lax.all_to_all(grads, NEAR, 0, 0)

time: 179 us -> 183 us (1.022)
  blocking collectives: 139 us -> 131 us
  starting transfers between devices: 15.3 us -> 22.6 us
  Pallas kernels: 6.19 us -> 10.4 us
  waiting for transfers between devices: 11.6 us -> 14 us
  local copies, waits for them, and re-layouts: 2.86 us -> 1.02 us
    all_to_all x1, blocking collectives: 50.1 us -> 36.3 us  [per_device(): shares = lax.all_to_all(term.reshape(-1, 2, nodes, LANES), HOME, 0, 0)]
    ppermute x3 -> x4, starting transfers between devices: 11.6 us -> 18.8 us  [swap(): return lax.ppermute(array, axis, [(0, 1), (1, 0)])]
    all_to_all x1, blocking collectives: 9.65 us -> 14.5 us  [per_device(): grads = lax.all_to_all(grads, Z, 0, 0)]
    ppermute x3 -> x4, waiting for transfers between devices: 8.67 us -> 11.3 us  [swap(): return lax.ppermute(array, axis, [(0, 1), (1, 0)])]
    pallas_call x7 -> x9, Pallas kernels: 2.25 us -> 4.49 us  [call(): pl.pallas_call(kernel, out_shape=shapes, in_specs=[SMEM] * scalars + [VME...]
    pallas_call x1, Pallas kernels: 3.94 us -> 5.9 us  [per_device(): pl.pallas_call(tile_kernel, out_shape=jax.ShapeDtypeStruct((2, n_pair, 2,...]
    broadcast_in_dim x1 -> x0, local copies, waits for them, and re-layouts: 1.84 us -> none  [per_device(): jnp.broadcast_to(near[None], (n_x,) + near.shape)]
  transfers between devices with their start and end apart: 4 -> 5, of which waited for: 2 -> 3; matrix products, arithmetic and copies ran while one was open for 1% -> 0% of each run, Pallas kernels for 0% -> 1%
where the time goes in v9:
time: 183 us; the launch traced here: 182 us
  blocking collectives  131 us (72%)
  starting transfers between devices  22.6 us (12%)
  waiting for transfers between devices  14 us (8%)
  Pallas kernels  10.4 us (6%)
    all_to_all x1, blocking collectives, per_device(): shares = lax.all_to_all(term.reshape(-1, 2, nodes, LANES), HOME, 0, 0)  36.3 us
    all_to_all x2, blocking collectives, per_device(): grads = lax.all_to_all(grads, NEAR, 0, 0)  33 us
    all_to_all x2, blocking collectives, per_device(): grads = lax.all_to_all(grads, Y, 0, 0)  21.8 us
    ppermute x4, starting transfers between devices, swap(): return lax.ppermute(array, axis, [(0, 1), (1, 0)])  18.8 us
    all_to_all x1, blocking collectives, per_device(): grads = lax.all_to_all(grads, Z, 0, 0)  14.5 us
    all_to_all x1, blocking collectives, per_device(): quarters = lax.all_to_all(quarters, QUAD, 0, 0)  13.6 us
    all_gather x1, blocking collectives, per_device(): near = lax.all_gather(quarters[:, :nodes], 'z_lo', axis=0)  12.2 us
    ppermute x4, waiting for transfers between devices, swap(): return lax.ppermute(array, axis, [(0, 1), (1, 0)])  11.3 us
  transfers between devices with their start and end apart: 5, of which 3 were waited for; matrix products, arithmetic and copies ran while one was open for 0% of the time, Pallas kernels for 1%

profile of v9, /device:TPU:1, one launch (start us, length us, event | category | flops | bytes accessed | tf_op | source)
XLA Modules:
  0.0 182.3 jit_solution(4632449707413566953)
XLA Ops:
  1.3 0.1 pad.8.clone
  1.4 0.7 convert_bitcast_fusion
  2.0 0.1 maximum_maximum_fusion
  2.1 0.0 copy-start.2
  2.1 0.9 copy-done.2
  3.0 13.6 %all_to_all.40 = bf16[4,144,128]{2,1,0:T(8,128)(2,1)S(1)} all-to-all(bf16[4,144,128]{2,1,0:T(8,128)(2,1)S(1)} %shard_map.103), channel_id=1, replica_groups=mesh['z_lo'=4,'x'=4,'core'=2,'z_hi'=2,'y_pair'=4,'y_odd'=2] {'core','y_o..., dimensions={0} | all-to-all | bytes 294912 | tf_op jit(solution)/shard_map/all_to_all | solution.py:224
  16.6 0.0 copy-start.5
  16.6 2.0 %collective-permute-start = (bf16[11,256,256]{2,1,0:T(8,128)(2,1)}, bf16[11,256,256]{2,1,0:T(8,128)(2,1)}, u32[]{:S(2)}, u32[]{:S(2)}) collective-permute-start(bf16[11,256,256]{2,1,0:T(8,128)(2,1)} %bitcast.19), channel_id=1, source_target_pairs={{0,1},{1,0},{2,3},{3,2},{4,5},{5,4},{6,7},{7,6},{8,9},{9,8},{10,11... | collective-permute-start | bytes 4325384 | tf_op jit(solution)/shard_map/ppermute | solution.py:210
  18.6 0.0 copy-done.5
  18.7 12.2 %all-gather = bf16[16,128,128]{2,1,0:T(8,128)(2,1)S(1)} all-gather(bf16[4,128,128]{2,1,0:T(8,128)(2,1)S(1)} %slice.7), channel_id=2, replica_groups=mesh['z_lo'=4,'x'=4,'core'=2,'z_hi'=2,'y_pair'=4,'y_odd'=2] {'z_lo'}, dimensions={0}, use_global_device_ids=true | all-gather | bytes 655360 | tf_op jit(solution)/shard_map/all_gather | solution.py:230
  30.9 1.6 shard_map.104
  32.5 0.0 copy-start
  32.5 3.7 %all-to-all-start.1 = ((bf16[4,4,4,128,128]{4,3,2,1,0:T(8,128)(2,1)}), bf16[4,4,4,128,128]{4,3,2,1,0:T(8,128)(2,1)S(1)}, u32[]{:S(2)}, u32[]{:S(2)}) async-start(bf16[4,4,4,128,128]{4,3,2,1,0:T(8,128)(2,1)} %shard_map.104), calls=%async_computation.1 | async-start | bytes 4194304 | tf_op jit(solution)/shard_map/all_to_all | solution.py:232
  36.3 0.0 copy-done
  36.3 6.3 %collective-permute-start.1 = (bf16[11,256,256]{2,1,0:T(8,128)(2,1)S(1)}, bf16[11,256,256]{2,1,0:T(8,128)(2,1)}, u32[]{:S(2)}, u32[]{:S(2)}) collective-permute-start(bf16[11,256,256]{2,1,0:T(8,128)(2,1)S(1)} %bitcast.20), channel_id=1, source_target_pairs={{0,16},{16,0},{1,17},{17,1},{2,18},{18,2},{3,19},{19,3},{4,20},{20... | collective-permute-start | bytes 4325384 | tf_op jit(solution)/shard_map/ppermute | solution.py:210
  42.6 8.9 %collective-permute-done.refs_1_ = bf16[11,256,256]{2,1,0:T(8,128)(2,1)} collective-permute-done((bf16[11,256,256]{2,1,0:T(8,128)(2,1)}, bf16[11,256,256]{2,1,0:T(8,128)(2,1)}, u32[]{:S(2)}, u32[]{:S(2)}) %collective-permute-start) | collective-permute-done | bytes 1441824 | tf_op jit(solution)/shard_map/ppermute | solution.py:210
  51.5 3.2 %collective-permute-start.2 = (bf16[11,256,256]{2,1,0:T(8,128)(2,1)}, bf16[11,256,256]{2,1,0:T(8,128)(2,1)}, u32[]{:S(2)}, u32[]{:S(2)}) collective-permute-start(bf16[11,256,256]{2,1,0:T(8,128)(2,1)} %collective-permute-done.refs_1_), channel_id=1, source_target_pairs={{0,16},{16,0},{1,17},{17,1},{2,18},{18,2},{3,19},{19,3},{4,20},{20... | collective-permute-start | bytes 4325384 | tf_op jit(solution)/shard_map/ppermute | solution.py:210
  54.7 0.1 pad_add_fusion.place_ref
  54.8 0.7 slice_convert_fusion.meta_ref
  55.5 0.0 collective-permute-done.1.refs_2_
  55.5 2.7 %all-to-all-done.1.refs_4_ = bf16[4,4,4,128,128]{4,3,2,1,0:T(8,128)(2,1)S(1)} async-done(((bf16[4,4,4,128,128]{4,3,2,1,0:T(8,128)(2,1)}), bf16[4,4,4,128,128]{4,3,2,1,0:T(8,128)(2,1)S(1)}, u32[]{:S(2)}, u32[]{:S(2)}) %all-to-all-start.1) | async-done | bytes 2097184 | tf_op jit(solution)/shard_map/all_to_all | solution.py:232
  58.2 0.0 collective-permute-done.2.refs_3_
  58.2 5.9 %shard_map.105 = bf16[2,4,2,2,128,128]{5,4,3,2,1,0:T(8,128)(2,1)S(1)} custom-call(s32[3]{0:T(128)S(1)} %pad_add_fusion.place_ref, s32[4,3,11]{2,1,0:T(4,128)S(1)} %slice_convert_fusion.meta_ref, bf16[11,256,256]{2,1,0:T(8,128)(2,1)S(1)} %bitcast.21, bf16[11,256,256]{2,1,0:T(8,128)(2,1)} %collective-permute-done.refs_1_, ...), custom_call_target="tpu_custom_call" | custom-call | tf_op jit(solution)/shard_map/pallas_call | solution.py:234
  64.1 0.0 copy-start.1
  64.1 0.0 copy-start.3
  64.1 0.0 copy-start.4
  64.1 36.3 %all_to_all.41 = bf16[16,2,128,128]{3,2,1,0:T(8,128)(2,1)S(1)} all-to-all(bf16[16,2,128,128]{3,2,1,0:T(8,128)(2,1)S(1)} %bitcast.17), channel_id=1, replica_groups=mesh['z_lo'=4,'x'=4,'core'=2,'z_hi'=2,'y_pair'=4,'y_odd'=2] {'core','y_p..., dimensions={0} | all-to-all | bytes 2097152 | tf_op jit(solution)/shard_map/all_to_all | solution.py:246
  100.5 0.7 shard_map.106
  101.1 7.3 %collective-permute-start.3 = (bf16[4,128,128]{2,1,0:T(8,128)(2,1)S(1)}, bf16[4,128,128]{2,1,0:T(8,128)(2,1)S(1)}, u32[]{:S(2)}, u32[]{:S(2)}) collective-permute-start(bf16[4,128,128]{2,1,0:T(8,128)(2,1)S(1)} %get-tuple-element.14), channel_id=1, source_target_pairs={{0,8},{8,0},{1,9},{9,1},{2,10},{10,2},{3,11},{11,3},{4,12},{12,4},... | collective-permute-start | bytes 393224 | tf_op jit(solution)/shard_map/ppermute | solution.py:210
  108.4 2.4 %collective-permute-done.3.given_ref = bf16[4,128,128]{2,1,0:T(8,128)(2,1)S(1)} collective-permute-done((bf16[4,128,128]{2,1,0:T(8,128)(2,1)S(1)}, bf16[4,128,128]{2,1,0:T(8,128)(2,1)S(1)}, u32[]{:S(2)}, u32[]{:S(2)}) %collective-permute-start.3) | collective-permute-done | bytes 131104 | tf_op jit(solution)/shard_map/ppermute | solution.py:210
  110.9 0.0 copy-done.1
  110.9 0.0 copy-done.3
  110.9 0.0 copy-done.4
  110.9 1.0 shard_map.107
  111.8 15.6 %all_to_all.42.parts_ref = bf16[8,72,512]{2,1,0:T(8,128)(2,1)S(1)} all-to-all(bf16[8,72,512]{2,1,0:T(8,128)(2,1)S(1)} %get-tuple-element.16), channel_id=1, replica_groups=mesh['z_lo'=4,'x'=4,'core'=2,'z_hi'=2,'y_pair'=4,'y_odd'=2] {'x','core'}, dimensions={0} | all-to-all | bytes 1179648 | tf_op jit(solution)/shard_map/all_to_all | solution.py:267
  127.4 0.1 shard_map.108
  127.5 12.0 %all_to_all.43.parts_ref = bf16[8,8,640]{2,1,0:T(8,128)(2,1)S(1)} all-to-all(bf16[8,8,640]{2,1,0:T(8,128)(2,1)S(1)} %shard_map.108), channel_id=1, replica_groups=mesh['z_lo'=4,'x'=4,'core'=2,'z_hi'=2,'y_pair'=4,'y_odd'=2] {'y_pair','y..., dimensions={0} | all-to-all | bytes 163840 | tf_op jit(solution)/shard_map/all_to_all | solution.py:269
  139.6 14.5 %all_to_all.44.parts_ref = bf16[8,8,640]{2,1,0:T(8,128)(2,1)S(1)} all-to-all(bf16[8,8,640]{2,1,0:T(8,128)(2,1)S(1)} %shard_map.109), channel_id=1, replica_groups=mesh['z_lo'=4,'x'=4,'core'=2,'z_hi'=2,'y_pair'=4,'y_odd'=2] {'z_lo','z_hi'}, dimensions={0} | all-to-all | bytes 163840 | tf_op jit(solution)/shard_map/all_to_all | solution.py:271
  154.1 9.8 %all_to_all.45.parts_ref = bf16[8,8,640]{2,1,0:T(8,128)(2,1)S(1)} all-to-all(bf16[8,8,640]{2,1,0:T(8,128)(2,1)S(1)} %shard_map.110), channel_id=1, replica_groups=mesh['z_lo'=4,'x'=4,'core'=2,'z_hi'=2,'y_pair'=4,'y_odd'=2] {'y_pair','y..., dimensions={0} | all-to-all | bytes 163840 | tf_op jit(solution)/shard_map/all_to_all | solution.py:273
  163.9 17.4 %all_to_all.46.parts_ref = bf16[8,72,512]{2,1,0:T(8,128)(2,1)S(1)} all-to-all(bf16[8,72,512]{2,1,0:T(8,128)(2,1)S(1)} %shard_map.111), channel_id=1, replica_groups=mesh['z_lo'=4,'x'=4,'core'=2,'z_hi'=2,'y_pair'=4,'y_odd'=2] {'x','core'}, dimensions={0} | all-to-all | bytes 1179648 | tf_op jit(solution)/shard_map/all_to_all | solution.py:275
  181.3 1.0 shard_map.112
  (6 shorter events, 0.1 us)
Async XLA Ops:
  2.1 0.9 copy-start.2
  16.6 2.0 %copy-start.5 = (bf16[4,144,128]{2,1,0:T(8,128)(2,1)}, bf16[4,144,128]{2,1,0:T(8,128)(2,1)S(1)}, u32[]{:S(2)}) copy-start(bf16[4,144,128]{2,1,0:T(8,128)(2,1)S(1)} %all_to_all.40) | copy-start | bytes 442372
  16.6 34.9 %collective-permute-start = (bf16[11,256,256]{2,1,0:T(8,128)(2,1)}, bf16[11,256,256]{2,1,0:T(8,128)(2,1)}, u32[]{:S(2)}, u32[]{:S(2)}) collective-permute-start(bf16[11,256,256]{2,1,0:T(8,128)(2,1)} %bitcast.19), channel_id=1, source_target_pairs={{0,1},{1,0},{2,3},{3,2},{4,5},{5,4},{6,7},{7,6},{8,9},{9,8},{10,11... | collective-permute-start | bytes 4325384 | tf_op jit(solution)/shard_map/ppermute | solution.py:210
  32.5 3.8 %copy-start = (bf16[1,1,11,256,256]{4,3,2,1,0:T(8,128)(2,1)S(1)}, bf16[1,1,11,256,256]{4,3,2,1,0:T(8,128)(2,1)}, u32[]{:S(2)}) copy-start(bf16[1,1,11,256,256]{4,3,2,1,0:T(8,128)(2,1)} %param.12) | copy-start | bytes 4325380
  32.5 25.7 %all-to-all-start.1 = ((bf16[4,4,4,128,128]{4,3,2,1,0:T(8,128)(2,1)}), bf16[4,4,4,128,128]{4,3,2,1,0:T(8,128)(2,1)S(1)}, u32[]{:S(2)}, u32[]{:S(2)}) async-start(bf16[4,4,4,128,128]{4,3,2,1,0:T(8,128)(2,1)} %shard_map.104), calls=%async_computation.1 | async-start | bytes 4194304 | tf_op jit(solution)/shard_map/all_to_all | solution.py:232
  36.3 19.2 %collective-permute-start.1 = (bf16[11,256,256]{2,1,0:T(8,128)(2,1)S(1)}, bf16[11,256,256]{2,1,0:T(8,128)(2,1)}, u32[]{:S(2)}, u32[]{:S(2)}) collective-permute-start(bf16[11,256,256]{2,1,0:T(8,128)(2,1)S(1)} %bitcast.20), channel_id=1, source_target_pairs={{0,16},{16,0},{1,17},{17,1},{2,18},{18,2},{3,19},{19,3},{4,20},{20... | collective-permute-start | bytes 4325384 | tf_op jit(solution)/shard_map/ppermute | solution.py:210
  51.5 6.7 %collective-permute-start.2 = (bf16[11,256,256]{2,1,0:T(8,128)(2,1)}, bf16[11,256,256]{2,1,0:T(8,128)(2,1)}, u32[]{:S(2)}, u32[]{:S(2)}) collective-permute-start(bf16[11,256,256]{2,1,0:T(8,128)(2,1)} %collective-permute-done.refs_1_), channel_id=1, source_target_pairs={{0,16},{16,0},{1,17},{17,1},{2,18},{18,2},{3,19},{19,3},{4,20},{20... | collective-permute-start | bytes 4325384 | tf_op jit(solution)/shard_map/ppermute | solution.py:210
  64.1 46.8 %copy-start.1 = (bf16[512,512]{1,0:T(8,128)(2,1)S(1)}, bf16[512,512]{1,0:T(8,128)(2,1)}, u32[]{:S(2)}) copy-start(bf16[512,512]{1,0:T(8,128)(2,1)} %weight_ref.1) | copy-start | bytes 1572868
  64.1 46.7 %copy-start.3 = (bf16[128,512]{1,0:T(8,128)(2,1)S(1)}, bf16[128,512]{1,0:T(8,128)(2,1)}, u32[]{:S(2)}) copy-start(bf16[128,512]{1,0:T(8,128)(2,1)} %cot_ref.1) | copy-start | bytes 393220
  64.1 46.7 %copy-start.4 = (f32[512]{0:T(512)S(1)}, f32[512]{0:T(512)}, u32[]{:S(2)}) copy-start(f32[512]{0:T(512)} %param.10) | copy-start | bytes 6148
  101.1 9.7 %collective-permute-start.3 = (bf16[4,128,128]{2,1,0:T(8,128)(2,1)S(1)}, bf16[4,128,128]{2,1,0:T(8,128)(2,1)S(1)}, u32[]{:S(2)}, u32[]{:S(2)}) collective-permute-start(bf16[4,128,128]{2,1,0:T(8,128)(2,1)S(1)} %get-tuple-element.14), channel_id=1, source_target_pairs={{0,8},{8,0},{1,9},{9,1},{2,10},{10,2},{3,11},{11,3},{4,12},{12,4},... | collective-permute-start | bytes 393224 | tf_op jit(solution)/shard_map/ppermute | solution.py:210

commit v10 on v8

--- a/solution.py
+++ b/solution.py
@@ -62,19 +62,32 @@
     for which in range(4):
         cell_core, cell_odd, cell = cell_of(which)
 
-        def step(slot, carry):
-            tile_copy(which, slot).wait()
+        used = meta_ref[cell, 2, 0]
+
+        def product(slot):
             chip = meta_ref[cell, 1, slot]
             z, x = chip // n_x, lax.rem(chip, n_x)
             window = jnp.concatenate(
                 [block_ref[x, z, cell_odd], block_ref[x, z, 2 + cell_odd]], axis=0
             )
-            total[cell_core, meta_ref[cell, 0, slot]] += jnp.dot(
-                tiles[which, slot], window, preferred_element_type=F32
-            )
+            return jnp.dot(tiles[which, slot], window, preferred_element_type=F32)
+
+        def step(index, carry):
+            slot = 2 * index
+            both = slot + 1 < used
+            other = jnp.where(both, slot + 1, slot)
+            tile_copy(which, slot).wait()
+
+            @pl.when(both)
+            def _():
+                tile_copy(which, other).wait()
+
+            one, two = product(slot), product(other)
+            total[cell_core, meta_ref[cell, 0, slot]] += one
+            total[cell_core, meta_ref[cell, 0, other]] += jnp.where(both, two, 0.0)
             return carry
 
-        lax.fori_loop(0, meta_ref[cell, 2, 0], step, 0)
+        lax.fori_loop(0, (used + 1) // 2, step, 0)
     out_ref[...] = total[...].astype(BF16)
 
 
@@ -83,6 +96,11 @@
     for part in range(1, ref.shape[0]):
         total = total + ref[part].astype(F32)
     return total
+
+
+def repeat_kernel(given_ref, out_ref):
+    for copy in range(out_ref.shape[0]):
+        out_ref[copy] = given_ref[...]
 
 
 def with_bias(main, row):
@@ -183,7 +201,8 @@
     tiles_both = swap(tiles_y, "core")
     meta = quarters[:, nodes : nodes + 3, :slots].astype(jnp.int32)
     near = lax.all_gather(quarters[:, :nodes], "z_lo", axis=0)
-    blocks = lax.all_to_all(jnp.broadcast_to(near[None], (n_x,) + near.shape), "x", 0, 0)
+    near = call(repeat_kernel, ((n_x,) + near.shape, BF16), near)
+    blocks = lax.all_to_all(near, "x", 0, 0)
     place = jnp.stack([lax.axis_index(axis) for axis in QUAD]).astype(jnp.int32)
     term = pl.pallas_call(
         tile_kernel,

time: 179 us -> 178 us (level)
  local copies, waits for them, and re-layouts: 2.86 us -> 1.02 us
    broadcast_in_dim x1 -> x0, local copies, waits for them, and re-layouts: 1.84 us -> none  [per_device(): jnp.broadcast_to(near[None], (n_x,) + near.shape)]
    pallas_call x7 -> x8, Pallas kernels: 2.25 us -> 3.85 us  [call(): pl.pallas_call(kernel, out_shape=shapes, in_specs=[SMEM] * scalars + [VME...]
  transfers between devices with their start and end apart: 4 -> 4, of which waited for: 2 -> 2; matrix products, arithmetic and copies ran while one was open for 1% -> 0% of each run, Pallas kernels for 0% -> 1%
where the time goes in v10:
time: 178 us
  blocking collectives  139 us (78%)
  starting transfers between devices  15.3 us (9%)
  waiting for transfers between devices  11.6 us (7%)
  Pallas kernels  7.6 us (4%)
    all_to_all x1, blocking collectives, per_device(): shares = lax.all_to_all(term.reshape(-1, nodes, LANES), HOME, 0, 0)  49.1 us
    all_to_all x2, blocking collectives, per_device(): grads = lax.all_to_all(grads, NEAR, 0, 0)  31.4 us
    all_to_all x2, blocking collectives, per_device(): grads = lax.all_to_all(grads, Y, 0, 0)  22.3 us
    all_to_all x1, blocking collectives, per_device(): quarters = lax.all_to_all(quarters, QUAD, 0, 0)  13.6 us
    all_gather x1, blocking collectives, per_device(): near = lax.all_gather(quarters[:, :nodes], 'z_lo', axis=0)  12.2 us
    ppermute x3, starting transfers between devices, swap(): return lax.ppermute(array, axis, [(0, 1), (1, 0)])  11.6 us
    all_to_all x1, blocking collectives, per_device(): grads = lax.all_to_all(grads, Z, 0, 0)  10.7 us
    ppermute x3, waiting for transfers between devices, swap(): return lax.ppermute(array, axis, [(0, 1), (1, 0)])  8.91 us
  transfers between devices with their start and end apart: 4, of which 2 were waited for; matrix products, arithmetic and copies ran while one was open for 0% of the time, Pallas kernels for 1%

profile of v10, /device:TPU:1, one launch (start us, length us, event | category | flops | bytes accessed | tf_op | source)
XLA Modules:
  0.0 177.7 jit_solution(747776457372529922)
XLA Ops:
  1.3 0.1 pad.8.clone
  1.4 0.7 convert_bitcast_fusion
  2.0 0.1 maximum_maximum_fusion
  2.1 0.0 copy-start.2
  2.1 0.9 copy-done.2
  3.0 13.6 %all_to_all.40 = bf16[4,144,128]{2,1,0:T(8,128)(2,1)S(1)} all-to-all(bf16[4,144,128]{2,1,0:T(8,128)(2,1)S(1)} %shard_map.103), channel_id=1, replica_groups=mesh['z_lo'=4,'x'=4,'core'=2,'z_hi'=2,'y_pair'=4,'y_odd'=2] {'core','y_o..., dimensions={0} | all-to-all | bytes 294912 | tf_op jit(solution)/shard_map/all_to_all | solution.py:197
  16.6 0.0 copy-start.5
  16.6 2.0 %collective-permute-start = (bf16[11,256,256]{2,1,0:T(8,128)(2,1)}, bf16[11,256,256]{2,1,0:T(8,128)(2,1)}, u32[]{:S(2)}, u32[]{:S(2)}) collective-permute-start(bf16[11,256,256]{2,1,0:T(8,128)(2,1)} %bitcast.18), channel_id=1, source_target_pairs={{0,1},{1,0},{2,3},{3,2},{4,5},{5,4},{6,7},{7,6},{8,9},{9,8},{10,11... | collective-permute-start | bytes 4325384 | tf_op jit(solution)/shard_map/ppermute | solution.py:183
  18.6 0.0 copy-done.5
  18.7 12.2 %all-gather = bf16[16,128,128]{2,1,0:T(8,128)(2,1)S(1)} all-gather(bf16[4,128,128]{2,1,0:T(8,128)(2,1)S(1)} %slice.7), channel_id=2, replica_groups=mesh['z_lo'=4,'x'=4,'core'=2,'z_hi'=2,'y_pair'=4,'y_odd'=2] {'z_lo'}, dimensions={0}, use_global_device_ids=true | all-gather | bytes 655360 | tf_op jit(solution)/shard_map/all_gather | solution.py:203
  30.9 1.6 shard_map.104
  32.5 0.0 copy-start
  32.5 3.7 %all-to-all-start.1 = ((bf16[4,4,4,128,128]{4,3,2,1,0:T(8,128)(2,1)}), bf16[4,4,4,128,128]{4,3,2,1,0:T(8,128)(2,1)S(1)}, u32[]{:S(2)}, u32[]{:S(2)}) async-start(bf16[4,4,4,128,128]{4,3,2,1,0:T(8,128)(2,1)} %shard_map.104), calls=%async_computation.1 | async-start | bytes 4194304 | tf_op jit(solution)/shard_map/all_to_all | solution.py:205
  36.3 0.0 copy-done
  36.3 6.3 %collective-permute-start.1 = (bf16[11,256,256]{2,1,0:T(8,128)(2,1)S(1)}, bf16[11,256,256]{2,1,0:T(8,128)(2,1)}, u32[]{:S(2)}, u32[]{:S(2)}) collective-permute-start(bf16[11,256,256]{2,1,0:T(8,128)(2,1)S(1)} %bitcast.19), channel_id=1, source_target_pairs={{0,16},{16,0},{1,17},{17,1},{2,18},{18,2},{3,19},{19,3},{4,20},{20... | collective-permute-start | bytes 4325384 | tf_op jit(solution)/shard_map/ppermute | solution.py:183
  42.6 8.9 %collective-permute-done.refs_1_ = bf16[11,256,256]{2,1,0:T(8,128)(2,1)} collective-permute-done((bf16[11,256,256]{2,1,0:T(8,128)(2,1)}, bf16[11,256,256]{2,1,0:T(8,128)(2,1)}, u32[]{:S(2)}, u32[]{:S(2)}) %collective-permute-start) | collective-permute-done | bytes 1441824 | tf_op jit(solution)/shard_map/ppermute | solution.py:183
  51.5 3.2 %collective-permute-start.2 = (bf16[11,256,256]{2,1,0:T(8,128)(2,1)}, bf16[11,256,256]{2,1,0:T(8,128)(2,1)}, u32[]{:S(2)}, u32[]{:S(2)}) collective-permute-start(bf16[11,256,256]{2,1,0:T(8,128)(2,1)} %collective-permute-done.refs_1_), channel_id=1, source_target_pairs={{0,16},{16,0},{1,17},{17,1},{2,18},{18,2},{3,19},{19,3},{4,20},{20... | collective-permute-start | bytes 4325384 | tf_op jit(solution)/shard_map/ppermute | solution.py:183
  54.7 0.1 pad_add_fusion.place_ref
  54.8 0.7 slice_convert_fusion.meta_ref
  55.5 0.0 collective-permute-done.1.refs_2_
  55.5 2.7 %all-to-all-done.1.refs_4_ = bf16[4,4,4,128,128]{4,3,2,1,0:T(8,128)(2,1)S(1)} async-done(((bf16[4,4,4,128,128]{4,3,2,1,0:T(8,128)(2,1)}), bf16[4,4,4,128,128]{4,3,2,1,0:T(8,128)(2,1)S(1)}, u32[]{:S(2)}, u32[]{:S(2)}) %all-to-all-start.1) | async-done | bytes 2097184 | tf_op jit(solution)/shard_map/all_to_all | solution.py:205
  58.2 0.0 collective-permute-done.2.refs_3_
  58.2 3.8 %shard_map.105 = bf16[2,8,256,128]{3,2,1,0:T(8,128)(2,1)S(1)} custom-call(s32[2]{0:T(128)S(1)} %pad_add_fusion.place_ref, s32[4,3,11]{2,1,0:T(4,128)S(1)} %slice_convert_fusion.meta_ref, bf16[11,256,256]{2,1,0:T(8,128)(2,1)S(1)} %bitcast.20, bf16[11,256,256]{2,1,0:T(8,128)(2,1)} %collective-permute-done.refs_1_, ...), custom_call_target="tpu_custom_call" | custom-call | tf_op jit(solution)/shard_map/pallas_call | solution.py:207
  62.0 0.0 copy-start.1
  62.0 0.0 copy-start.3
  62.0 0.0 copy-start.4
  62.0 49.1 %all_to_all.41 = bf16[32,128,128]{2,1,0:T(8,128)(2,1)S(1)} all-to-all(bf16[32,128,128]{2,1,0:T(8,128)(2,1)S(1)} %bitcast.16), channel_id=1, replica_groups=mesh['z_lo'=4,'x'=4,'core'=2,'z_hi'=2,'y_pair'=4,'y_odd'=2] {'core','z_h..., dimensions={0} | all-to-all | bytes 2097152 | tf_op jit(solution)/shard_map/all_to_all | solution.py:219
  111.1 0.0 copy-done.1
  111.1 0.0 copy-done.3
  111.1 0.0 copy-done.4
  111.1 1.0 shard_map.106
  112.1 13.4 %all_to_all.42.parts_ref = bf16[8,72,512]{2,1,0:T(8,128)(2,1)S(1)} all-to-all(bf16[8,72,512]{2,1,0:T(8,128)(2,1)S(1)} %get-tuple-element.12), channel_id=1, replica_groups=mesh['z_lo'=4,'x'=4,'core'=2,'z_hi'=2,'y_pair'=4,'y_odd'=2] {'x','core'}, dimensions={0} | all-to-all | bytes 1179648 | tf_op jit(solution)/shard_map/all_to_all | solution.py:231
  125.5 0.1 shard_map.107
  125.6 12.0 %all_to_all.43.parts_ref = bf16[8,16,512]{2,1,0:T(8,128)(2,1)S(1)} all-to-all(bf16[8,16,512]{2,1,0:T(8,128)(2,1)S(1)} %shard_map.107), channel_id=1, replica_groups=mesh['z_lo'=4,'x'=4,'core'=2,'z_hi'=2,'y_pair'=4,'y_odd'=2] {'y_pair','y..., dimensions={0} | all-to-all | bytes 262144 | tf_op jit(solution)/shard_map/all_to_all | solution.py:233
  137.6 10.7 %all_to_all.44.parts_ref = bf16[8,16,512]{2,1,0:T(8,128)(2,1)S(1)} all-to-all(bf16[8,16,512]{2,1,0:T(8,128)(2,1)S(1)} %shard_map.108), channel_id=1, replica_groups=mesh['z_lo'=4,'x'=4,'core'=2,'z_hi'=2,'y_pair'=4,'y_odd'=2] {'z_lo','z_hi'}, dimensions={0} | all-to-all | bytes 262144 | tf_op jit(solution)/shard_map/all_to_all | solution.py:235
  148.4 10.3 %all_to_all.45.parts_ref = bf16[8,16,512]{2,1,0:T(8,128)(2,1)S(1)} all-to-all(bf16[8,16,512]{2,1,0:T(8,128)(2,1)S(1)} %shard_map.109), channel_id=1, replica_groups=mesh['z_lo'=4,'x'=4,'core'=2,'z_hi'=2,'y_pair'=4,'y_odd'=2] {'y_pair','y..., dimensions={0} | all-to-all | bytes 262144 | tf_op jit(solution)/shard_map/all_to_all | solution.py:237
  158.7 18.0 %all_to_all.46.parts_ref = bf16[8,72,512]{2,1,0:T(8,128)(2,1)S(1)} all-to-all(bf16[8,72,512]{2,1,0:T(8,128)(2,1)S(1)} %shard_map.110), channel_id=1, replica_groups=mesh['z_lo'=4,'x'=4,'core'=2,'z_hi'=2,'y_pair'=4,'y_odd'=2] {'x','core'}, dimensions={0} | all-to-all | bytes 1179648 | tf_op jit(solution)/shard_map/all_to_all | solution.py:239
  176.7 1.0 shard_map.111
  (6 shorter events, 0.1 us)
Async XLA Ops:
  2.1 0.9 copy-start.2
  16.6 2.0 %copy-start.5 = (bf16[4,144,128]{2,1,0:T(8,128)(2,1)}, bf16[4,144,128]{2,1,0:T(8,128)(2,1)S(1)}, u32[]{:S(2)}) copy-start(bf16[4,144,128]{2,1,0:T(8,128)(2,1)S(1)} %all_to_all.40) | copy-start | bytes 442372
  16.6 34.9 %collective-permute-start = (bf16[11,256,256]{2,1,0:T(8,128)(2,1)}, bf16[11,256,256]{2,1,0:T(8,128)(2,1)}, u32[]{:S(2)}, u32[]{:S(2)}) collective-permute-start(bf16[11,256,256]{2,1,0:T(8,128)(2,1)} %bitcast.18), channel_id=1, source_target_pairs={{0,1},{1,0},{2,3},{3,2},{4,5},{5,4},{6,7},{7,6},{8,9},{9,8},{10,11... | collective-permute-start | bytes 4325384 | tf_op jit(solution)/shard_map/ppermute | solution.py:183
  32.5 3.8 %copy-start = (bf16[1,1,11,256,256]{4,3,2,1,0:T(8,128)(2,1)S(1)}, bf16[1,1,11,256,256]{4,3,2,1,0:T(8,128)(2,1)}, u32[]{:S(2)}) copy-start(bf16[1,1,11,256,256]{4,3,2,1,0:T(8,128)(2,1)} %param.12) | copy-start | bytes 4325380
  32.5 25.7 %all-to-all-start.1 = ((bf16[4,4,4,128,128]{4,3,2,1,0:T(8,128)(2,1)}), bf16[4,4,4,128,128]{4,3,2,1,0:T(8,128)(2,1)S(1)}, u32[]{:S(2)}, u32[]{:S(2)}) async-start(bf16[4,4,4,128,128]{4,3,2,1,0:T(8,128)(2,1)} %shard_map.104), calls=%async_computation.1 | async-start | bytes 4194304 | tf_op jit(solution)/shard_map/all_to_all | solution.py:205
  36.3 19.2 %collective-permute-start.1 = (bf16[11,256,256]{2,1,0:T(8,128)(2,1)S(1)}, bf16[11,256,256]{2,1,0:T(8,128)(2,1)}, u32[]{:S(2)}, u32[]{:S(2)}) collective-permute-start(bf16[11,256,256]{2,1,0:T(8,128)(2,1)S(1)} %bitcast.19), channel_id=1, source_target_pairs={{0,16},{16,0},{1,17},{17,1},{2,18},{18,2},{3,19},{19,3},{4,20},{20... | collective-permute-start | bytes 4325384 | tf_op jit(solution)/shard_map/ppermute | solution.py:183
  51.5 6.7 %collective-permute-start.2 = (bf16[11,256,256]{2,1,0:T(8,128)(2,1)}, bf16[11,256,256]{2,1,0:T(8,128)(2,1)}, u32[]{:S(2)}, u32[]{:S(2)}) collective-permute-start(bf16[11,256,256]{2,1,0:T(8,128)(2,1)} %collective-permute-done.refs_1_), channel_id=1, source_target_pairs={{0,16},{16,0},{1,17},{17,1},{2,18},{18,2},{3,19},{19,3},{4,20},{20... | collective-permute-start | bytes 4325384 | tf_op jit(solution)/shard_map/ppermute | solution.py:183
  62.0 49.2 %copy-start.1 = (bf16[512,512]{1,0:T(8,128)(2,1)S(1)}, bf16[512,512]{1,0:T(8,128)(2,1)}, u32[]{:S(2)}) copy-start(bf16[512,512]{1,0:T(8,128)(2,1)} %weight_ref.1) | copy-start | bytes 1572868
  62.0 49.1 %copy-start.3 = (bf16[128,512]{1,0:T(8,128)(2,1)S(1)}, bf16[128,512]{1,0:T(8,128)(2,1)}, u32[]{:S(2)}) copy-start(bf16[128,512]{1,0:T(8,128)(2,1)} %cot_ref.1) | copy-start | bytes 393220
  62.0 49.1 %copy-start.4 = (f32[512]{0:T(512)S(1)}, f32[512]{0:T(512)}, u32[]{:S(2)}) copy-start(f32[512]{0:T(512)} %param.10) | copy-start | bytes 6148

commit v11 on v10

--- a/solution.py
+++ b/solution.py
@@ -16,7 +16,7 @@
 ROW = ("z_lo", "x", "core")
 COL = ("z_hi", "y_pair", "y_odd")
 QUAD = ("core", "y_odd")
-HOME = ("core", "z_hi", "y_pair", "y_odd")
+HOME = ("core", "y_pair", "y_odd", "z_hi")
 NEAR = ("x", "core")
 Y = ("y_pair", "y_odd")
 Z = ("z_lo", "z_hi")
@@ -88,7 +88,15 @@
             return carry
 
         lax.fori_loop(0, (used + 1) // 2, step, 0)
-    out_ref[...] = total[...].astype(BF16)
+    n_pair, nodes = out_ref.shape[1], out_ref.shape[4]
+    for cell_core in range(2):
+        for pair in range(n_pair):
+            for high in range(2):
+                rows = total[cell_core, high * n_pair + pair].astype(BF16)
+                for cell_odd in range(2):
+                    out_ref[cell_core, pair, cell_odd, high] = rows[
+                        cell_odd * nodes : (cell_odd + 1) * nodes
+                    ]
 
 
 def add(ref):
@@ -118,13 +126,14 @@
 
 
 def node_kernel(parts_ref, weight_ref, bias_ref, cot_ref, act_ref, grads_ref):
-    n_high, n_odd = parts_ref.shape[1], parts_ref.shape[2]
+    n_core, n_pair, n_odd, n_high = parts_ref.shape[:4]
     quarters = []
-    for core in range(parts_ref.shape[0]):
+    for core in range(n_core):
         for odd in range(n_odd):
-            total = parts_ref[core, 0, odd].astype(F32)
-            for high in range(1, n_high):
-                total = total + parts_ref[core, high, odd].astype(F32)
+            senders = [(pair, high) for pair in range(n_pair) for high in range(n_high)]
+            total = parts_ref[core, 0, odd, 0].astype(F32)
+            for pair, high in senders[1:]:
+                total = total + parts_ref[core, pair, odd, high].astype(F32)
             quarters.append(total.astype(BF16))
     aggregated = jnp.concatenate(quarters, axis=1)
     preact = jnp.dot(aggregated, weight_ref[...], preferred_element_type=F32) + bias_ref[...]
@@ -162,13 +171,14 @@
         out_ref[copy] = rows
 
 
-def last_kernel(parts_ref, weight_ref, bias_ref):
-    depth = parts_ref.shape[1] - PAIR
-    for chunk in range(parts_ref.shape[0]):
-        rows = parts_ref[chunk].astype(F32)
-        weight_ref[chunk * depth : (chunk + 1) * depth] = rows[:depth]
-        if chunk == 0:
-            bias_ref[...] = bias_of(rows)
+def last_kernel(place_ref, own_ref, other_ref, weight_ref, bias_ref):
+    depth = own_ref.shape[1] - PAIR
+    for chunk in range(own_ref.shape[0]):
+        for core, ref in ((place_ref[0], own_ref), (1 - place_ref[0], other_ref)):
+            rows = pl.ds(pl.multiple_of((chunk * 2 + core) * depth, depth), depth)
+            part = ref[chunk].astype(F32)
+            weight_ref[rows] = part[:depth]
+    bias_ref[...] = bias_of(own_ref[0].astype(F32))
 
 
 def call(kernel, out, *args, scalars=0):
@@ -206,7 +216,7 @@
     place = jnp.stack([lax.axis_index(axis) for axis in QUAD]).astype(jnp.int32)
     term = pl.pallas_call(
         tile_kernel,
-        out_shape=jax.ShapeDtypeStruct((2, 2 * n_pair, size, LANES), BF16),
+        out_shape=jax.ShapeDtypeStruct((2, n_pair, 2, 2, nodes, LANES), BF16),
         in_specs=[SMEM, SMEM] + [HBM] * 4 + [VMEM],
         out_specs=VMEM,
         scratch_shapes=[
@@ -223,7 +233,7 @@
     activations, grads = call(
         node_kernel,
         (((nodes, width), BF16), ((n_near, tall, width), BF16)),
-        shares.reshape(2, 2 * n_pair, 2, nodes, LANES),
+        shares.reshape(2, n_pair, 2, 2, nodes, LANES),
         weight,
         bias_term[None, :],
         cotangent,
@@ -235,10 +245,15 @@
     grads = lax.all_to_all(grads, Z, 0, 0)
     grads = call(sum_kernel, ((n_y, short, width), BF16), grads)
     grads = lax.all_to_all(grads, Y, 0, 0)
-    grads = call(copy_kernel, ((n_near, tall, width), BF16), grads)
-    grads = lax.all_to_all(grads, NEAR, 0, 0)
+    grads = call(copy_kernel, ((n_x, tall, width), BF16), grads)
+    grads = lax.all_to_all(grads, "x", 0, 0)
     weight_grad, bias_grad = call(
-        last_kernel, (((width, width), F32), ((1, width), F32)), grads
+        last_kernel,
+        (((width, width), F32), ((1, width), F32)),
+        place,
+        grads,
+        swap(grads, "core"),
+        scalars=1,
     )
     return activations, weight_grad, bias_grad[0]
 

time: 178 us -> 178 us (level)
  blocking collectives: 139 us -> 129 us
  starting transfers between devices: 15.3 us -> 23.6 us
    all_to_all x2 -> x1, blocking collectives: 31.4 us -> 13.9 us  [per_device(): grads = lax.all_to_all(grads, NEAR, 0, 0)]
    ppermute x3 -> x4, starting transfers between devices: 11.6 us -> 19.8 us  [swap(): return lax.ppermute(array, axis, [(0, 1), (1, 0)])]
    all_to_all x0 -> x1, blocking collectives: none -> 8.07 us  [per_device(): grads = lax.all_to_all(grads, 'x', 0, 0)]
    ppermute x3 -> x4, waiting for transfers between devices: 8.91 us -> 10.1 us  [swap(): return lax.ppermute(array, axis, [(0, 1), (1, 0)])]
  transfers between devices with their start and end apart: 4 -> 5, of which waited for: 2 -> 3; matrix products, arithmetic and copies ran while one was open for 0% -> 0% of each run, Pallas kernels for 1% -> 1%
where the time goes in v11:
time: 178 us
  blocking collectives  129 us (72%)
  starting transfers between devices  23.6 us (13%)
  waiting for transfers between devices  12.8 us (7%)
  Pallas kernels  8.88 us (5%)
    all_to_all x1, blocking collectives, per_device(): shares = lax.all_to_all(term.reshape(-1, nodes, LANES), HOME, 0, 0)  49.3 us
    all_to_all x2, blocking collectives, per_device(): grads = lax.all_to_all(grads, Y, 0, 0)  22 us
    ppermute x4, starting transfers between devices, swap(): return lax.ppermute(array, axis, [(0, 1), (1, 0)])  19.8 us
    all_to_all x1, blocking collectives, per_device(): grads = lax.all_to_all(grads, NEAR, 0, 0)  13.9 us
    all_to_all x1, blocking collectives, per_device(): quarters = lax.all_to_all(quarters, QUAD, 0, 0)  13.6 us
    all_gather x1, blocking collectives, per_device(): near = lax.all_gather(quarters[:, :nodes], 'z_lo', axis=0)  12.2 us
    ppermute x4, waiting for transfers between devices, swap(): return lax.ppermute(array, axis, [(0, 1), (1, 0)])  10.1 us
    all_to_all x1, blocking collectives, per_device(): grads = lax.all_to_all(grads, Z, 0, 0)  9.53 us
  transfers between devices with their start and end apart: 5, of which 3 were waited for; matrix products, arithmetic and copies ran while one was open for 0% of the time, Pallas kernels for 1%

profile of v11, /device:TPU:1, one launch (start us, length us, event | category | flops | bytes accessed | tf_op | source)
XLA Modules:
  0.0 177.8 jit_solution(14808501411582893677)
XLA Ops:
  1.3 0.1 pad.8.clone
  1.4 0.7 convert_bitcast_fusion
  2.0 0.1 maximum_maximum_fusion
  2.1 0.0 copy-start.2
  2.1 0.9 copy-done.2
  3.0 13.6 %all_to_all.40 = bf16[4,144,128]{2,1,0:T(8,128)(2,1)S(1)} all-to-all(bf16[4,144,128]{2,1,0:T(8,128)(2,1)S(1)} %shard_map.103), channel_id=1, replica_groups=mesh['z_lo'=4,'x'=4,'core'=2,'z_hi'=2,'y_pair'=4,'y_odd'=2] {'core','y_o..., dimensions={0} | all-to-all | bytes 294912 | tf_op jit(solution)/shard_map/all_to_all | solution.py:207
  16.6 0.0 copy-start.5
  16.6 2.0 %collective-permute-start = (bf16[11,256,256]{2,1,0:T(8,128)(2,1)}, bf16[11,256,256]{2,1,0:T(8,128)(2,1)}, u32[]{:S(2)}, u32[]{:S(2)}) collective-permute-start(bf16[11,256,256]{2,1,0:T(8,128)(2,1)} %bitcast.18), channel_id=1, source_target_pairs={{0,1},{1,0},{2,3},{3,2},{4,5},{5,4},{6,7},{7,6},{8,9},{9,8},{10,11... | collective-permute-start | bytes 4325384 | tf_op jit(solution)/shard_map/ppermute | solution.py:193
  18.6 0.0 copy-done.5
  18.7 12.2 %all-gather = bf16[16,128,128]{2,1,0:T(8,128)(2,1)S(1)} all-gather(bf16[4,128,128]{2,1,0:T(8,128)(2,1)S(1)} %slice.7), channel_id=2, replica_groups=mesh['z_lo'=4,'x'=4,'core'=2,'z_hi'=2,'y_pair'=4,'y_odd'=2] {'z_lo'}, dimensions={0}, use_global_device_ids=true | all-gather | bytes 655360 | tf_op jit(solution)/shard_map/all_gather | solution.py:213
  30.9 1.6 shard_map.104
  32.5 0.0 copy-start
  32.5 3.7 %all-to-all-start.1 = ((bf16[4,4,4,128,128]{4,3,2,1,0:T(8,128)(2,1)}), bf16[4,4,4,128,128]{4,3,2,1,0:T(8,128)(2,1)S(1)}, u32[]{:S(2)}, u32[]{:S(2)}) async-start(bf16[4,4,4,128,128]{4,3,2,1,0:T(8,128)(2,1)} %shard_map.104), calls=%async_computation.1 | async-start | bytes 4194304 | tf_op jit(solution)/shard_map/all_to_all | solution.py:215
  36.3 0.0 copy-done
  36.3 6.3 %collective-permute-start.1 = (bf16[11,256,256]{2,1,0:T(8,128)(2,1)S(1)}, bf16[11,256,256]{2,1,0:T(8,128)(2,1)}, u32[]{:S(2)}, u32[]{:S(2)}) collective-permute-start(bf16[11,256,256]{2,1,0:T(8,128)(2,1)S(1)} %bitcast.19), channel_id=1, source_target_pairs={{0,16},{16,0},{1,17},{17,1},{2,18},{18,2},{3,19},{19,3},{4,20},{20... | collective-permute-start | bytes 4325384 | tf_op jit(solution)/shard_map/ppermute | solution.py:193
  42.6 8.9 %collective-permute-done.refs_1_ = bf16[11,256,256]{2,1,0:T(8,128)(2,1)} collective-permute-done((bf16[11,256,256]{2,1,0:T(8,128)(2,1)}, bf16[11,256,256]{2,1,0:T(8,128)(2,1)}, u32[]{:S(2)}, u32[]{:S(2)}) %collective-permute-start) | collective-permute-done | bytes 1441824 | tf_op jit(solution)/shard_map/ppermute | solution.py:193
  51.5 3.2 %collective-permute-start.2 = (bf16[11,256,256]{2,1,0:T(8,128)(2,1)}, bf16[11,256,256]{2,1,0:T(8,128)(2,1)}, u32[]{:S(2)}, u32[]{:S(2)}) collective-permute-start(bf16[11,256,256]{2,1,0:T(8,128)(2,1)} %collective-permute-done.refs_1_), channel_id=1, source_target_pairs={{0,16},{16,0},{1,17},{17,1},{2,18},{18,2},{3,19},{19,3},{4,20},{20... | collective-permute-start | bytes 4325384 | tf_op jit(solution)/shard_map/ppermute | solution.py:193
  54.7 0.1 pad_add_fusion.place_ref
  54.8 0.7 slice_convert_fusion.meta_ref
  55.5 0.0 collective-permute-done.1.refs_2_
  55.5 2.7 %all-to-all-done.1.refs_4_ = bf16[4,4,4,128,128]{4,3,2,1,0:T(8,128)(2,1)S(1)} async-done(((bf16[4,4,4,128,128]{4,3,2,1,0:T(8,128)(2,1)}), bf16[4,4,4,128,128]{4,3,2,1,0:T(8,128)(2,1)S(1)}, u32[]{:S(2)}, u32[]{:S(2)}) %all-to-all-start.1) | async-done | bytes 2097184 | tf_op jit(solution)/shard_map/all_to_all | solution.py:215
  58.2 0.0 collective-permute-done.2.refs_3_
  58.2 4.5 %shard_map.105 = bf16[2,4,2,2,128,128]{5,4,3,2,1,0:T(8,128)(2,1)S(1)} custom-call(s32[2]{0:T(128)S(1)} %pad_add_fusion.place_ref, s32[4,3,11]{2,1,0:T(4,128)S(1)} %slice_convert_fusion.meta_ref, bf16[11,256,256]{2,1,0:T(8,128)(2,1)S(1)} %bitcast.20, bf16[11,256,256]{2,1,0:T(8,128)(2,1)} %collective-permute-done.refs_1_, ...), custom_call_target="tpu_custom_call" | custom-call | tf_op jit(solution)/shard_map/pallas_call | solution.py:217
  62.7 0.0 copy-start.1
  62.7 0.0 copy-start.3
  62.7 0.0 copy-start.4
  62.8 49.3 %all_to_all.41 = bf16[32,128,128]{2,1,0:T(8,128)(2,1)S(1)} all-to-all(bf16[32,128,128]{2,1,0:T(8,128)(2,1)S(1)} %bitcast.16), channel_id=1, replica_groups=mesh['z_lo'=4,'x'=4,'core'=2,'z_hi'=2,'y_pair'=4,'y_odd'=2] {'core','y_p..., dimensions={0} | all-to-all | bytes 2097152 | tf_op jit(solution)/shard_map/all_to_all | solution.py:229
  112.0 0.0 copy-done.1
  112.0 0.0 copy-done.3
  112.0 0.0 copy-done.4
  112.0 1.0 shard_map.106
  113.0 13.9 %all_to_all.42.parts_ref = bf16[8,72,512]{2,1,0:T(8,128)(2,1)S(1)} all-to-all(bf16[8,72,512]{2,1,0:T(8,128)(2,1)S(1)} %get-tuple-element.12), channel_id=1, replica_groups=mesh['z_lo'=4,'x'=4,'core'=2,'z_hi'=2,'y_pair'=4,'y_odd'=2] {'x','core'}, dimensions={0} | all-to-all | bytes 1179648 | tf_op jit(solution)/shard_map/all_to_all | solution.py:241
  126.9 0.1 shard_map.107
  127.0 11.7 %all_to_all.43.parts_ref = bf16[8,16,512]{2,1,0:T(8,128)(2,1)S(1)} all-to-all(bf16[8,16,512]{2,1,0:T(8,128)(2,1)S(1)} %shard_map.107), channel_id=1, replica_groups=mesh['z_lo'=4,'x'=4,'core'=2,'z_hi'=2,'y_pair'=4,'y_odd'=2] {'y_pair','y..., dimensions={0} | all-to-all | bytes 262144 | tf_op jit(solution)/shard_map/all_to_all | solution.py:243
  138.8 9.5 %all_to_all.44.parts_ref = bf16[8,16,512]{2,1,0:T(8,128)(2,1)S(1)} all-to-all(bf16[8,16,512]{2,1,0:T(8,128)(2,1)S(1)} %shard_map.108), channel_id=1, replica_groups=mesh['z_lo'=4,'x'=4,'core'=2,'z_hi'=2,'y_pair'=4,'y_odd'=2] {'z_lo','z_hi'}, dimensions={0} | all-to-all | bytes 262144 | tf_op jit(solution)/shard_map/all_to_all | solution.py:245
  148.3 10.3 %all_to_all.45.parts_ref = bf16[8,16,512]{2,1,0:T(8,128)(2,1)S(1)} all-to-all(bf16[8,16,512]{2,1,0:T(8,128)(2,1)S(1)} %shard_map.109), channel_id=1, replica_groups=mesh['z_lo'=4,'x'=4,'core'=2,'z_hi'=2,'y_pair'=4,'y_odd'=2] {'y_pair','y..., dimensions={0} | all-to-all | bytes 262144 | tf_op jit(solution)/shard_map/all_to_all | solution.py:247
  158.6 8.1 %all_to_all.46.own_ref = bf16[4,72,512]{2,1,0:T(8,128)(2,1)S(1)} all-to-all(bf16[4,72,512]{2,1,0:T(8,128)(2,1)S(1)} %shard_map.110), channel_id=1, replica_groups=mesh['z_lo'=4,'x'=4,'core'=2,'z_hi'=2,'y_pair'=4,'y_odd'=2] {'x'}, dimensions={0} | all-to-all | bytes 589824 | tf_op jit(solution)/shard_map/all_to_all | solution.py:249
  166.7 8.3 %collective-permute-start.3 = (bf16[4,72,512]{2,1,0:T(8,128)(2,1)S(1)}, bf16[4,72,512]{2,1,0:T(8,128)(2,1)S(1)}, u32[]{:S(2)}, u32[]{:S(2)}) collective-permute-start(bf16[4,72,512]{2,1,0:T(8,128)(2,1)S(1)} %all_to_all.46.own_ref), channel_id=1, source_target_pairs={{0,16},{16,0},{1,17},{17,1},{2,18},{18,2},{3,19},{19,3},{4,20},{20... | collective-permute-start | bytes 884744 | tf_op jit(solution)/shard_map/ppermute | solution.py:193
  175.0 1.2 collective-permute-done.3.other_ref
  176.2 1.6 shard_map.111
  (6 shorter events, 0.1 us)
Async XLA Ops:
  2.1 0.9 copy-start.2
  16.6 2.0 %copy-start.5 = (bf16[4,144,128]{2,1,0:T(8,128)(2,1)}, bf16[4,144,128]{2,1,0:T(8,128)(2,1)S(1)}, u32[]{:S(2)}) copy-start(bf16[4,144,128]{2,1,0:T(8,128)(2,1)S(1)} %all_to_all.40) | copy-start | bytes 442372
  16.6 34.9 %collective-permute-start = (bf16[11,256,256]{2,1,0:T(8,128)(2,1)}, bf16[11,256,256]{2,1,0:T(8,128)(2,1)}, u32[]{:S(2)}, u32[]{:S(2)}) collective-permute-start(bf16[11,256,256]{2,1,0:T(8,128)(2,1)} %bitcast.18), channel_id=1, source_target_pairs={{0,1},{1,0},{2,3},{3,2},{4,5},{5,4},{6,7},{7,6},{8,9},{9,8},{10,11... | collective-permute-start | bytes 4325384 | tf_op jit(solution)/shard_map/ppermute | solution.py:193
  32.5 3.8 %copy-start = (bf16[1,1,11,256,256]{4,3,2,1,0:T(8,128)(2,1)S(1)}, bf16[1,1,11,256,256]{4,3,2,1,0:T(8,128)(2,1)}, u32[]{:S(2)}) copy-start(bf16[1,1,11,256,256]{4,3,2,1,0:T(8,128)(2,1)} %param.12) | copy-start | bytes 4325380
  32.5 25.7 %all-to-all-start.1 = ((bf16[4,4,4,128,128]{4,3,2,1,0:T(8,128)(2,1)}), bf16[4,4,4,128,128]{4,3,2,1,0:T(8,128)(2,1)S(1)}, u32[]{:S(2)}, u32[]{:S(2)}) async-start(bf16[4,4,4,128,128]{4,3,2,1,0:T(8,128)(2,1)} %shard_map.104), calls=%async_computation.1 | async-start | bytes 4194304 | tf_op jit(solution)/shard_map/all_to_all | solution.py:215
  36.3 19.2 %collective-permute-start.1 = (bf16[11,256,256]{2,1,0:T(8,128)(2,1)S(1)}, bf16[11,256,256]{2,1,0:T(8,128)(2,1)}, u32[]{:S(2)}, u32[]{:S(2)}) collective-permute-start(bf16[11,256,256]{2,1,0:T(8,128)(2,1)S(1)} %bitcast.19), channel_id=1, source_target_pairs={{0,16},{16,0},{1,17},{17,1},{2,18},{18,2},{3,19},{19,3},{4,20},{20... | collective-permute-start | bytes 4325384 | tf_op jit(solution)/shard_map/ppermute | solution.py:193
  51.5 6.7 %collective-permute-start.2 = (bf16[11,256,256]{2,1,0:T(8,128)(2,1)}, bf16[11,256,256]{2,1,0:T(8,128)(2,1)}, u32[]{:S(2)}, u32[]{:S(2)}) collective-permute-start(bf16[11,256,256]{2,1,0:T(8,128)(2,1)} %collective-permute-done.refs_1_), channel_id=1, source_target_pairs={{0,16},{16,0},{1,17},{17,1},{2,18},{18,2},{3,19},{19,3},{4,20},{20... | collective-permute-start | bytes 4325384 | tf_op jit(solution)/shard_map/ppermute | solution.py:193
  62.7 49.3 %copy-start.1 = (bf16[512,512]{1,0:T(8,128)(2,1)S(1)}, bf16[512,512]{1,0:T(8,128)(2,1)}, u32[]{:S(2)}) copy-start(bf16[512,512]{1,0:T(8,128)(2,1)} %weight_ref.1) | copy-start | bytes 1572868
  62.7 49.3 %copy-start.3 = (bf16[128,512]{1,0:T(8,128)(2,1)S(1)}, bf16[128,512]{1,0:T(8,128)(2,1)}, u32[]{:S(2)}) copy-start(bf16[128,512]{1,0:T(8,128)(2,1)} %cot_ref.1) | copy-start | bytes 393220
  62.7 49.3 %copy-start.4 = (f32[512]{0:T(512)S(1)}, f32[512]{0:T(512)}, u32[]{:S(2)}) copy-start(f32[512]{0:T(512)} %param.10) | copy-start | bytes 6148
  166.7 9.5 %collective-permute-start.3 = (bf16[4,72,512]{2,1,0:T(8,128)(2,1)S(1)}, bf16[4,72,512]{2,1,0:T(8,128)(2,1)S(1)}, u32[]{:S(2)}, u32[]{:S(2)}) collective-permute-start(bf16[4,72,512]{2,1,0:T(8,128)(2,1)S(1)} %all_to_all.46.own_ref), channel_id=1, source_target_pairs={{0,16},{16,0},{1,17},{17,1},{2,18},{18,2},{3,19},{19,3},{4,20},{20... | collective-permute-start | bytes 884744 | tf_op jit(solution)/shard_map/ppermute | solution.py:193

commit v12 on v11

--- a/solution.py
+++ b/solution.py
@@ -37,27 +37,14 @@
 
 
 def tile_kernel(place_ref, meta_ref, *refs):
-    given, block_ref, out_ref, tiles, total, sems = refs[:4], refs[4], refs[5], refs[6], refs[7], refs[8]
-    _, slots, size, _ = tiles.shape
+    given, block_ref, out_ref, total = refs[:4], refs[4], refs[5], refs[6]
     n_x = block_ref.shape[0]
     core, odd = place_ref[0], place_ref[1]
-
-    def tile_copy(which, slot):
-        return pltpu.make_async_copy(
-            given[which].at[slot], tiles.at[which, slot], sems.at[which, slot]
-        )
 
     def cell_of(which):
         cell_core, cell_odd = (core + which // 2) % 2, (odd + which % 2) % 2
         return cell_core, cell_odd, cell_core * 2 + cell_odd
 
-    for which in range(4):
-
-        def fetch(slot, carry):
-            tile_copy(which, slot).start()
-            return carry
-
-        lax.fori_loop(0, meta_ref[cell_of(which)[2], 2, 0], fetch, 0)
     total[...] = jnp.zeros_like(total)
     for which in range(4):
         cell_core, cell_odd, cell = cell_of(which)
@@ -70,18 +57,12 @@
             window = jnp.concatenate(
                 [block_ref[x, z, cell_odd], block_ref[x, z, 2 + cell_odd]], axis=0
             )
-            return jnp.dot(tiles[which, slot], window, preferred_element_type=F32)
+            return jnp.dot(given[which][slot], window, preferred_element_type=F32)
 
         def step(index, carry):
             slot = 2 * index
             both = slot + 1 < used
             other = jnp.where(both, slot + 1, slot)
-            tile_copy(which, slot).wait()
-
-            @pl.when(both)
-            def _():
-                tile_copy(which, other).wait()
-
             one, two = product(slot), product(other)
             total[cell_core, meta_ref[cell, 0, slot]] += one
             total[cell_core, meta_ref[cell, 0, other]] += jnp.where(both, two, 0.0)
@@ -106,9 +87,15 @@
     return total
 
 
-def repeat_kernel(given_ref, out_ref):
-    for copy in range(out_ref.shape[0]):
-        out_ref[copy] = given_ref[...]
+def repeat_kernel(given_ref, out_ref, sems):
+    copies = [
+        pltpu.make_async_copy(given_ref, out_ref.at[copy], sems.at[copy])
+        for copy in range(out_ref.shape[0])
+    ]
+    for copy in copies:
+        copy.start()
+    for copy in copies:
+        copy.wait()
 
 
 def with_bias(main, row):
@@ -171,14 +158,13 @@
         out_ref[copy] = rows
 
 
-def last_kernel(place_ref, own_ref, other_ref, weight_ref, bias_ref):
-    depth = own_ref.shape[1] - PAIR
-    for chunk in range(own_ref.shape[0]):
-        for core, ref in ((place_ref[0], own_ref), (1 - place_ref[0], other_ref)):
-            rows = pl.ds(pl.multiple_of((chunk * 2 + core) * depth, depth), depth)
-            part = ref[chunk].astype(F32)
-            weight_ref[rows] = part[:depth]
-    bias_ref[...] = bias_of(own_ref[0].astype(F32))
+def last_kernel(parts_ref, weight_ref, bias_ref):
+    depth = parts_ref.shape[1] - PAIR
+    for chunk in range(parts_ref.shape[0]):
+        rows = parts_ref[chunk].astype(F32)
+        weight_ref[chunk * depth : (chunk + 1) * depth] = rows[:depth]
+        if chunk == 0:
+            bias_ref[...] = bias_of(rows)
 
 
 def call(kernel, out, *args, scalars=0):
@@ -211,18 +197,23 @@
     tiles_both = swap(tiles_y, "core")
     meta = quarters[:, nodes : nodes + 3, :slots].astype(jnp.int32)
     near = lax.all_gather(quarters[:, :nodes], "z_lo", axis=0)
-    near = call(repeat_kernel, ((n_x,) + near.shape, BF16), near)
+    near = pl.pallas_call(
+        repeat_kernel,
+        out_shape=jax.ShapeDtypeStruct((n_x,) + near.shape, BF16),
+        in_specs=[VMEM],
+        out_specs=HBM,
+        scratch_shapes=[pltpu.SemaphoreType.DMA((n_x,))],
+        compiler_params=PARAMS,
+    )(near)
     blocks = lax.all_to_all(near, "x", 0, 0)
     place = jnp.stack([lax.axis_index(axis) for axis in QUAD]).astype(jnp.int32)
     term = pl.pallas_call(
         tile_kernel,
         out_shape=jax.ShapeDtypeStruct((2, n_pair, 2, 2, nodes, LANES), BF16),
-        in_specs=[SMEM, SMEM] + [HBM] * 4 + [VMEM],
+        in_specs=[SMEM, SMEM] + [VMEM] * 5,
         out_specs=VMEM,
         scratch_shapes=[
-            pltpu.VMEM((4, slots, size, size), BF16),
             pltpu.VMEM((2, 2 * n_pair, size, LANES), F32),
-            pltpu.SemaphoreType.DMA((4, slots)),
         ],
         compiler_params=PARAMS,
     )(place, meta, tiles, tiles_y, tiles_core, tiles_both, blocks)
@@ -245,15 +236,10 @@
     grads = lax.all_to_all(grads, Z, 0, 0)
     grads = call(sum_kernel, ((n_y, short, width), BF16), grads)
     grads = lax.all_to_all(grads, Y, 0, 0)
-    grads = call(copy_kernel, ((n_x, tall, width), BF16), grads)
-    grads = lax.all_to_all(grads, "x", 0, 0)
+    grads = call(copy_kernel, ((n_near, tall, width), BF16), grads)
+    grads = lax.all_to_all(grads, NEAR, 0, 0)
     weight_grad, bias_grad = call(
-        last_kernel,
-        (((width, width), F32), ((1, width), F32)),
-        place,
-        grads,
-        swap(grads, "core"),
-        scalars=1,
+        last_kernel, (((width, width), F32), ((1, width), F32)), grads
     )
     return activations, weight_grad, bias_grad[0]
 

time: 178 us -> 177 us (level)
  blocking collectives: 129 us -> 138 us
  starting transfers between devices: 23.6 us -> 15.3 us
    all_to_all x1 -> x2, blocking collectives: 13.9 us -> 31.7 us  [per_device(): grads = lax.all_to_all(grads, NEAR, 0, 0)]
    ppermute x4 -> x3, starting transfers between devices: 19.8 us -> 11.6 us  [swap(): return lax.ppermute(array, axis, [(0, 1), (1, 0)])]
    all_to_all x1 -> x0, blocking collectives: 8.07 us -> none  [per_device(): grads = lax.all_to_all(grads, 'x', 0, 0)]
    pallas_call x8 -> x7, Pallas kernels: 4.38 us -> 2.25 us  [call(): pl.pallas_call(kernel, out_shape=shapes, in_specs=[SMEM] * scalars + [VME...]
    ppermute x4 -> x3, waiting for transfers between devices: 10.1 us -> 9.11 us  [swap(): return lax.ppermute(array, axis, [(0, 1), (1, 0)])]
  transfers between devices with their start and end apart: 5 -> 4, of which waited for: 3 -> 2; matrix products, arithmetic and copies ran while one was open for 0% -> 0% of each run, Pallas kernels for 1% -> 1%
where the time goes in v12:
time: 177 us
  blocking collectives  138 us (78%)
  starting transfers between devices  15.3 us (9%)
  waiting for transfers between devices  11.6 us (7%)
  Pallas kernels  7.8 us (4%)
    all_to_all x1, blocking collectives, per_device(): shares = lax.all_to_all(term.reshape(-1, nodes, LANES), HOME, 0, 0)  48.8 us
    all_to_all x2, blocking collectives, per_device(): grads = lax.all_to_all(grads, NEAR, 0, 0)  31.7 us
    all_to_all x2, blocking collectives, per_device(): grads = lax.all_to_all(grads, Y, 0, 0)  22.1 us
    all_to_all x1, blocking collectives, per_device(): quarters = lax.all_to_all(quarters, QUAD, 0, 0)  13.6 us
    all_gather x1, blocking collectives, per_device(): near = lax.all_gather(quarters[:, :nodes], 'z_lo', axis=0)  12.2 us
    ppermute x3, starting transfers between devices, swap(): return lax.ppermute(array, axis, [(0, 1), (1, 0)])  11.6 us
    all_to_all x1, blocking collectives, per_device(): grads = lax.all_to_all(grads, Z, 0, 0)  9.37 us
    ppermute x3, waiting for transfers between devices, swap(): return lax.ppermute(array, axis, [(0, 1), (1, 0)])  9.11 us
  transfers between devices with their start and end apart: 4, of which 2 were waited for; matrix products, arithmetic and copies ran while one was open for 0% of the time, Pallas kernels for 1%

profile of v12, /device:TPU:1, one launch (start us, length us, event | category | flops | bytes accessed | tf_op | source)
XLA Modules:
  0.0 176.5 jit_solution(472037967134370401)
XLA Ops:
  1.3 0.1 pad.8.clone
  1.4 0.7 convert_bitcast_fusion
  2.0 0.1 maximum_maximum_fusion
  2.1 0.0 copy-start.2
  2.1 0.9 copy-done.2
  3.0 13.6 %all_to_all.40 = bf16[4,144,128]{2,1,0:T(8,128)(2,1)S(1)} all-to-all(bf16[4,144,128]{2,1,0:T(8,128)(2,1)S(1)} %shard_map.103), channel_id=1, replica_groups=mesh['z_lo'=4,'x'=4,'core'=2,'z_hi'=2,'y_pair'=4,'y_odd'=2] {'core','y_o..., dimensions={0} | all-to-all | bytes 294912 | tf_op jit(solution)/shard_map/all_to_all | solution.py:193
  16.6 0.0 copy-start.5
  16.6 2.0 %collective-permute-start = (bf16[11,256,256]{2,1,0:T(8,128)(2,1)}, bf16[11,256,256]{2,1,0:T(8,128)(2,1)}, u32[]{:S(2)}, u32[]{:S(2)}) collective-permute-start(bf16[11,256,256]{2,1,0:T(8,128)(2,1)} %bitcast.18), channel_id=1, source_target_pairs={{0,1},{1,0},{2,3},{3,2},{4,5},{5,4},{6,7},{7,6},{8,9},{9,8},{10,11... | collective-permute-start | bytes 4325384 | tf_op jit(solution)/shard_map/ppermute | solution.py:179
  18.6 0.0 copy-done.5
  18.7 12.2 %all-gather = bf16[16,128,128]{2,1,0:T(8,128)(2,1)S(1)} all-gather(bf16[4,128,128]{2,1,0:T(8,128)(2,1)S(1)} %slice.7), channel_id=2, replica_groups=mesh['z_lo'=4,'x'=4,'core'=2,'z_hi'=2,'y_pair'=4,'y_odd'=2] {'z_lo'}, dimensions={0}, use_global_device_ids=true | all-gather | bytes 655360 | tf_op jit(solution)/shard_map/all_gather | solution.py:199
  30.9 1.4 shard_map.104
  32.3 0.0 copy-start
  32.3 3.8 %all-to-all-start.1 = ((bf16[4,4,4,128,128]{4,3,2,1,0:T(8,128)(2,1)}), bf16[4,4,4,128,128]{4,3,2,1,0:T(8,128)(2,1)S(1)}, u32[]{:S(2)}, u32[]{:S(2)}) async-start(bf16[4,4,4,128,128]{4,3,2,1,0:T(8,128)(2,1)} %shard_map.104), calls=%async_computation.1 | async-start | bytes 4194304 | tf_op jit(solution)/shard_map/all_to_all | solution.py:208
  36.1 0.0 copy-done
  36.1 6.3 %collective-permute-start.1 = (bf16[11,256,256]{2,1,0:T(8,128)(2,1)S(1)}, bf16[11,256,256]{2,1,0:T(8,128)(2,1)}, u32[]{:S(2)}, u32[]{:S(2)}) collective-permute-start(bf16[11,256,256]{2,1,0:T(8,128)(2,1)S(1)} %bitcast.19), channel_id=1, source_target_pairs={{0,16},{16,0},{1,17},{17,1},{2,18},{18,2},{3,19},{19,3},{4,20},{20... | collective-permute-start | bytes 4325384 | tf_op jit(solution)/shard_map/ppermute | solution.py:179
  42.4 9.1 %collective-permute-done.refs_1_ = bf16[11,256,256]{2,1,0:T(8,128)(2,1)} collective-permute-done((bf16[11,256,256]{2,1,0:T(8,128)(2,1)}, bf16[11,256,256]{2,1,0:T(8,128)(2,1)}, u32[]{:S(2)}, u32[]{:S(2)}) %collective-permute-start) | collective-permute-done | bytes 1441824 | tf_op jit(solution)/shard_map/ppermute | solution.py:179
  51.5 3.2 %collective-permute-start.2 = (bf16[11,256,256]{2,1,0:T(8,128)(2,1)}, bf16[11,256,256]{2,1,0:T(8,128)(2,1)}, u32[]{:S(2)}, u32[]{:S(2)}) collective-permute-start(bf16[11,256,256]{2,1,0:T(8,128)(2,1)} %collective-permute-done.refs_1_), channel_id=1, source_target_pairs={{0,16},{16,0},{1,17},{17,1},{2,18},{18,2},{3,19},{19,3},{4,20},{20... | collective-permute-start | bytes 4325384 | tf_op jit(solution)/shard_map/ppermute | solution.py:179
  54.7 0.1 pad_add_fusion.place_ref
  54.8 0.7 slice_convert_fusion.meta_ref
  55.5 0.0 collective-permute-done.1.refs_2_
  55.5 2.5 %all-to-all-done.1.refs_4_ = bf16[4,4,4,128,128]{4,3,2,1,0:T(8,128)(2,1)S(1)} async-done(((bf16[4,4,4,128,128]{4,3,2,1,0:T(8,128)(2,1)}), bf16[4,4,4,128,128]{4,3,2,1,0:T(8,128)(2,1)S(1)}, u32[]{:S(2)}, u32[]{:S(2)}) %all-to-all-start.1) | async-done | bytes 2097184 | tf_op jit(solution)/shard_map/all_to_all | solution.py:208
  58.0 0.0 collective-permute-done.2.refs_3_
  58.0 4.2 %shard_map.105 = bf16[2,4,2,2,128,128]{5,4,3,2,1,0:T(8,128)(2,1)S(1)} custom-call(s32[2]{0:T(128)S(1)} %pad_add_fusion.place_ref, s32[4,3,11]{2,1,0:T(4,128)S(1)} %slice_convert_fusion.meta_ref, bf16[11,256,256]{2,1,0:T(8,128)(2,1)S(1)} %bitcast.20, bf16[11,256,256]{2,1,0:T(8,128)(2,1)} %collective-permute-done.refs_1_, ...), custom_call_target="tpu_custom_call" | custom-call | tf_op jit(solution)/shard_map/pallas_call | solution.py:210
  62.2 0.0 copy-start.1
  62.2 0.0 copy-start.3
  62.2 0.0 copy-start.4
  62.2 48.8 %all_to_all.41 = bf16[32,128,128]{2,1,0:T(8,128)(2,1)S(1)} all-to-all(bf16[32,128,128]{2,1,0:T(8,128)(2,1)S(1)} %bitcast.16), channel_id=1, replica_groups=mesh['z_lo'=4,'x'=4,'core'=2,'z_hi'=2,'y_pair'=4,'y_odd'=2] {'core','y_p..., dimensions={0} | all-to-all | bytes 2097152 | tf_op jit(solution)/shard_map/all_to_all | solution.py:220
  111.1 0.0 copy-done.1
  111.1 0.0 copy-done.3
  111.1 0.0 copy-done.4
  111.1 1.0 shard_map.106
  112.1 13.7 %all_to_all.42.parts_ref = bf16[8,72,512]{2,1,0:T(8,128)(2,1)S(1)} all-to-all(bf16[8,72,512]{2,1,0:T(8,128)(2,1)S(1)} %get-tuple-element.12), channel_id=1, replica_groups=mesh['z_lo'=4,'x'=4,'core'=2,'z_hi'=2,'y_pair'=4,'y_odd'=2] {'x','core'}, dimensions={0} | all-to-all | bytes 1179648 | tf_op jit(solution)/shard_map/all_to_all | solution.py:232
  125.8 0.1 shard_map.107
  125.9 11.8 %all_to_all.43.parts_ref = bf16[8,16,512]{2,1,0:T(8,128)(2,1)S(1)} all-to-all(bf16[8,16,512]{2,1,0:T(8,128)(2,1)S(1)} %shard_map.107), channel_id=1, replica_groups=mesh['z_lo'=4,'x'=4,'core'=2,'z_hi'=2,'y_pair'=4,'y_odd'=2] {'y_pair','y..., dimensions={0} | all-to-all | bytes 262144 | tf_op jit(solution)/shard_map/all_to_all | solution.py:234
  137.8 9.4 %all_to_all.44.parts_ref = bf16[8,16,512]{2,1,0:T(8,128)(2,1)S(1)} all-to-all(bf16[8,16,512]{2,1,0:T(8,128)(2,1)S(1)} %shard_map.108), channel_id=1, replica_groups=mesh['z_lo'=4,'x'=4,'core'=2,'z_hi'=2,'y_pair'=4,'y_odd'=2] {'z_lo','z_hi'}, dimensions={0} | all-to-all | bytes 262144 | tf_op jit(solution)/shard_map/all_to_all | solution.py:236
  147.2 10.3 %all_to_all.45.parts_ref = bf16[8,16,512]{2,1,0:T(8,128)(2,1)S(1)} all-to-all(bf16[8,16,512]{2,1,0:T(8,128)(2,1)S(1)} %shard_map.109), channel_id=1, replica_groups=mesh['z_lo'=4,'x'=4,'core'=2,'z_hi'=2,'y_pair'=4,'y_odd'=2] {'y_pair','y..., dimensions={0} | all-to-all | bytes 262144 | tf_op jit(solution)/shard_map/all_to_all | solution.py:238
  157.5 18.0 %all_to_all.46.parts_ref = bf16[8,72,512]{2,1,0:T(8,128)(2,1)S(1)} all-to-all(bf16[8,72,512]{2,1,0:T(8,128)(2,1)S(1)} %shard_map.110), channel_id=1, replica_groups=mesh['z_lo'=4,'x'=4,'core'=2,'z_hi'=2,'y_pair'=4,'y_odd'=2] {'x','core'}, dimensions={0} | all-to-all | bytes 1179648 | tf_op jit(solution)/shard_map/all_to_all | solution.py:240
  175.5 1.0 shard_map.111
  (6 shorter events, 0.1 us)
Async XLA Ops:
  2.1 0.9 copy-start.2
  16.6 2.0 %copy-start.5 = (bf16[4,144,128]{2,1,0:T(8,128)(2,1)}, bf16[4,144,128]{2,1,0:T(8,128)(2,1)S(1)}, u32[]{:S(2)}) copy-start(bf16[4,144,128]{2,1,0:T(8,128)(2,1)S(1)} %all_to_all.40) | copy-start | bytes 442372
  16.6 34.9 %collective-permute-start = (bf16[11,256,256]{2,1,0:T(8,128)(2,1)}, bf16[11,256,256]{2,1,0:T(8,128)(2,1)}, u32[]{:S(2)}, u32[]{:S(2)}) collective-permute-start(bf16[11,256,256]{2,1,0:T(8,128)(2,1)} %bitcast.18), channel_id=1, source_target_pairs={{0,1},{1,0},{2,3},{3,2},{4,5},{5,4},{6,7},{7,6},{8,9},{9,8},{10,11... | collective-permute-start | bytes 4325384 | tf_op jit(solution)/shard_map/ppermute | solution.py:179
  32.3 3.8 %copy-start = (bf16[1,1,11,256,256]{4,3,2,1,0:T(8,128)(2,1)S(1)}, bf16[1,1,11,256,256]{4,3,2,1,0:T(8,128)(2,1)}, u32[]{:S(2)}) copy-start(bf16[1,1,11,256,256]{4,3,2,1,0:T(8,128)(2,1)} %param.12) | copy-start | bytes 4325380
  32.3 25.7 %all-to-all-start.1 = ((bf16[4,4,4,128,128]{4,3,2,1,0:T(8,128)(2,1)}), bf16[4,4,4,128,128]{4,3,2,1,0:T(8,128)(2,1)S(1)}, u32[]{:S(2)}, u32[]{:S(2)}) async-start(bf16[4,4,4,128,128]{4,3,2,1,0:T(8,128)(2,1)} %shard_map.104), calls=%async_computation.1 | async-start | bytes 4194304 | tf_op jit(solution)/shard_map/all_to_all | solution.py:208
  36.1 19.4 %collective-permute-start.1 = (bf16[11,256,256]{2,1,0:T(8,128)(2,1)S(1)}, bf16[11,256,256]{2,1,0:T(8,128)(2,1)}, u32[]{:S(2)}, u32[]{:S(2)}) collective-permute-start(bf16[11,256,256]{2,1,0:T(8,128)(2,1)S(1)} %bitcast.19), channel_id=1, source_target_pairs={{0,16},{16,0},{1,17},{17,1},{2,18},{18,2},{3,19},{19,3},{4,20},{20... | collective-permute-start | bytes 4325384 | tf_op jit(solution)/shard_map/ppermute | solution.py:179
  51.5 6.5 %collective-permute-start.2 = (bf16[11,256,256]{2,1,0:T(8,128)(2,1)}, bf16[11,256,256]{2,1,0:T(8,128)(2,1)}, u32[]{:S(2)}, u32[]{:S(2)}) collective-permute-start(bf16[11,256,256]{2,1,0:T(8,128)(2,1)} %collective-permute-done.refs_1_), channel_id=1, source_target_pairs={{0,16},{16,0},{1,17},{17,1},{2,18},{18,2},{3,19},{19,3},{4,20},{20... | collective-permute-start | bytes 4325384 | tf_op jit(solution)/shard_map/ppermute | solution.py:179
  62.2 48.9 %copy-start.1 = (bf16[512,512]{1,0:T(8,128)(2,1)S(1)}, bf16[512,512]{1,0:T(8,128)(2,1)}, u32[]{:S(2)}) copy-start(bf16[512,512]{1,0:T(8,128)(2,1)} %weight_ref.1) | copy-start | bytes 1572868
  62.2 48.9 %copy-start.3 = (bf16[128,512]{1,0:T(8,128)(2,1)S(1)}, bf16[128,512]{1,0:T(8,128)(2,1)}, u32[]{:S(2)}) copy-start(bf16[128,512]{1,0:T(8,128)(2,1)} %cot_ref.1) | copy-start | bytes 393220
  62.2 48.9 %copy-start.4 = (f32[512]{0:T(512)S(1)}, f32[512]{0:T(512)}, u32[]{:S(2)}) copy-start(f32[512]{0:T(512)} %param.10) | copy-start | bytes 6148

commit v13 on v12

--- a/solution.py
+++ b/solution.py
@@ -88,8 +88,9 @@
 
 
 def repeat_kernel(given_ref, out_ref, sems):
+    given = given_ref.at[:, pl.ds(0, out_ref.shape[2])]
     copies = [
-        pltpu.make_async_copy(given_ref, out_ref.at[copy], sems.at[copy])
+        pltpu.make_async_copy(given, out_ref.at[copy], sems.at[copy])
         for copy in range(out_ref.shape[0])
     ]
     for copy in copies:
@@ -175,6 +176,17 @@
     )(*args)
 
 
+def repeat(array, copies, rows):
+    return pl.pallas_call(
+        repeat_kernel,
+        out_shape=jax.ShapeDtypeStruct((copies, array.shape[0], rows, LANES), BF16),
+        in_specs=[VMEM],
+        out_specs=HBM,
+        scratch_shapes=[pltpu.SemaphoreType.DMA((copies,))],
+        compiler_params=PARAMS,
+    )(array)
+
+
 def swap(array, axis):
     return lax.ppermute(array, axis, [(0, 1), (1, 0)])
 
@@ -196,15 +208,8 @@
     tiles_core = swap(tiles, "core")
     tiles_both = swap(tiles_y, "core")
     meta = quarters[:, nodes : nodes + 3, :slots].astype(jnp.int32)
-    near = lax.all_gather(quarters[:, :nodes], "z_lo", axis=0)
-    near = pl.pallas_call(
-        repeat_kernel,
-        out_shape=jax.ShapeDtypeStruct((n_x,) + near.shape, BF16),
-        in_specs=[VMEM],
-        out_specs=HBM,
-        scratch_shapes=[pltpu.SemaphoreType.DMA((n_x,))],
-        compiler_params=PARAMS,
-    )(near)
+    near = lax.all_to_all(repeat(quarters, n_z, nodes), "z_lo", 0, 0)
+    near = repeat(near.reshape(-1, nodes, LANES), n_x, nodes).reshape((n_x,) + near.shape)
     blocks = lax.all_to_all(near, "x", 0, 0)
     place = jnp.stack([lax.axis_index(axis) for axis in QUAD]).astype(jnp.int32)
     term = pl.pallas_call(

time: 177 us -> 182 us (1.028)
  waiting for transfers between devices: 11.6 us -> 17.5 us
  starting transfers between devices: 15.3 us -> 12.3 us
    all_to_all x0 -> x1, blocking collectives: none -> 16.4 us  [per_device(): near = lax.all_to_all(repeat(quarters, n_z, nodes), 'z_lo', 0, 0)]
    all_gather x1 -> x0, blocking collectives: 12.2 us -> none  [per_device(): near = lax.all_gather(quarters[:, :nodes], 'z_lo', axis=0)]
    all_to_all x1, waiting for transfers between devices: 2.49 us -> 10.5 us  [per_device(): blocks = lax.all_to_all(near, 'x', 0, 0)]
    all_to_all x1, blocking collectives: 48.8 us -> 44.4 us  [per_device(): shares = lax.all_to_all(term.reshape(-1, nodes, LANES), HOME, 0, 0)]
    ppermute x3, starting transfers between devices: 11.6 us -> 8.58 us  [swap(): return lax.ppermute(array, axis, [(0, 1), (1, 0)])]
    ppermute x3, waiting for transfers between devices: 9.11 us -> 7.06 us  [swap(): return lax.ppermute(array, axis, [(0, 1), (1, 0)])]
where the time goes in v13:
time: 182 us
  blocking collectives  139 us (76%)
  waiting for transfers between devices  17.5 us (10%)
  starting transfers between devices  12.3 us (7%)
  Pallas kernels  8.72 us (5%)
    all_to_all x1, blocking collectives, per_device(): shares = lax.all_to_all(term.reshape(-1, nodes, LANES), HOME, 0, 0)  44.4 us
    all_to_all x2, blocking collectives, per_device(): grads = lax.all_to_all(grads, NEAR, 0, 0)  31.8 us
    all_to_all x2, blocking collectives, per_device(): grads = lax.all_to_all(grads, Y, 0, 0)  22.2 us
    all_to_all x1, blocking collectives, per_device(): near = lax.all_to_all(repeat(quarters, n_z, nodes), 'z_lo', 0, 0)  16.4 us
    all_to_all x1, blocking collectives, per_device(): quarters = lax.all_to_all(quarters, QUAD, 0, 0)  13.6 us
    all_to_all x1, waiting for transfers between devices, per_device(): blocks = lax.all_to_all(near, 'x', 0, 0)  10.5 us
    all_to_all x1, blocking collectives, per_device(): grads = lax.all_to_all(grads, Z, 0, 0)  10.2 us
    ppermute x3, starting transfers between devices, swap(): return lax.ppermute(array, axis, [(0, 1), (1, 0)])  8.58 us
  transfers between devices with their start and end apart: 4, of which 2 were waited for; matrix products, arithmetic and copies ran while one was open for 0% of the time, Pallas kernels for 1%

profile of v13, /device:TPU:1, one launch (start us, length us, event | category | flops | bytes accessed | tf_op | source)
XLA Modules:
  0.0 181.8 jit_solution(1754167593999982631)
XLA Ops:
  1.3 0.1 pad.8.clone
  1.4 0.7 convert_bitcast_fusion
  2.0 0.1 maximum_maximum_fusion
  2.1 0.0 copy-start.3
  2.1 0.9 copy-done.3
  3.0 13.6 %all_to_all.45.given_ref = bf16[4,144,128]{2,1,0:T(8,128)(2,1)S(1)} all-to-all(bf16[4,144,128]{2,1,0:T(8,128)(2,1)S(1)} %shard_map.103), channel_id=1, replica_groups=mesh['z_lo'=4,'x'=4,'core'=2,'z_hi'=2,'y_pair'=4,'y_odd'=2] {'core','y_o..., dimensions={0} | all-to-all | bytes 294912 | tf_op jit(solution)/shard_map/all_to_all | solution.py:205
  16.6 2.0 %collective-permute-start = (bf16[11,256,256]{2,1,0:T(8,128)(2,1)}, bf16[11,256,256]{2,1,0:T(8,128)(2,1)}, u32[]{:S(2)}, u32[]{:S(2)}) collective-permute-start(bf16[11,256,256]{2,1,0:T(8,128)(2,1)} %bitcast.19), channel_id=1, source_target_pairs={{0,1},{1,0},{2,3},{3,2},{4,5},{5,4},{6,7},{7,6},{8,9},{9,8},{10,11... | collective-permute-start | bytes 4325384 | tf_op jit(solution)/shard_map/ppermute | solution.py:191
  18.6 0.2 shard_map.104
  18.9 0.0 copy-start.1
  18.9 0.7 copy-done.1
  19.5 16.4 %all_to_all.46 = bf16[4,4,128,128]{3,2,1,0:T(8,128)(2,1)S(1)} all-to-all(bf16[4,4,128,128]{3,2,1,0:T(8,128)(2,1)S(1)} %shard_map.104), channel_id=1, replica_groups=mesh['z_lo'=4,'x'=4,'core'=2,'z_hi'=2,'y_pair'=4,'y_odd'=2] {'z_lo'}, dimensions={0} | all-to-all | bytes 1048576 | tf_op jit(solution)/shard_map/all_to_all | solution.py:211
  35.9 1.4 shard_map.105
  37.3 0.0 copy-start
  37.3 3.8 %all-to-all-start.2 = ((bf16[4,4,4,128,128]{4,3,2,1,0:T(8,128)(2,1)}), bf16[4,4,4,128,128]{4,3,2,1,0:T(8,128)(2,1)S(1)}, u32[]{:S(2)}, u32[]{:S(2)}) async-start(bf16[4,4,4,128,128]{4,3,2,1,0:T(8,128)(2,1)} %bitcast.7), calls=%async_computation.2 | async-start | bytes 4194304 | tf_op jit(solution)/shard_map/all_to_all | solution.py:213
  41.1 0.0 copy-done
  41.1 3.3 %collective-permute-start.1 = (bf16[11,256,256]{2,1,0:T(8,128)(2,1)S(1)}, bf16[11,256,256]{2,1,0:T(8,128)(2,1)}, u32[]{:S(2)}, u32[]{:S(2)}) collective-permute-start(bf16[11,256,256]{2,1,0:T(8,128)(2,1)S(1)} %bitcast.20), channel_id=1, source_target_pairs={{0,16},{16,0},{1,17},{17,1},{2,18},{18,2},{3,19},{19,3},{4,20},{20... | collective-permute-start | bytes 4325384 | tf_op jit(solution)/shard_map/ppermute | solution.py:191
  44.4 7.1 %collective-permute-done.refs_1_ = bf16[11,256,256]{2,1,0:T(8,128)(2,1)} collective-permute-done((bf16[11,256,256]{2,1,0:T(8,128)(2,1)}, bf16[11,256,256]{2,1,0:T(8,128)(2,1)}, u32[]{:S(2)}, u32[]{:S(2)}) %collective-permute-start) | collective-permute-done | bytes 1441824 | tf_op jit(solution)/shard_map/ppermute | solution.py:191
  51.5 3.2 %collective-permute-start.2 = (bf16[11,256,256]{2,1,0:T(8,128)(2,1)}, bf16[11,256,256]{2,1,0:T(8,128)(2,1)}, u32[]{:S(2)}, u32[]{:S(2)}) collective-permute-start(bf16[11,256,256]{2,1,0:T(8,128)(2,1)} %collective-permute-done.refs_1_), channel_id=1, source_target_pairs={{0,16},{16,0},{1,17},{17,1},{2,18},{18,2},{3,19},{19,3},{4,20},{20... | collective-permute-start | bytes 4325384 | tf_op jit(solution)/shard_map/ppermute | solution.py:191
  54.7 0.1 pad_add_fusion.place_ref
  54.8 0.7 slice_convert_fusion.meta_ref
  55.5 0.0 collective-permute-done.1.refs_2_
  55.5 10.5 %all-to-all-done.2.refs_4_ = bf16[4,4,4,128,128]{4,3,2,1,0:T(8,128)(2,1)S(1)} async-done(((bf16[4,4,4,128,128]{4,3,2,1,0:T(8,128)(2,1)}), bf16[4,4,4,128,128]{4,3,2,1,0:T(8,128)(2,1)S(1)}, u32[]{:S(2)}, u32[]{:S(2)}) %all-to-all-start.2) | async-done | bytes 2097184 | tf_op jit(solution)/shard_map/all_to_all | solution.py:213
  66.0 0.0 collective-permute-done.2.refs_3_
  66.0 4.9 %shard_map.106 = bf16[2,4,2,2,128,128]{5,4,3,2,1,0:T(8,128)(2,1)S(1)} custom-call(s32[2]{0:T(128)S(1)} %pad_add_fusion.place_ref, s32[4,3,11]{2,1,0:T(4,128)S(1)} %slice_convert_fusion.meta_ref, bf16[11,256,256]{2,1,0:T(8,128)(2,1)S(1)} %bitcast.21, bf16[11,256,256]{2,1,0:T(8,128)(2,1)} %collective-permute-done.refs_1_, ...), custom_call_target="tpu_custom_call" | custom-call | tf_op jit(solution)/shard_map/pallas_call | solution.py:215
  70.9 0.0 copy-start.2
  70.9 0.0 copy-start.4
  70.9 0.0 copy-start.5
  70.9 44.4 %all_to_all.47 = bf16[32,128,128]{2,1,0:T(8,128)(2,1)S(1)} all-to-all(bf16[32,128,128]{2,1,0:T(8,128)(2,1)S(1)} %bitcast.17), channel_id=1, replica_groups=mesh['z_lo'=4,'x'=4,'core'=2,'z_hi'=2,'y_pair'=4,'y_odd'=2] {'core','y_p..., dimensions={0} | all-to-all | bytes 2097152 | tf_op jit(solution)/shard_map/all_to_all | solution.py:225
  115.3 0.0 copy-done.2
  115.3 0.0 copy-done.4
  115.3 0.0 copy-done.5
  115.3 1.0 shard_map.107
  116.3 13.8 %all_to_all.48.parts_ref = bf16[8,72,512]{2,1,0:T(8,128)(2,1)S(1)} all-to-all(bf16[8,72,512]{2,1,0:T(8,128)(2,1)S(1)} %get-tuple-element.12), channel_id=1, replica_groups=mesh['z_lo'=4,'x'=4,'core'=2,'z_hi'=2,'y_pair'=4,'y_odd'=2] {'x','core'}, dimensions={0} | all-to-all | bytes 1179648 | tf_op jit(solution)/shard_map/all_to_all | solution.py:237
  130.1 0.1 shard_map.108
  130.2 11.9 %all_to_all.49.parts_ref = bf16[8,16,512]{2,1,0:T(8,128)(2,1)S(1)} all-to-all(bf16[8,16,512]{2,1,0:T(8,128)(2,1)S(1)} %shard_map.108), channel_id=1, replica_groups=mesh['z_lo'=4,'x'=4,'core'=2,'z_hi'=2,'y_pair'=4,'y_odd'=2] {'y_pair','y..., dimensions={0} | all-to-all | bytes 262144 | tf_op jit(solution)/shard_map/all_to_all | solution.py:239
  142.2 10.2 %all_to_all.50.parts_ref = bf16[8,16,512]{2,1,0:T(8,128)(2,1)S(1)} all-to-all(bf16[8,16,512]{2,1,0:T(8,128)(2,1)S(1)} %shard_map.109), channel_id=1, replica_groups=mesh['z_lo'=4,'x'=4,'core'=2,'z_hi'=2,'y_pair'=4,'y_odd'=2] {'z_lo','z_hi'}, dimensions={0} | all-to-all | bytes 262144 | tf_op jit(solution)/shard_map/all_to_all | solution.py:241
  152.4 10.3 %all_to_all.51.parts_ref = bf16[8,16,512]{2,1,0:T(8,128)(2,1)S(1)} all-to-all(bf16[8,16,512]{2,1,0:T(8,128)(2,1)S(1)} %shard_map.110), channel_id=1, replica_groups=mesh['z_lo'=4,'x'=4,'core'=2,'z_hi'=2,'y_pair'=4,'y_odd'=2] {'y_pair','y..., dimensions={0} | all-to-all | bytes 262144 | tf_op jit(solution)/shard_map/all_to_all | solution.py:243
  162.7 18.0 %all_to_all.52.parts_ref = bf16[8,72,512]{2,1,0:T(8,128)(2,1)S(1)} all-to-all(bf16[8,72,512]{2,1,0:T(8,128)(2,1)S(1)} %shard_map.111), channel_id=1, replica_groups=mesh['z_lo'=4,'x'=4,'core'=2,'z_hi'=2,'y_pair'=4,'y_odd'=2] {'x','core'}, dimensions={0} | all-to-all | bytes 1179648 | tf_op jit(solution)/shard_map/all_to_all | solution.py:245
  180.7 1.0 shard_map.112
  (5 shorter events, 0.1 us)
Async XLA Ops:
  2.1 0.9 copy-start.3
  16.6 34.9 %collective-permute-start = (bf16[11,256,256]{2,1,0:T(8,128)(2,1)}, bf16[11,256,256]{2,1,0:T(8,128)(2,1)}, u32[]{:S(2)}, u32[]{:S(2)}) collective-permute-start(bf16[11,256,256]{2,1,0:T(8,128)(2,1)} %bitcast.19), channel_id=1, source_target_pairs={{0,1},{1,0},{2,3},{3,2},{4,5},{5,4},{6,7},{7,6},{8,9},{9,8},{10,11... | collective-permute-start | bytes 4325384 | tf_op jit(solution)/shard_map/ppermute | solution.py:191
  18.9 0.7 copy-start.1
  37.3 3.8 %copy-start = (bf16[1,1,11,256,256]{4,3,2,1,0:T(8,128)(2,1)S(1)}, bf16[1,1,11,256,256]{4,3,2,1,0:T(8,128)(2,1)}, u32[]{:S(2)}) copy-start(bf16[1,1,11,256,256]{4,3,2,1,0:T(8,128)(2,1)} %param.12) | copy-start | bytes 4325380
  37.3 28.6 %all-to-all-start.2 = ((bf16[4,4,4,128,128]{4,3,2,1,0:T(8,128)(2,1)}), bf16[4,4,4,128,128]{4,3,2,1,0:T(8,128)(2,1)S(1)}, u32[]{:S(2)}, u32[]{:S(2)}) async-start(bf16[4,4,4,128,128]{4,3,2,1,0:T(8,128)(2,1)} %bitcast.7), calls=%async_computation.2 | async-start | bytes 4194304 | tf_op jit(solution)/shard_map/all_to_all | solution.py:213
  41.1 14.4 %collective-permute-start.1 = (bf16[11,256,256]{2,1,0:T(8,128)(2,1)S(1)}, bf16[11,256,256]{2,1,0:T(8,128)(2,1)}, u32[]{:S(2)}, u32[]{:S(2)}) collective-permute-start(bf16[11,256,256]{2,1,0:T(8,128)(2,1)S(1)} %bitcast.20), channel_id=1, source_target_pairs={{0,16},{16,0},{1,17},{17,1},{2,18},{18,2},{3,19},{19,3},{4,20},{20... | collective-permute-start | bytes 4325384 | tf_op jit(solution)/shard_map/ppermute | solution.py:191
  51.5 14.5 %collective-permute-start.2 = (bf16[11,256,256]{2,1,0:T(8,128)(2,1)}, bf16[11,256,256]{2,1,0:T(8,128)(2,1)}, u32[]{:S(2)}, u32[]{:S(2)}) collective-permute-start(bf16[11,256,256]{2,1,0:T(8,128)(2,1)} %collective-permute-done.refs_1_), channel_id=1, source_target_pairs={{0,16},{16,0},{1,17},{17,1},{2,18},{18,2},{3,19},{19,3},{4,20},{20... | collective-permute-start | bytes 4325384 | tf_op jit(solution)/shard_map/ppermute | solution.py:191
  70.9 44.5 %copy-start.2 = (bf16[512,512]{1,0:T(8,128)(2,1)S(1)}, bf16[512,512]{1,0:T(8,128)(2,1)}, u32[]{:S(2)}) copy-start(bf16[512,512]{1,0:T(8,128)(2,1)} %weight_ref.1) | copy-start | bytes 1572868
  70.9 44.4 %copy-start.4 = (bf16[128,512]{1,0:T(8,128)(2,1)S(1)}, bf16[128,512]{1,0:T(8,128)(2,1)}, u32[]{:S(2)}) copy-start(bf16[128,512]{1,0:T(8,128)(2,1)} %cot_ref.1) | copy-start | bytes 393220
  70.9 44.4 %copy-start.5 = (f32[512]{0:T(512)S(1)}, f32[512]{0:T(512)}, u32[]{:S(2)}) copy-start(f32[512]{0:T(512)} %param.10) | copy-start | bytes 6148

commit v14 on v12

--- a/solution.py
+++ b/solution.py
@@ -218,7 +218,7 @@
         compiler_params=PARAMS,
     )(place, meta, tiles, tiles_y, tiles_core, tiles_both, blocks)
     shares = lax.all_to_all(term.reshape(-1, nodes, LANES), HOME, 0, 0)
-    n_near, n_y, n_deep = lax.axis_size(NEAR), lax.axis_size(Y), lax.axis_size(Z)
+    n_near, n_y = lax.axis_size(NEAR), lax.axis_size(Y)
     depth = width // n_near
     tall, short = depth + PAIR, depth // n_y + PAIR
     activations, grads = call(
@@ -232,12 +232,12 @@
     grads = lax.all_to_all(grads, NEAR, 0, 0)
     grads = call(scatter_kernel, ((n_y, short, width), BF16), grads)
     grads = lax.all_to_all(grads, Y, 0, 0)
-    grads = call(sum_kernel, ((n_deep, short, width), BF16), grads)
-    grads = lax.all_to_all(grads, Z, 0, 0)
-    grads = call(sum_kernel, ((n_y, short, width), BF16), grads)
-    grads = lax.all_to_all(grads, Y, 0, 0)
-    grads = call(copy_kernel, ((n_near, tall, width), BF16), grads)
-    grads = lax.all_to_all(grads, NEAR, 0, 0)
+    grads = call(sum_kernel, ((1, short, width), BF16), grads)
+    grads = lax.all_gather(grads[0], Z, axis=0)
+    grads = call(sum_kernel, ((1, short, width), BF16), grads)
+    grads = lax.all_gather(grads[0], Y, axis=0)
+    grads = call(copy_kernel, ((1, tall, width), BF16), grads)
+    grads = lax.all_gather(grads[0], NEAR, axis=0)
     weight_grad, bias_grad = call(
         last_kernel, (((width, width), F32), ((1, width), F32)), grads
     )

time: 177 us -> 215 us (1.21)
  blocking collectives: 138 us -> 176 us
    all_gather x0 -> x3, blocking collectives: none -> 75.4 us  [the longest x1 29.3 us: per_device(): grads = lax.all_gather(grads[0], Z, axis=0)]
    all_to_all x2 -> x1, blocking collectives: 31.7 us -> 13.9 us  [per_device(): grads = lax.all_to_all(grads, NEAR, 0, 0)]
    all_to_all x2 -> x1, blocking collectives: 22.1 us -> 12 us  [per_device(): grads = lax.all_to_all(grads, Y, 0, 0)]
    all_to_all x1 -> x0, blocking collectives: 9.37 us -> none  [per_device(): grads = lax.all_to_all(grads, Z, 0, 0)]
where the time goes in v14:
time: 215 us; the launch traced here: 214 us
  blocking collectives  176 us (82%)
  starting transfers between devices  15.3 us (7%)
  waiting for transfers between devices  11.6 us (5%)
  Pallas kernels  7.29 us (3%)
    all_to_all x1, blocking collectives, per_device(): shares = lax.all_to_all(term.reshape(-1, nodes, LANES), HOME, 0, 0)  49.1 us
    all_gather x1, blocking collectives, per_device(): grads = lax.all_gather(grads[0], Z, axis=0)  29.3 us
    all_gather x1, blocking collectives, per_device(): grads = lax.all_gather(grads[0], NEAR, axis=0)  27.8 us
    all_gather x1, blocking collectives, per_device(): grads = lax.all_gather(grads[0], Y, axis=0)  18.2 us
    all_to_all x1, blocking collectives, per_device(): grads = lax.all_to_all(grads, NEAR, 0, 0)  13.9 us
    all_to_all x1, blocking collectives, per_device(): quarters = lax.all_to_all(quarters, QUAD, 0, 0)  13.6 us
    all_gather x1, blocking collectives, per_device(): near = lax.all_gather(quarters[:, :nodes], 'z_lo', axis=0)  12.2 us
    all_to_all x1, blocking collectives, per_device(): grads = lax.all_to_all(grads, Y, 0, 0)  12 us
  transfers between devices with their start and end apart: 4, of which 2 were waited for; matrix products, arithmetic and copies ran while one was open for 0% of the time, Pallas kernels for 1%

profile of v14, /device:TPU:1, one launch (start us, length us, event | category | flops | bytes accessed | tf_op | source)
XLA Modules:
  0.0 214.3 jit_solution(1621103572381588804)
XLA Ops:
  1.3 0.1 pad.8.clone
  1.4 0.7 convert_bitcast_fusion
  2.0 0.1 maximum_maximum_fusion
  2.1 0.0 copy-start.2
  2.1 0.9 copy-done.2
  3.0 13.6 %all_to_all.25 = bf16[4,144,128]{2,1,0:T(8,128)(2,1)S(1)} all-to-all(bf16[4,144,128]{2,1,0:T(8,128)(2,1)S(1)} %shard_map.103), channel_id=1, replica_groups=mesh['z_lo'=4,'x'=4,'core'=2,'z_hi'=2,'y_pair'=4,'y_odd'=2] {'core','y_o..., dimensions={0} | all-to-all | bytes 294912 | tf_op jit(solution)/shard_map/all_to_all | solution.py:193
  16.6 0.0 copy-start.5
  16.6 2.0 collective-permute-start
  18.6 0.0 copy-done.5
  18.7 12.2 %all-gather = bf16[16,128,128]{2,1,0:T(8,128)(2,1)S(1)} all-gather(bf16[4,128,128]{2,1,0:T(8,128)(2,1)S(1)} %slice.7), channel_id=2, replica_groups=mesh['z_lo'=4,'x'=4,'core'=2,'z_hi'=2,'y_pair'=4,'y_odd'=2] {'z_lo'}, dimensions={0}, use_global_device_ids=true | all-gather | bytes 655360 | tf_op jit(solution)/shard_map/all_gather | solution.py:199
  30.9 1.4 shard_map.104
  32.3 0.0 copy-start
  32.3 3.8 %all-to-all-start.1 = ((bf16[4,4,4,128,128]{4,3,2,1,0:T(8,128)(2,1)}), bf16[4,4,4,128,128]{4,3,2,1,0:T(8,128)(2,1)S(1)}, u32[]{:S(2)}, u32[]{:S(2)}) async-start(bf16[4,4,4,128,128]{4,3,2,1,0:T(8,128)(2,1)} %shard_map.104), calls=%async_computation.1 | async-start | bytes 4194304 | tf_op jit(solution)/shard_map/all_to_all | solution.py:208
  36.1 0.0 copy-done
  36.1 6.3 %collective-permute-start.1 = (bf16[11,256,256]{2,1,0:T(8,128)(2,1)S(1)}, bf16[11,256,256]{2,1,0:T(8,128)(2,1)}, u32[]{:S(2)}, u32[]{:S(2)}) collective-permute-start(bf16[11,256,256]{2,1,0:T(8,128)(2,1)S(1)} %bitcast.19), channel_id=1, source_target_pairs={{0,16},{16,0},{1,17},{17,1},{2,18},{18,2},{3,19},{19,3},{4,20},{20... | collective-permute-start | bytes 4325384 | tf_op jit(solution)/shard_map/ppermute | solution.py:179
  42.4 9.1 %collective-permute-done.refs_1_ = bf16[11,256,256]{2,1,0:T(8,128)(2,1)} collective-permute-done((bf16[11,256,256]{2,1,0:T(8,128)(2,1)}, bf16[11,256,256]{2,1,0:T(8,128)(2,1)}, u32[]{:S(2)}, u32[]{:S(2)}) %collective-permute-start) | collective-permute-done | bytes 1441824 | tf_op jit(solution)/shard_map/ppermute | solution.py:179
  51.5 3.2 %collective-permute-start.2 = (bf16[11,256,256]{2,1,0:T(8,128)(2,1)}, bf16[11,256,256]{2,1,0:T(8,128)(2,1)}, u32[]{:S(2)}, u32[]{:S(2)}) collective-permute-start(bf16[11,256,256]{2,1,0:T(8,128)(2,1)} %collective-permute-done.refs_1_), channel_id=1, source_target_pairs={{0,16},{16,0},{1,17},{17,1},{2,18},{18,2},{3,19},{19,3},{4,20},{20... | collective-permute-start | bytes 4325384 | tf_op jit(solution)/shard_map/ppermute | solution.py:179
  54.7 0.1 pad_add_fusion.place_ref
  54.8 0.7 slice_convert_fusion.meta_ref
  55.5 0.0 collective-permute-done.1.refs_2_
  55.5 2.5 %all-to-all-done.1.refs_4_ = bf16[4,4,4,128,128]{4,3,2,1,0:T(8,128)(2,1)S(1)} async-done(((bf16[4,4,4,128,128]{4,3,2,1,0:T(8,128)(2,1)}), bf16[4,4,4,128,128]{4,3,2,1,0:T(8,128)(2,1)S(1)}, u32[]{:S(2)}, u32[]{:S(2)}) %all-to-all-start.1) | async-done | bytes 2097184 | tf_op jit(solution)/shard_map/all_to_all | solution.py:208
  58.0 0.0 collective-permute-done.2.refs_3_
  58.0 3.7 %shard_map.105 = bf16[2,4,2,2,128,128]{5,4,3,2,1,0:T(8,128)(2,1)S(1)} custom-call(s32[2]{0:T(128)S(1)} %pad_add_fusion.place_ref, s32[4,3,11]{2,1,0:T(4,128)S(1)} %slice_convert_fusion.meta_ref, bf16[11,256,256]{2,1,0:T(8,128)(2,1)S(1)} %bitcast.20, bf16[11,256,256]{2,1,0:T(8,128)(2,1)} %collective-permute-done.refs_1_, ...), custom_call_target="tpu_custom_call" | custom-call | tf_op jit(solution)/shard_map/pallas_call | solution.py:210
  61.7 0.0 copy-start.1
  61.7 0.0 copy-start.3
  61.7 0.0 copy-start.4
  61.8 49.1 %all_to_all.26 = bf16[32,128,128]{2,1,0:T(8,128)(2,1)S(1)} all-to-all(bf16[32,128,128]{2,1,0:T(8,128)(2,1)S(1)} %bitcast.16), channel_id=1, replica_groups=mesh['z_lo'=4,'x'=4,'core'=2,'z_hi'=2,'y_pair'=4,'y_odd'=2] {'core','y_p..., dimensions={0} | all-to-all | bytes 2097152 | tf_op jit(solution)/shard_map/all_to_all | solution.py:220
  110.8 0.0 copy-done.1
  110.8 0.0 copy-done.3
  110.9 0.0 copy-done.4
  110.9 1.0 shard_map.106
  111.9 13.9 %all_to_all.27.parts_ref = bf16[8,72,512]{2,1,0:T(8,128)(2,1)S(1)} all-to-all(bf16[8,72,512]{2,1,0:T(8,128)(2,1)S(1)} %get-tuple-element.12), channel_id=1, replica_groups=mesh['z_lo'=4,'x'=4,'core'=2,'z_hi'=2,'y_pair'=4,'y_odd'=2] {'x','core'}, dimensions={0} | all-to-all | bytes 1179648 | tf_op jit(solution)/shard_map/all_to_all | solution.py:232
  125.8 0.1 shard_map.107
  125.9 12.0 %all_to_all.28.parts_ref = bf16[8,16,512]{2,1,0:T(8,128)(2,1)S(1)} all-to-all(bf16[8,16,512]{2,1,0:T(8,128)(2,1)S(1)} %shard_map.107), channel_id=1, replica_groups=mesh['z_lo'=4,'x'=4,'core'=2,'z_hi'=2,'y_pair'=4,'y_odd'=2] {'y_pair','y..., dimensions={0} | all-to-all | bytes 262144 | tf_op jit(solution)/shard_map/all_to_all | solution.py:234
  137.9 29.3 %all_gather.17.parts_ref = bf16[8,16,512]{2,1,0:T(8,128)(2,1)S(1)} all-gather(bf16[1,16,512]{2,1,0:T(8,128)(2,1)S(1)} %shard_map.108), channel_id=1, replica_groups=mesh['z_lo'=4,'x'=4,'core'=2,'z_hi'=2,'y_pair'=4,'y_odd'=2] {'z_lo','z_hi'}, dimensions={0}, use_global_device_ids=true | all-gather | bytes 147456 | tf_op jit(solution)/shard_map/all_gather | solution.py:236
  167.2 18.2 %all_gather.18.parts_ref = bf16[8,16,512]{2,1,0:T(8,128)(2,1)S(1)} all-gather(bf16[1,16,512]{2,1,0:T(8,128)(2,1)S(1)} %shard_map.109), channel_id=1, replica_groups=mesh['z_lo'=4,'x'=4,'core'=2,'z_hi'=2,'y_pair'=4,'y_odd'=2] {'y_pair','y..., dimensions={0}, use_global_device_ids=true | all-gather | bytes 147456 | tf_op jit(solution)/shard_map/all_gather | solution.py:238
  185.5 27.8 %all_gather.19.parts_ref = bf16[8,72,512]{2,1,0:T(8,128)(2,1)S(1)} all-gather(bf16[1,72,512]{2,1,0:T(8,128)(2,1)S(1)} %shard_map.110), channel_id=1, replica_groups=mesh['z_lo'=4,'x'=4,'core'=2,'z_hi'=2,'y_pair'=4,'y_odd'=2] {'x','core'}, dimensions={0}, use_global_device_ids=true | all-gather | bytes 663552 | tf_op jit(solution)/shard_map/all_gather | solution.py:240
  213.3 1.0 shard_map.111
  (6 shorter events, 0.1 us)
Async XLA Ops:
  2.1 0.9 copy-start.2
  16.6 2.0 copy-start.5
  16.6 34.9 %collective-permute-start = (bf16[11,256,256]{2,1,0:T(8,128)(2,1)}, bf16[11,256,256]{2,1,0:T(8,128)(2,1)}, u32[]{:S(2)}, u32[]{:S(2)}) collective-permute-start(bf16[11,256,256]{2,1,0:T(8,128)(2,1)} %bitcast.18), channel_id=1, source_target_pairs={{0,1},{1,0},{2,3},{3,2},{4,5},{5,4},{6,7},{7,6},{8,9},{9,8},{10,11... | collective-permute-start | bytes 4325384 | tf_op jit(solution)/shard_map/ppermute | solution.py:179
  32.3 3.8 %copy-start = (bf16[1,1,11,256,256]{4,3,2,1,0:T(8,128)(2,1)S(1)}, bf16[1,1,11,256,256]{4,3,2,1,0:T(8,128)(2,1)}, u32[]{:S(2)}) copy-start(bf16[1,1,11,256,256]{4,3,2,1,0:T(8,128)(2,1)} %param.12) | copy-start | bytes 4325380
  32.3 25.7 %all-to-all-start.1 = ((bf16[4,4,4,128,128]{4,3,2,1,0:T(8,128)(2,1)}), bf16[4,4,4,128,128]{4,3,2,1,0:T(8,128)(2,1)S(1)}, u32[]{:S(2)}, u32[]{:S(2)}) async-start(bf16[4,4,4,128,128]{4,3,2,1,0:T(8,128)(2,1)} %shard_map.104), calls=%async_computation.1 | async-start | bytes 4194304 | tf_op jit(solution)/shard_map/all_to_all | solution.py:208
  36.1 19.4 %collective-permute-start.1 = (bf16[11,256,256]{2,1,0:T(8,128)(2,1)S(1)}, bf16[11,256,256]{2,1,0:T(8,128)(2,1)}, u32[]{:S(2)}, u32[]{:S(2)}) collective-permute-start(bf16[11,256,256]{2,1,0:T(8,128)(2,1)S(1)} %bitcast.19), channel_id=1, source_target_pairs={{0,16},{16,0},{1,17},{17,1},{2,18},{18,2},{3,19},{19,3},{4,20},{20... | collective-permute-start | bytes 4325384 | tf_op jit(solution)/shard_map/ppermute | solution.py:179
  51.5 6.5 %collective-permute-start.2 = (bf16[11,256,256]{2,1,0:T(8,128)(2,1)}, bf16[11,256,256]{2,1,0:T(8,128)(2,1)}, u32[]{:S(2)}, u32[]{:S(2)}) collective-permute-start(bf16[11,256,256]{2,1,0:T(8,128)(2,1)} %collective-permute-done.refs_1_), channel_id=1, source_target_pairs={{0,16},{16,0},{1,17},{17,1},{2,18},{18,2},{3,19},{19,3},{4,20},{20... | collective-permute-start | bytes 4325384 | tf_op jit(solution)/shard_map/ppermute | solution.py:179
  61.7 49.1 %copy-start.1 = (bf16[512,512]{1,0:T(8,128)(2,1)S(1)}, bf16[512,512]{1,0:T(8,128)(2,1)}, u32[]{:S(2)}) copy-start(bf16[512,512]{1,0:T(8,128)(2,1)} %weight_ref.1) | copy-start | bytes 1572868
  61.7 49.1 %copy-start.3 = (bf16[128,512]{1,0:T(8,128)(2,1)S(1)}, bf16[128,512]{1,0:T(8,128)(2,1)}, u32[]{:S(2)}) copy-start(bf16[128,512]{1,0:T(8,128)(2,1)} %cot_ref.1) | copy-start | bytes 393220
  61.7 49.1 %copy-start.4 = (f32[512]{0:T(512)S(1)}, f32[512]{0:T(512)}, u32[]{:S(2)}) copy-start(f32[512]{0:T(512)} %param.10) | copy-start | bytes 6148

commit v15 on v12

--- a/solution.py
+++ b/solution.py
@@ -136,24 +136,39 @@
         grads_ref[chunk] = with_bias(product[chunk * depth : (chunk + 1) * depth], row)
 
 
+def beside_bias(main, bias):
+    high = bias.astype(BF16).astype(F32)
+    side = jnp.concatenate([high, bias - high], axis=0)
+    return jnp.concatenate([main, side], axis=1).astype(BF16)
+
+
 def scatter_kernel(parts_ref, out_ref):
     total = add(parts_ref)
-    depth = out_ref.shape[1] - PAIR
+    depth, width = out_ref.shape[1], parts_ref.shape[2]
+    row = bias_of(total)
+    bias = jnp.concatenate([row[:, lanes_of(part)] for part in range(width // LANES)], axis=0)
     for chunk in range(out_ref.shape[0]):
-        out_ref[chunk] = with_bias(total[chunk * depth : (chunk + 1) * depth], bias_of(total))
+        out_ref[chunk] = beside_bias(total[chunk * depth : (chunk + 1) * depth], bias)
 
 
 def sum_kernel(parts_ref, out_ref):
     total = add(parts_ref)
-    rounded = with_bias(total[: total.shape[0] - PAIR], bias_of(total))
+    width = total.shape[1] - LANES
+    side = total[:, width:]
+    half = side.shape[0] // 2
+    rounded = beside_bias(total[:, :width], side[:half] + side[half:])
     for copy in range(out_ref.shape[0]):
         out_ref[copy] = rounded
 
 
 def copy_kernel(parts_ref, out_ref):
-    depth = parts_ref.shape[1] - PAIR
+    width = out_ref.shape[2]
     parts = [parts_ref[part].astype(F32) for part in range(parts_ref.shape[0])]
-    rows = jnp.concatenate([part[:depth] for part in parts] + [parts[0][depth:]], axis=0).astype(BF16)
+    side = parts[0][:, width:]
+    half = side.shape[0] // 2
+    bias = side[:half] + side[half:]
+    row = jnp.concatenate([bias[part : part + 1] for part in range(half)], axis=1)
+    rows = with_bias(jnp.concatenate([part[:, :width] for part in parts], axis=0), row)
     for copy in range(out_ref.shape[0]):
         out_ref[copy] = rows
 
@@ -220,7 +235,7 @@
     shares = lax.all_to_all(term.reshape(-1, nodes, LANES), HOME, 0, 0)
     n_near, n_y, n_deep = lax.axis_size(NEAR), lax.axis_size(Y), lax.axis_size(Z)
     depth = width // n_near
-    tall, short = depth + PAIR, depth // n_y + PAIR
+    tall, wide = depth + PAIR, width + LANES
     activations, grads = call(
         node_kernel,
         (((nodes, width), BF16), ((n_near, tall, width), BF16)),
@@ -230,11 +245,11 @@
         cotangent,
     )
     grads = lax.all_to_all(grads, NEAR, 0, 0)
-    grads = call(scatter_kernel, ((n_y, short, width), BF16), grads)
+    grads = call(scatter_kernel, ((n_y, depth // n_y, wide), BF16), grads)
     grads = lax.all_to_all(grads, Y, 0, 0)
-    grads = call(sum_kernel, ((n_deep, short, width), BF16), grads)
+    grads = call(sum_kernel, ((n_deep, depth // n_y, wide), BF16), grads)
     grads = lax.all_to_all(grads, Z, 0, 0)
-    grads = call(sum_kernel, ((n_y, short, width), BF16), grads)
+    grads = call(sum_kernel, ((n_y, depth // n_y, wide), BF16), grads)
     grads = lax.all_to_all(grads, Y, 0, 0)
     grads = call(copy_kernel, ((n_near, tall, width), BF16), grads)
     grads = lax.all_to_all(grads, NEAR, 0, 0)

time: 177 us -> 176 us (level)
  blocking collectives: 138 us -> 136 us
where the time goes in v15:
time: 176 us; the launch traced here: 175 us
  blocking collectives  136 us (77%)
  starting transfers between devices  15.3 us (9%)
  waiting for transfers between devices  11.6 us (7%)
  Pallas kernels  8.02 us (5%)
    all_to_all x1, blocking collectives, per_device(): shares = lax.all_to_all(term.reshape(-1, nodes, LANES), HOME, 0, 0)  49.1 us
    all_to_all x2, blocking collectives, per_device(): grads = lax.all_to_all(grads, NEAR, 0, 0)  30.9 us
    all_to_all x2, blocking collectives, per_device(): grads = lax.all_to_all(grads, Y, 0, 0)  21.2 us
    all_to_all x1, blocking collectives, per_device(): quarters = lax.all_to_all(quarters, QUAD, 0, 0)  13.6 us
    all_gather x1, blocking collectives, per_device(): near = lax.all_gather(quarters[:, :nodes], 'z_lo', axis=0)  12.2 us
    ppermute x3, starting transfers between devices, swap(): return lax.ppermute(array, axis, [(0, 1), (1, 0)])  11.6 us
    all_to_all x1, blocking collectives, per_device(): grads = lax.all_to_all(grads, Z, 0, 0)  9.3 us
    ppermute x3, waiting for transfers between devices, swap(): return lax.ppermute(array, axis, [(0, 1), (1, 0)])  9.11 us
  transfers between devices with their start and end apart: 4, of which 2 were waited for; matrix products, arithmetic and copies ran while one was open for 0% of the time, Pallas kernels for 1%

profile of v15, /device:TPU:1, one launch (start us, length us, event | category | flops | bytes accessed | tf_op | source)
XLA Modules:
  0.0 175.2 jit_solution(4146283023743381297)
XLA Ops:
  1.3 0.1 pad.8.clone
  1.4 0.7 convert_bitcast_fusion
  2.0 0.1 maximum_maximum_fusion
  2.1 0.0 copy-start.2
  2.1 0.9 copy-done.2
  3.0 13.6 %all_to_all.40 = bf16[4,144,128]{2,1,0:T(8,128)(2,1)S(1)} all-to-all(bf16[4,144,128]{2,1,0:T(8,128)(2,1)S(1)} %shard_map.103), channel_id=1, replica_groups=mesh['z_lo'=4,'x'=4,'core'=2,'z_hi'=2,'y_pair'=4,'y_odd'=2] {'core','y_o..., dimensions={0} | all-to-all | bytes 294912 | tf_op jit(solution)/shard_map/all_to_all | solution.py:208
  16.6 0.0 copy-start.5
  16.6 2.0 %collective-permute-start = (bf16[11,256,256]{2,1,0:T(8,128)(2,1)}, bf16[11,256,256]{2,1,0:T(8,128)(2,1)}, u32[]{:S(2)}, u32[]{:S(2)}) collective-permute-start(bf16[11,256,256]{2,1,0:T(8,128)(2,1)} %bitcast.18), channel_id=1, source_target_pairs={{0,1},{1,0},{2,3},{3,2},{4,5},{5,4},{6,7},{7,6},{8,9},{9,8},{10,11... | collective-permute-start | bytes 4325384 | tf_op jit(solution)/shard_map/ppermute | solution.py:194
  18.6 0.0 copy-done.5
  18.7 12.2 %all-gather = bf16[16,128,128]{2,1,0:T(8,128)(2,1)S(1)} all-gather(bf16[4,128,128]{2,1,0:T(8,128)(2,1)S(1)} %slice.7), channel_id=2, replica_groups=mesh['z_lo'=4,'x'=4,'core'=2,'z_hi'=2,'y_pair'=4,'y_odd'=2] {'z_lo'}, dimensions={0}, use_global_device_ids=true | all-gather | bytes 655360 | tf_op jit(solution)/shard_map/all_gather | solution.py:214
  30.9 1.4 shard_map.104
  32.3 0.0 copy-start
  32.3 3.8 %all-to-all-start.1 = ((bf16[4,4,4,128,128]{4,3,2,1,0:T(8,128)(2,1)}), bf16[4,4,4,128,128]{4,3,2,1,0:T(8,128)(2,1)S(1)}, u32[]{:S(2)}, u32[]{:S(2)}) async-start(bf16[4,4,4,128,128]{4,3,2,1,0:T(8,128)(2,1)} %shard_map.104), calls=%async_computation.1 | async-start | bytes 4194304 | tf_op jit(solution)/shard_map/all_to_all | solution.py:223
  36.1 0.0 copy-done
  36.1 6.3 %collective-permute-start.1 = (bf16[11,256,256]{2,1,0:T(8,128)(2,1)S(1)}, bf16[11,256,256]{2,1,0:T(8,128)(2,1)}, u32[]{:S(2)}, u32[]{:S(2)}) collective-permute-start(bf16[11,256,256]{2,1,0:T(8,128)(2,1)S(1)} %bitcast.19), channel_id=1, source_target_pairs={{0,16},{16,0},{1,17},{17,1},{2,18},{18,2},{3,19},{19,3},{4,20},{20... | collective-permute-start | bytes 4325384 | tf_op jit(solution)/shard_map/ppermute | solution.py:194
  42.4 9.1 %collective-permute-done.refs_1_ = bf16[11,256,256]{2,1,0:T(8,128)(2,1)} collective-permute-done((bf16[11,256,256]{2,1,0:T(8,128)(2,1)}, bf16[11,256,256]{2,1,0:T(8,128)(2,1)}, u32[]{:S(2)}, u32[]{:S(2)}) %collective-permute-start) | collective-permute-done | bytes 1441824 | tf_op jit(solution)/shard_map/ppermute | solution.py:194
  51.5 3.2 %collective-permute-start.2 = (bf16[11,256,256]{2,1,0:T(8,128)(2,1)}, bf16[11,256,256]{2,1,0:T(8,128)(2,1)}, u32[]{:S(2)}, u32[]{:S(2)}) collective-permute-start(bf16[11,256,256]{2,1,0:T(8,128)(2,1)} %collective-permute-done.refs_1_), channel_id=1, source_target_pairs={{0,16},{16,0},{1,17},{17,1},{2,18},{18,2},{3,19},{19,3},{4,20},{20... | collective-permute-start | bytes 4325384 | tf_op jit(solution)/shard_map/ppermute | solution.py:194
  54.7 0.1 pad_add_fusion.place_ref
  54.8 0.7 slice_convert_fusion.meta_ref
  55.5 0.0 collective-permute-done.1.refs_2_
  55.5 2.5 %all-to-all-done.1.refs_4_ = bf16[4,4,4,128,128]{4,3,2,1,0:T(8,128)(2,1)S(1)} async-done(((bf16[4,4,4,128,128]{4,3,2,1,0:T(8,128)(2,1)}), bf16[4,4,4,128,128]{4,3,2,1,0:T(8,128)(2,1)S(1)}, u32[]{:S(2)}, u32[]{:S(2)}) %all-to-all-start.1) | async-done | bytes 2097184 | tf_op jit(solution)/shard_map/all_to_all | solution.py:223
  58.0 0.0 collective-permute-done.2.refs_3_
  58.0 4.4 %shard_map.105 = bf16[2,4,2,2,128,128]{5,4,3,2,1,0:T(8,128)(2,1)S(1)} custom-call(s32[2]{0:T(128)S(1)} %pad_add_fusion.place_ref, s32[4,3,11]{2,1,0:T(4,128)S(1)} %slice_convert_fusion.meta_ref, bf16[11,256,256]{2,1,0:T(8,128)(2,1)S(1)} %bitcast.20, bf16[11,256,256]{2,1,0:T(8,128)(2,1)} %collective-permute-done.refs_1_, ...), custom_call_target="tpu_custom_call" | custom-call | tf_op jit(solution)/shard_map/pallas_call | solution.py:225
  62.4 0.0 copy-start.1
  62.4 0.0 copy-start.3
  62.4 0.0 copy-start.4
  62.5 49.1 %all_to_all.41 = bf16[32,128,128]{2,1,0:T(8,128)(2,1)S(1)} all-to-all(bf16[32,128,128]{2,1,0:T(8,128)(2,1)S(1)} %bitcast.16), channel_id=1, replica_groups=mesh['z_lo'=4,'x'=4,'core'=2,'z_hi'=2,'y_pair'=4,'y_odd'=2] {'core','y_p..., dimensions={0} | all-to-all | bytes 2097152 | tf_op jit(solution)/shard_map/all_to_all | solution.py:235
  111.5 0.0 copy-done.1
  111.5 0.0 copy-done.3
  111.5 0.0 copy-done.4
  111.5 1.0 shard_map.106
  112.5 13.5 %all_to_all.42.parts_ref = bf16[8,72,512]{2,1,0:T(8,128)(2,1)S(1)} all-to-all(bf16[8,72,512]{2,1,0:T(8,128)(2,1)S(1)} %get-tuple-element.12), channel_id=1, replica_groups=mesh['z_lo'=4,'x'=4,'core'=2,'z_hi'=2,'y_pair'=4,'y_odd'=2] {'x','core'}, dimensions={0} | all-to-all | bytes 1179648 | tf_op jit(solution)/shard_map/all_to_all | solution.py:247
  126.1 0.1 shard_map.107
  126.1 11.5 %all_to_all.43.parts_ref = bf16[8,8,640]{2,1,0:T(8,128)(2,1)S(1)} all-to-all(bf16[8,8,640]{2,1,0:T(8,128)(2,1)S(1)} %shard_map.107), channel_id=1, replica_groups=mesh['z_lo'=4,'x'=4,'core'=2,'z_hi'=2,'y_pair'=4,'y_odd'=2] {'y_pair','y..., dimensions={0} | all-to-all | bytes 163840 | tf_op jit(solution)/shard_map/all_to_all | solution.py:249
  137.6 9.3 %all_to_all.44.parts_ref = bf16[8,8,640]{2,1,0:T(8,128)(2,1)S(1)} all-to-all(bf16[8,8,640]{2,1,0:T(8,128)(2,1)S(1)} %shard_map.108), channel_id=1, replica_groups=mesh['z_lo'=4,'x'=4,'core'=2,'z_hi'=2,'y_pair'=4,'y_odd'=2] {'z_lo','z_hi'}, dimensions={0} | all-to-all | bytes 163840 | tf_op jit(solution)/shard_map/all_to_all | solution.py:251
  147.0 9.8 %all_to_all.45.parts_ref = bf16[8,8,640]{2,1,0:T(8,128)(2,1)S(1)} all-to-all(bf16[8,8,640]{2,1,0:T(8,128)(2,1)S(1)} %shard_map.109), channel_id=1, replica_groups=mesh['z_lo'=4,'x'=4,'core'=2,'z_hi'=2,'y_pair'=4,'y_odd'=2] {'y_pair','y..., dimensions={0} | all-to-all | bytes 163840 | tf_op jit(solution)/shard_map/all_to_all | solution.py:253
  156.8 17.4 %all_to_all.46.parts_ref = bf16[8,72,512]{2,1,0:T(8,128)(2,1)S(1)} all-to-all(bf16[8,72,512]{2,1,0:T(8,128)(2,1)S(1)} %shard_map.110), channel_id=1, replica_groups=mesh['z_lo'=4,'x'=4,'core'=2,'z_hi'=2,'y_pair'=4,'y_odd'=2] {'x','core'}, dimensions={0} | all-to-all | bytes 1179648 | tf_op jit(solution)/shard_map/all_to_all | solution.py:255
  174.2 1.0 shard_map.111
  (6 shorter events, 0.1 us)
Async XLA Ops:
  2.1 0.9 copy-start.2
  16.6 2.0 %copy-start.5 = (bf16[4,144,128]{2,1,0:T(8,128)(2,1)}, bf16[4,144,128]{2,1,0:T(8,128)(2,1)S(1)}, u32[]{:S(2)}) copy-start(bf16[4,144,128]{2,1,0:T(8,128)(2,1)S(1)} %all_to_all.40) | copy-start | bytes 442372
  16.6 34.9 %collective-permute-start = (bf16[11,256,256]{2,1,0:T(8,128)(2,1)}, bf16[11,256,256]{2,1,0:T(8,128)(2,1)}, u32[]{:S(2)}, u32[]{:S(2)}) collective-permute-start(bf16[11,256,256]{2,1,0:T(8,128)(2,1)} %bitcast.18), channel_id=1, source_target_pairs={{0,1},{1,0},{2,3},{3,2},{4,5},{5,4},{6,7},{7,6},{8,9},{9,8},{10,11... | collective-permute-start | bytes 4325384 | tf_op jit(solution)/shard_map/ppermute | solution.py:194
  32.3 3.8 %copy-start = (bf16[1,1,11,256,256]{4,3,2,1,0:T(8,128)(2,1)S(1)}, bf16[1,1,11,256,256]{4,3,2,1,0:T(8,128)(2,1)}, u32[]{:S(2)}) copy-start(bf16[1,1,11,256,256]{4,3,2,1,0:T(8,128)(2,1)} %param.12) | copy-start | bytes 4325380
  32.3 25.7 %all-to-all-start.1 = ((bf16[4,4,4,128,128]{4,3,2,1,0:T(8,128)(2,1)}), bf16[4,4,4,128,128]{4,3,2,1,0:T(8,128)(2,1)S(1)}, u32[]{:S(2)}, u32[]{:S(2)}) async-start(bf16[4,4,4,128,128]{4,3,2,1,0:T(8,128)(2,1)} %shard_map.104), calls=%async_computation.1 | async-start | bytes 4194304 | tf_op jit(solution)/shard_map/all_to_all | solution.py:223
  36.1 19.4 %collective-permute-start.1 = (bf16[11,256,256]{2,1,0:T(8,128)(2,1)S(1)}, bf16[11,256,256]{2,1,0:T(8,128)(2,1)}, u32[]{:S(2)}, u32[]{:S(2)}) collective-permute-start(bf16[11,256,256]{2,1,0:T(8,128)(2,1)S(1)} %bitcast.19), channel_id=1, source_target_pairs={{0,16},{16,0},{1,17},{17,1},{2,18},{18,2},{3,19},{19,3},{4,20},{20... | collective-permute-start | bytes 4325384 | tf_op jit(solution)/shard_map/ppermute | solution.py:194
  51.5 6.5 %collective-permute-start.2 = (bf16[11,256,256]{2,1,0:T(8,128)(2,1)}, bf16[11,256,256]{2,1,0:T(8,128)(2,1)}, u32[]{:S(2)}, u32[]{:S(2)}) collective-permute-start(bf16[11,256,256]{2,1,0:T(8,128)(2,1)} %collective-permute-done.refs_1_), channel_id=1, source_target_pairs={{0,16},{16,0},{1,17},{17,1},{2,18},{18,2},{3,19},{19,3},{4,20},{20... | collective-permute-start | bytes 4325384 | tf_op jit(solution)/shard_map/ppermute | solution.py:194
  62.4 49.1 %copy-start.1 = (bf16[512,512]{1,0:T(8,128)(2,1)S(1)}, bf16[512,512]{1,0:T(8,128)(2,1)}, u32[]{:S(2)}) copy-start(bf16[512,512]{1,0:T(8,128)(2,1)} %weight_ref.1) | copy-start | bytes 1572868
  62.4 49.1 %copy-start.3 = (bf16[128,512]{1,0:T(8,128)(2,1)S(1)}, bf16[128,512]{1,0:T(8,128)(2,1)}, u32[]{:S(2)}) copy-start(bf16[128,512]{1,0:T(8,128)(2,1)} %cot_ref.1) | copy-start | bytes 393220
  62.4 49.1 %copy-start.4 = (f32[512]{0:T(512)S(1)}, f32[512]{0:T(512)}, u32[]{:S(2)}) copy-start(f32[512]{0:T(512)} %param.10) | copy-start | bytes 6148

commit v16 on v15

--- a/solution.py
+++ b/solution.py
@@ -233,7 +233,7 @@
         compiler_params=PARAMS,
     )(place, meta, tiles, tiles_y, tiles_core, tiles_both, blocks)
     shares = lax.all_to_all(term.reshape(-1, nodes, LANES), HOME, 0, 0)
-    n_near, n_y, n_deep = lax.axis_size(NEAR), lax.axis_size(Y), lax.axis_size(Z)
+    n_near, n_deep, n_y = lax.axis_size(NEAR), lax.axis_size(Z), lax.axis_size(Y)
     depth = width // n_near
     tall, wide = depth + PAIR, width + LANES
     activations, grads = call(
@@ -245,12 +245,12 @@
         cotangent,
     )
     grads = lax.all_to_all(grads, NEAR, 0, 0)
-    grads = call(scatter_kernel, ((n_y, depth // n_y, wide), BF16), grads)
+    grads = call(scatter_kernel, ((n_deep, depth // n_deep, wide), BF16), grads)
+    grads = lax.all_to_all(grads, Z, 0, 0)
+    grads = call(sum_kernel, ((n_y, depth // n_deep, wide), BF16), grads)
     grads = lax.all_to_all(grads, Y, 0, 0)
-    grads = call(sum_kernel, ((n_deep, depth // n_y, wide), BF16), grads)
+    grads = call(sum_kernel, ((n_deep, depth // n_deep, wide), BF16), grads)
     grads = lax.all_to_all(grads, Z, 0, 0)
-    grads = call(sum_kernel, ((n_y, depth // n_y, wide), BF16), grads)
-    grads = lax.all_to_all(grads, Y, 0, 0)
     grads = call(copy_kernel, ((n_near, tall, width), BF16), grads)
     grads = lax.all_to_all(grads, NEAR, 0, 0)
     weight_grad, bias_grad = call(

time: 176 us -> 175 us (level)
    all_to_all x2 -> x1, blocking collectives: 21.2 us -> 11.4 us  [per_device(): grads = lax.all_to_all(grads, Y, 0, 0)]
    all_to_all x1 -> x2, blocking collectives: 9.3 us -> 18.2 us  [per_device(): grads = lax.all_to_all(grads, Z, 0, 0)]
where the time goes in v16:
time: 175 us; the launch traced here: 174 us
  blocking collectives  136 us (78%)
  starting transfers between devices  15.3 us (9%)
  waiting for transfers between devices  11.6 us (7%)
  Pallas kernels  7.79 us (4%)
    all_to_all x1, blocking collectives, per_device(): shares = lax.all_to_all(term.reshape(-1, nodes, LANES), HOME, 0, 0)  49.1 us
    all_to_all x2, blocking collectives, per_device(): grads = lax.all_to_all(grads, NEAR, 0, 0)  31.2 us
    all_to_all x2, blocking collectives, per_device(): grads = lax.all_to_all(grads, Z, 0, 0)  18.2 us
    all_to_all x1, blocking collectives, per_device(): quarters = lax.all_to_all(quarters, QUAD, 0, 0)  13.6 us
    all_gather x1, blocking collectives, per_device(): near = lax.all_gather(quarters[:, :nodes], 'z_lo', axis=0)  12.2 us
    ppermute x3, starting transfers between devices, swap(): return lax.ppermute(array, axis, [(0, 1), (1, 0)])  11.6 us
    all_to_all x1, blocking collectives, per_device(): grads = lax.all_to_all(grads, Y, 0, 0)  11.4 us
    ppermute x3, waiting for transfers between devices, swap(): return lax.ppermute(array, axis, [(0, 1), (1, 0)])  9.11 us
  transfers between devices with their start and end apart: 4, of which 2 were waited for; matrix products, arithmetic and copies ran while one was open for 0% of the time, Pallas kernels for 1%

profile of v16, /device:TPU:1, one launch (start us, length us, event | category | flops | bytes accessed | tf_op | source)
XLA Modules:
  0.0 174.3 jit_solution(13621258199472121587)
XLA Ops:
  1.3 0.1 pad.8.clone
  1.4 0.7 convert_bitcast_fusion
  2.0 0.1 maximum_maximum_fusion
  2.1 0.0 copy-start.2
  2.1 0.9 copy-done.2
  3.0 13.6 %all_to_all.40 = bf16[4,144,128]{2,1,0:T(8,128)(2,1)S(1)} all-to-all(bf16[4,144,128]{2,1,0:T(8,128)(2,1)S(1)} %shard_map.103), channel_id=1, replica_groups=mesh['z_lo'=4,'x'=4,'core'=2,'z_hi'=2,'y_pair'=4,'y_odd'=2] {'core','y_o..., dimensions={0} | all-to-all | bytes 294912 | tf_op jit(solution)/shard_map/all_to_all | solution.py:208
  16.6 0.0 copy-start.5
  16.6 2.0 %collective-permute-start = (bf16[11,256,256]{2,1,0:T(8,128)(2,1)}, bf16[11,256,256]{2,1,0:T(8,128)(2,1)}, u32[]{:S(2)}, u32[]{:S(2)}) collective-permute-start(bf16[11,256,256]{2,1,0:T(8,128)(2,1)} %bitcast.18), channel_id=1, source_target_pairs={{0,1},{1,0},{2,3},{3,2},{4,5},{5,4},{6,7},{7,6},{8,9},{9,8},{10,11... | collective-permute-start | bytes 4325384 | tf_op jit(solution)/shard_map/ppermute | solution.py:194
  18.6 0.0 copy-done.5
  18.7 12.2 %all-gather = bf16[16,128,128]{2,1,0:T(8,128)(2,1)S(1)} all-gather(bf16[4,128,128]{2,1,0:T(8,128)(2,1)S(1)} %slice.7), channel_id=2, replica_groups=mesh['z_lo'=4,'x'=4,'core'=2,'z_hi'=2,'y_pair'=4,'y_odd'=2] {'z_lo'}, dimensions={0}, use_global_device_ids=true | all-gather | bytes 655360 | tf_op jit(solution)/shard_map/all_gather | solution.py:214
  30.9 1.4 shard_map.104
  32.3 0.0 copy-start
  32.3 3.8 %all-to-all-start.1 = ((bf16[4,4,4,128,128]{4,3,2,1,0:T(8,128)(2,1)}), bf16[4,4,4,128,128]{4,3,2,1,0:T(8,128)(2,1)S(1)}, u32[]{:S(2)}, u32[]{:S(2)}) async-start(bf16[4,4,4,128,128]{4,3,2,1,0:T(8,128)(2,1)} %shard_map.104), calls=%async_computation.1 | async-start | bytes 4194304 | tf_op jit(solution)/shard_map/all_to_all | solution.py:223
  36.1 0.0 copy-done
  36.1 6.3 %collective-permute-start.1 = (bf16[11,256,256]{2,1,0:T(8,128)(2,1)S(1)}, bf16[11,256,256]{2,1,0:T(8,128)(2,1)}, u32[]{:S(2)}, u32[]{:S(2)}) collective-permute-start(bf16[11,256,256]{2,1,0:T(8,128)(2,1)S(1)} %bitcast.19), channel_id=1, source_target_pairs={{0,16},{16,0},{1,17},{17,1},{2,18},{18,2},{3,19},{19,3},{4,20},{20... | collective-permute-start | bytes 4325384 | tf_op jit(solution)/shard_map/ppermute | solution.py:194
  42.4 9.1 %collective-permute-done.refs_1_ = bf16[11,256,256]{2,1,0:T(8,128)(2,1)} collective-permute-done((bf16[11,256,256]{2,1,0:T(8,128)(2,1)}, bf16[11,256,256]{2,1,0:T(8,128)(2,1)}, u32[]{:S(2)}, u32[]{:S(2)}) %collective-permute-start) | collective-permute-done | bytes 1441824 | tf_op jit(solution)/shard_map/ppermute | solution.py:194
  51.5 3.2 %collective-permute-start.2 = (bf16[11,256,256]{2,1,0:T(8,128)(2,1)}, bf16[11,256,256]{2,1,0:T(8,128)(2,1)}, u32[]{:S(2)}, u32[]{:S(2)}) collective-permute-start(bf16[11,256,256]{2,1,0:T(8,128)(2,1)} %collective-permute-done.refs_1_), channel_id=1, source_target_pairs={{0,16},{16,0},{1,17},{17,1},{2,18},{18,2},{3,19},{19,3},{4,20},{20... | collective-permute-start | bytes 4325384 | tf_op jit(solution)/shard_map/ppermute | solution.py:194
  54.7 0.1 pad_add_fusion.place_ref
  54.8 0.7 slice_convert_fusion.meta_ref
  55.5 0.0 collective-permute-done.1.refs_2_
  55.5 2.5 %all-to-all-done.1.refs_4_ = bf16[4,4,4,128,128]{4,3,2,1,0:T(8,128)(2,1)S(1)} async-done(((bf16[4,4,4,128,128]{4,3,2,1,0:T(8,128)(2,1)}), bf16[4,4,4,128,128]{4,3,2,1,0:T(8,128)(2,1)S(1)}, u32[]{:S(2)}, u32[]{:S(2)}) %all-to-all-start.1) | async-done | bytes 2097184 | tf_op jit(solution)/shard_map/all_to_all | solution.py:223
  58.0 0.0 collective-permute-done.2.refs_3_
  58.0 4.2 %shard_map.105 = bf16[2,4,2,2,128,128]{5,4,3,2,1,0:T(8,128)(2,1)S(1)} custom-call(s32[2]{0:T(128)S(1)} %pad_add_fusion.place_ref, s32[4,3,11]{2,1,0:T(4,128)S(1)} %slice_convert_fusion.meta_ref, bf16[11,256,256]{2,1,0:T(8,128)(2,1)S(1)} %bitcast.20, bf16[11,256,256]{2,1,0:T(8,128)(2,1)} %collective-permute-done.refs_1_, ...), custom_call_target="tpu_custom_call" | custom-call | tf_op jit(solution)/shard_map/pallas_call | solution.py:225
  62.2 0.0 copy-start.1
  62.2 0.0 copy-start.3
  62.2 0.0 copy-start.4
  62.2 49.1 %all_to_all.41 = bf16[32,128,128]{2,1,0:T(8,128)(2,1)S(1)} all-to-all(bf16[32,128,128]{2,1,0:T(8,128)(2,1)S(1)} %bitcast.16), channel_id=1, replica_groups=mesh['z_lo'=4,'x'=4,'core'=2,'z_hi'=2,'y_pair'=4,'y_odd'=2] {'core','y_p..., dimensions={0} | all-to-all | bytes 2097152 | tf_op jit(solution)/shard_map/all_to_all | solution.py:235
  111.3 0.0 copy-done.1
  111.3 0.0 copy-done.3
  111.3 0.0 copy-done.4
  111.3 1.0 shard_map.106
  112.3 14.1 %all_to_all.42.parts_ref = bf16[8,72,512]{2,1,0:T(8,128)(2,1)S(1)} all-to-all(bf16[8,72,512]{2,1,0:T(8,128)(2,1)S(1)} %get-tuple-element.12), channel_id=1, replica_groups=mesh['z_lo'=4,'x'=4,'core'=2,'z_hi'=2,'y_pair'=4,'y_odd'=2] {'x','core'}, dimensions={0} | all-to-all | bytes 1179648 | tf_op jit(solution)/shard_map/all_to_all | solution.py:247
  126.4 0.1 shard_map.107
  126.5 9.0 %all_to_all.43.parts_ref = bf16[8,8,640]{2,1,0:T(8,128)(2,1)S(1)} all-to-all(bf16[8,8,640]{2,1,0:T(8,128)(2,1)S(1)} %shard_map.107), channel_id=1, replica_groups=mesh['z_lo'=4,'x'=4,'core'=2,'z_hi'=2,'y_pair'=4,'y_odd'=2] {'z_lo','z_hi'}, dimensions={0} | all-to-all | bytes 163840 | tf_op jit(solution)/shard_map/all_to_all | solution.py:249
  135.5 11.4 %all_to_all.44.parts_ref = bf16[8,8,640]{2,1,0:T(8,128)(2,1)S(1)} all-to-all(bf16[8,8,640]{2,1,0:T(8,128)(2,1)S(1)} %shard_map.108), channel_id=1, replica_groups=mesh['z_lo'=4,'x'=4,'core'=2,'z_hi'=2,'y_pair'=4,'y_odd'=2] {'y_pair','y..., dimensions={0} | all-to-all | bytes 163840 | tf_op jit(solution)/shard_map/all_to_all | solution.py:251
  146.9 9.2 %all_to_all.45.parts_ref = bf16[8,8,640]{2,1,0:T(8,128)(2,1)S(1)} all-to-all(bf16[8,8,640]{2,1,0:T(8,128)(2,1)S(1)} %shard_map.109), channel_id=1, replica_groups=mesh['z_lo'=4,'x'=4,'core'=2,'z_hi'=2,'y_pair'=4,'y_odd'=2] {'z_lo','z_hi'}, dimensions={0} | all-to-all | bytes 163840 | tf_op jit(solution)/shard_map/all_to_all | solution.py:253
  156.1 17.1 %all_to_all.46.parts_ref = bf16[8,72,512]{2,1,0:T(8,128)(2,1)S(1)} all-to-all(bf16[8,72,512]{2,1,0:T(8,128)(2,1)S(1)} %shard_map.110), channel_id=1, replica_groups=mesh['z_lo'=4,'x'=4,'core'=2,'z_hi'=2,'y_pair'=4,'y_odd'=2] {'x','core'}, dimensions={0} | all-to-all | bytes 1179648 | tf_op jit(solution)/shard_map/all_to_all | solution.py:255
  173.2 1.0 shard_map.111
  (6 shorter events, 0.1 us)
Async XLA Ops:
  2.1 0.9 copy-start.2
  16.6 2.0 %copy-start.5 = (bf16[4,144,128]{2,1,0:T(8,128)(2,1)}, bf16[4,144,128]{2,1,0:T(8,128)(2,1)S(1)}, u32[]{:S(2)}) copy-start(bf16[4,144,128]{2,1,0:T(8,128)(2,1)S(1)} %all_to_all.40) | copy-start | bytes 442372
  16.6 34.9 %collective-permute-start = (bf16[11,256,256]{2,1,0:T(8,128)(2,1)}, bf16[11,256,256]{2,1,0:T(8,128)(2,1)}, u32[]{:S(2)}, u32[]{:S(2)}) collective-permute-start(bf16[11,256,256]{2,1,0:T(8,128)(2,1)} %bitcast.18), channel_id=1, source_target_pairs={{0,1},{1,0},{2,3},{3,2},{4,5},{5,4},{6,7},{7,6},{8,9},{9,8},{10,11... | collective-permute-start | bytes 4325384 | tf_op jit(solution)/shard_map/ppermute | solution.py:194
  32.3 3.8 %copy-start = (bf16[1,1,11,256,256]{4,3,2,1,0:T(8,128)(2,1)S(1)}, bf16[1,1,11,256,256]{4,3,2,1,0:T(8,128)(2,1)}, u32[]{:S(2)}) copy-start(bf16[1,1,11,256,256]{4,3,2,1,0:T(8,128)(2,1)} %param.12) | copy-start | bytes 4325380
  32.3 25.7 %all-to-all-start.1 = ((bf16[4,4,4,128,128]{4,3,2,1,0:T(8,128)(2,1)}), bf16[4,4,4,128,128]{4,3,2,1,0:T(8,128)(2,1)S(1)}, u32[]{:S(2)}, u32[]{:S(2)}) async-start(bf16[4,4,4,128,128]{4,3,2,1,0:T(8,128)(2,1)} %shard_map.104), calls=%async_computation.1 | async-start | bytes 4194304 | tf_op jit(solution)/shard_map/all_to_all | solution.py:223
  36.1 19.4 %collective-permute-start.1 = (bf16[11,256,256]{2,1,0:T(8,128)(2,1)S(1)}, bf16[11,256,256]{2,1,0:T(8,128)(2,1)}, u32[]{:S(2)}, u32[]{:S(2)}) collective-permute-start(bf16[11,256,256]{2,1,0:T(8,128)(2,1)S(1)} %bitcast.19), channel_id=1, source_target_pairs={{0,16},{16,0},{1,17},{17,1},{2,18},{18,2},{3,19},{19,3},{4,20},{20... | collective-permute-start | bytes 4325384 | tf_op jit(solution)/shard_map/ppermute | solution.py:194
  51.5 6.5 %collective-permute-start.2 = (bf16[11,256,256]{2,1,0:T(8,128)(2,1)}, bf16[11,256,256]{2,1,0:T(8,128)(2,1)}, u32[]{:S(2)}, u32[]{:S(2)}) collective-permute-start(bf16[11,256,256]{2,1,0:T(8,128)(2,1)} %collective-permute-done.refs_1_), channel_id=1, source_target_pairs={{0,16},{16,0},{1,17},{17,1},{2,18},{18,2},{3,19},{19,3},{4,20},{20... | collective-permute-start | bytes 4325384 | tf_op jit(solution)/shard_map/ppermute | solution.py:194
  62.2 49.1 %copy-start.1 = (bf16[512,512]{1,0:T(8,128)(2,1)S(1)}, bf16[512,512]{1,0:T(8,128)(2,1)}, u32[]{:S(2)}) copy-start(bf16[512,512]{1,0:T(8,128)(2,1)} %weight_ref.1) | copy-start | bytes 1572868
  62.2 49.1 %copy-start.3 = (bf16[128,512]{1,0:T(8,128)(2,1)S(1)}, bf16[128,512]{1,0:T(8,128)(2,1)}, u32[]{:S(2)}) copy-start(bf16[128,512]{1,0:T(8,128)(2,1)} %cot_ref.1) | copy-start | bytes 393220
  62.2 49.1 %copy-start.4 = (f32[512]{0:T(512)S(1)}, f32[512]{0:T(512)}, u32[]{:S(2)}) copy-start(f32[512]{0:T(512)} %param.10) | copy-start | bytes 6148
